TPU v7x, 32 devices: a whole 2x2x4 slice. The times are simulated.
32 devices in a mesh: row: 4 (over y, x), col: 8 (over z, core).
Axes of the slice: x: 2, y: 2, z: 4, core: 2. Of those that a mesh axis runs over, the one named last changes fastest.
Arguments:
- density: bfloat16 [8192, 8192], P('col', 'row'), may hold values from -1 to 1
- pattern_p: int32 [64, 64], replicated, may hold values 0 or 1
- pattern_square: int32 [64, 64], replicated, may hold values 0 or 1
- pattern_cube: int32 [64, 64], replicated, may hold values 0 or 1
Outputs:
- purified: float32 [8192, 8192], P('col', 'row')
All inputs are finite; a program needn't handle non-finite values.
Results may differ from a plain program's by a relative error of at most 0.009.
Values may be sent and summed in bfloat16 or wider, within the bound.
No kernel may reach another device: no remote copies, remote signals or barrier semaphores. Data moves between devices by JAX's collectives and lax.ppermute only.
A program may use at most 128 MiB of HBM per device.

v0:
```python
import jax
import jax.numpy as jnp
from jax import lax
from jax.sharding import PartitionSpec as P

TILE = 128


def tile_mask(pattern, row_start, col_start, nrows, ncols):
    tile_rows = nrows // TILE + 2
    tile_cols = ncols // TILE + 2
    padded = jnp.pad(pattern, ((0, tile_rows), (0, tile_cols)))
    block = lax.dynamic_slice(
        padded, (row_start // TILE, col_start // TILE), (tile_rows, tile_cols)
    )
    spread = jnp.repeat(jnp.repeat(block, TILE, 0), TILE, 1)
    return lax.dynamic_slice(spread, (row_start % TILE, col_start % TILE), (nrows, ncols))


def local(density, pattern_p, pattern_square, pattern_cube):
    nrows, ncols = density.shape
    row_start = lax.axis_index("col") * nrows
    col_start = lax.axis_index("row") * ncols
    masked = density * tile_mask(pattern_p, row_start, col_start, nrows, ncols).astype(jnp.bfloat16)
    column_panel = lax.all_gather(masked, "col", axis=0, tiled=True)

    def right_fold(piece):
        return jnp.dot(piece, column_panel, preferred_element_type=jnp.float32)

    square = right_fold(lax.all_gather(masked, "row", axis=1, tiled=True))
    cube = right_fold(lax.all_gather(square.astype(jnp.bfloat16), "row", axis=1, tiled=True))
    keep_square = tile_mask(pattern_square, row_start, col_start, nrows, ncols).astype(jnp.float32)
    keep_cube = tile_mask(pattern_cube, row_start, col_start, nrows, ncols).astype(jnp.float32)
    return 3.0 * keep_square * square - 2.0 * keep_cube * cube


def solution(mesh):
    placed = (P("col", "row"), P(), P(), P())
    return jax.shard_map(
        local, mesh=mesh, in_specs=placed, out_specs=P("col", "row"), check_vma=False
    )
```

profile of v0, /device:TPU:0, one launch (start us, length us, event | category | flops | bytes accessed | tf_op | source)
XLA Modules:
  0.0 723.8 jit_solution(7274417316075455702)
XLA Ops:
  6.5 0.0 all-gather.4.cloned.1.call-start
  6.5 0.8 pad_dynamic-slice_fusion
  7.3 0.1 copy.13
  7.4 0.1 broadcast_bitcast_fusion.1
  7.6 6.4 copy.14
  14.0 0.9 broadcast_in_dim.21
  14.9 4.8 fusion
  19.7 0.0 all-gather.4.cloned.1.call-update
  19.7 0.0 all-gather.6.cloned.1.call-start
  19.8 0.7 all-gather.6.cloned.1.call-update
  20.5 0.0 copy-start
  20.5 0.0 all-gather.8.cloned.1.call-start
  20.5 159.5 %all-gather.4.cloned.1.call-done = bf16[1024,8192]{0,1:T(8,128)(2,1)} async-done(((bf16[1024,2048]{0,1:T(8,128)(2,1)}), bf16[1024,8192]{0,1:T(8,128)(2,1)}) %all-gather.4.cloned.1.call-update) | async-done | bytes 16777232 | tf_op jit(solution)/shard_map/all_gather | solution.py:30
  180.0 290.3 %all-gather.6.cloned.1.call-done = bf16[8192,2048]{0,1:T(8,128)(2,1)} async-done(((bf16[1024,2048]{0,1:T(8,128)(2,1)}), bf16[8192,2048]{0,1:T(8,128)(2,1)}) %all-gather.6.cloned.1.call-update) | async-done | bytes 33554448 | tf_op jit(solution)/shard_map/all_gather | solution.py:25
  470.2 45.4 %fusion.1 = (bf16[1024,2048]{1,0:T(8,128)(2,1)}, f32[1024,2048]{1,0:T(8,128)}) fusion(bf16[1024,8192]{0,1:T(8,128)(2,1)} %all-gather.4.cloned.1.call-done, bf16[8192,2048]{0,1:T(8,128)(2,1)} %all-gather.6.cloned.1.call-done), kind=kOutput, calls=%fused_computation.9 | convolution fusion | flops 34361835520 | bytes 62914560 | tf_op jit(solution)/shard_map/dot_general | solution.py:28
  515.6 0.0 all-gather.8.cloned.1.call-update
  515.6 0.0 copy-done
  515.6 0.1 pad_dynamic-slice_fusion.2
  515.7 0.1 copy.11
  515.8 0.1 copy.15
  515.9 0.1 broadcast_bitcast_fusion
  516.1 0.1 broadcast_bitcast_fusion.2
  516.3 0.9 broadcast_in_dim.19
  517.2 5.2 dynamic_slice.19
  522.4 10.0 %copy.17 = s32[1024,2048]{1,0:T(8,128)} copy(s32[1024,2048]{0,1:T(8,128)} %dynamic_slice.19) | data formatting | bytes 16777216
  532.4 0.9 broadcast_in_dim.23
  533.3 4.5 dynamic_slice.23
  537.8 9.1 %copy.18 = s32[1024,2048]{1,0:T(8,128)} copy(s32[1024,2048]{0,1:T(8,128)} %dynamic_slice.23) | data formatting | bytes 16777216
  546.9 124.5 %all-gather.8.cloned.1.call-done = bf16[1024,8192]{1,0:T(8,128)(2,1)} async-done(((bf16[1024,2048]{1,0:T(8,128)(2,1)}), bf16[1024,8192]{1,0:T(8,128)(2,1)}) %all-gather.8.cloned.1.call-update) | async-done | bytes 16777232 | tf_op jit(solution)/shard_map/all_gather | solution.py:31
  671.4 45.9 %multiply_subtract_fusion = f32[1024,2048]{1,0:T(8,128)} fusion(s32[1024,2048]{1,0:T(8,128)} %copy.18, f32[1024,2048]{1,0:T(8,128)} %get-tuple-element.6, s32[1024,2048]{1,0:T(8,128)} %copy.17, bf16[1024,8192]{1,0:T(8,128)(2,1)} %all-gather.8.cloned.1.call-done, bf16[8192,2048]{0,1:T(8,128)(2,1)} %all-gather.6.cloned.1.call-done), kind=kOutput, calls=%fused_computation | convolution fusion | flops 34374418432 | bytes 83886080 | tf_op jit(solution)/shard_map/dot_general | solution.py:28
  (6 shorter events, 0.2 us)
Async XLA Ops:
  6.5 173.4 %all-gather.4.cloned.1.call-start = ((), (), s32[]{:S(2)}) async-start(), calls=%async_computation | async-start | bytes 20971520 | tf_op jit(solution)/shard_map/all_gather | solution.py:30
  19.7 450.5 %all-gather.6.cloned.1.call-start = ((), (), s32[]{:S(2)}) async-start(), calls=%async_computation.1 | async-start | bytes 37748736 | tf_op jit(solution)/shard_map/all_gather | solution.py:25
  20.5 495.2 %copy-start = (s32[64,64]{1,0:T(8,128)S(1)}, s32[64,64]{1,0:T(8,128)}, u32[]{:S(2)}) copy-start(s32[64,64]{1,0:T(8,128)} %param.6) | copy-start | bytes 49156
  20.5 650.9 %all-gather.8.cloned.1.call-start = ((), (), s32[]{:S(2)}) async-start(), calls=%async_computation.2 | async-start | bytes 20971520 | tf_op jit(solution)/shard_map/all_gather | solution.py:31
Sparse Core Ops, SparseCore 0:
  19.8 160.0 all-gather.3
  181.6 288.6 all-gather.5
  515.8 155.6 all-gather.7
where the time goes:
time: 724 us
  waiting for transfers between devices  575 us (79%)
  matrix products  91.3 us (13%)
  local copies, waits for them, and re-layouts  39.6 us (5%)
  between operations  13.2 us (2%)
    all_gather x1, waiting for transfers between devices, local(): column_panel = lax.all_gather(masked, 'col', axis=0, tiled=True)  290 us
    all_gather x1, waiting for transfers between devices, local(): square = right_fold(lax.all_gather(masked, 'row', axis=1, tiled=True))  159 us
    all_gather x1, waiting for transfers between devices, local(): lax.all_gather(square.astype(jnp.bfloat16), 'row', axis=1, tiled=True)  124 us
    dot_general x2, matrix products, right_fold(): return jnp.dot(piece, column_panel, preferred_element_type=jnp.float32)  91.3 us
    unnamed x14, local copies, waits for them, and re-layouts  26 us
  transfers between devices with their start and end apart: 3, of which 3 were waited for; matrix products, arithmetic and copies ran while one was open for 4% of the time, Pallas kernels for 0%

commit v1 on v0

--- a/solution.py
+++ b/solution.py
@@ -1,9 +1,22 @@
+import functools
+import math
+
 import jax
 import jax.numpy as jnp
+import numpy as np
 from jax import lax
+from jax.experimental import pallas as pl
+from jax.experimental.pallas import tpu as pltpu
 from jax.sharding import PartitionSpec as P
 
 TILE = 128
+ROW_GROUP = 4
+WIDTHS = (4, 4, 4, 4)
+DEPTH = 1024
+VMEM_BYTES = 60 * 2**20
+SMEM = pl.BlockSpec(memory_space=pltpu.SMEM)
+VMEM = pl.BlockSpec(memory_space=pltpu.VMEM)
+ANY = pl.BlockSpec(memory_space=pl.ANY)
 
 
 def tile_mask(pattern, row_start, col_start, nrows, ncols):
@@ -17,7 +30,7 @@
     return lax.dynamic_slice(spread, (row_start % TILE, col_start % TILE), (nrows, ncols))
 
 
-def local(density, pattern_p, pattern_square, pattern_cube):
+def dense_step(density, pattern_p, pattern_square, pattern_cube):
     nrows, ncols = density.shape
     row_start = lax.axis_index("col") * nrows
     col_start = lax.axis_index("row") * ncols
@@ -34,6 +47,440 @@
     return 3.0 * keep_square * square - 2.0 * keep_cube * cube
 
 
+def chunk_bounds(tile_rows, widths):
+    bounds, cols = [], 0
+    for width in widths:
+        cols += width
+        tiles = tile_rows * cols
+        sigmas = 3.6 if cols == sum(widths) else 4.2
+        bounds.append(min(tiles, 2 * math.ceil((tiles + sigmas * math.sqrt(tiles)) / 4)))
+    return [min(b, bounds[-1]) for b in bounds]
+
+
+def slot_table(pattern, tile_rows, tile_cols):
+    n = pattern.shape[0]
+    at = np.arange(n)
+    same_rows = at[:, None] // tile_rows == at[None, :] // tile_rows
+    above = (same_rows & (at[None, :] < at[:, None])).astype(np.float32)
+    same_cols = at[:, None] // tile_cols == at[None, :] // tile_cols
+    left = (same_cols & (at[:, None] < at[None, :])).astype(np.float32)
+    kept = pattern.astype(jnp.bfloat16)
+    dot = functools.partial(jnp.dot, preferred_element_type=jnp.float32)
+    in_column = dot(jnp.asarray(above, jnp.bfloat16), kept)
+    column = dot(jnp.asarray(same_rows, jnp.bfloat16), kept).astype(jnp.bfloat16)
+    before = dot(column, jnp.asarray(left, jnp.bfloat16))
+    return jnp.where(pattern != 0, (in_column + before).astype(jnp.int32), -1)
+
+
+def tile_at(ref, i, j):
+    return ref.at[pl.ds(pl.multiple_of(i * TILE, TILE), TILE), pl.ds(pl.multiple_of(j * TILE, TILE), TILE)]
+
+
+def send_kept(table_ref, place_ref, x_ref, outs, sems, spans, shape):
+    tile_rows, tile_cols = shape
+    c, r = place_ref[0], place_ref[1]
+
+    def send(i, j, slot):
+        for q, (lo, hi) in enumerate(spans):
+            @pl.when((slot >= lo) & (slot < hi))
+            def _():
+                pltpu.make_async_copy(tile_at(x_ref, i, j), outs[q].at[slot - lo], sems.at[q]).start()
+
+    def step(n, used):
+        j, i = n // tile_rows, n % tile_rows
+        slot = table_ref[c * tile_rows + i, r * tile_cols + j]
+        send(i, j, slot)
+        return used + (slot >= 0).astype(jnp.int32)
+
+    used = lax.fori_loop(0, tile_rows * tile_cols, step, jnp.int32(0))
+    top = max(hi for _, hi in spans)
+
+    def fill(slot, z):
+        send(0, 0, slot)
+        return z
+
+    lax.fori_loop(used, jnp.int32(top), fill, 0)
+    for q, out in enumerate(outs):
+        pltpu.make_async_copy(out, out, sems.at[q]).wait()
+
+
+def pack(table, place, density, spans):
+    shape = density.shape[0] // TILE, density.shape[1] // TILE
+
+    def kernel(table_ref, place_ref, x_ref, *refs):
+        send_kept(table_ref, place_ref, x_ref, refs[:-1], refs[-1], spans, shape)
+
+    return pl.pallas_call(
+        kernel,
+        out_shape=[jax.ShapeDtypeStruct((hi - lo, TILE, TILE), density.dtype) for lo, hi in spans],
+        in_specs=[SMEM, SMEM, VMEM],
+        out_specs=[ANY] * len(spans),
+        scratch_shapes=[pltpu.SemaphoreType.DMA((len(spans),))],
+        name="pack",
+    )(table, place, density)
+
+
+def stage(halves, lo, hi, after):
+    cut = halves[0].shape[0]
+    parts = []
+    if lo < cut:
+        parts.append((0, lo, min(hi, cut)))
+    if hi > cut:
+        parts.append((1, max(lo, cut) - cut, hi - cut))
+
+    def kernel(h0, h1, after_ref, out, sem):
+        at, copies = 0, []
+        for which, first, end in parts:
+            src = (h0, h1)[which].at[pl.ds(first, end - first)]
+            copies.append(pltpu.make_async_copy(src, out.at[pl.ds(at, end - first)], sem.at[which]))
+            at += end - first
+        for copy in copies:
+            copy.start()
+        for copy in copies:
+            copy.wait()
+
+    return pl.pallas_call(
+        kernel,
+        out_shape=jax.ShapeDtypeStruct((hi - lo, TILE, TILE), halves[0].dtype),
+        in_specs=[ANY, ANY, ANY],
+        out_specs=VMEM,
+        scratch_shapes=[pltpu.SemaphoreType.DMA((2,))],
+        name="stage",
+    )(*halves, after)
+
+
+def row_unpack(table, place, density, pieces, widths):
+    nrows, ncols = density.shape
+    tile_rows, tile_cols = nrows // TILE, ncols // TILE
+    n_tiles = table.shape[0]
+    halves = [x.shape[0] for x in pieces[0]]
+    flat = [x for piece in pieces for x in piece]
+
+    def kernel(table_ref, place_ref, x_ref, *refs):
+        ins, (out, held, sems) = refs[:-3], refs[-3:]
+        i = pl.program_id(0)
+        c, r = place_ref[0], place_ref[1]
+
+        @pl.when(i == 0)
+        def _():
+            copies = []
+            for n, ref in enumerate(ins):
+                k, which = divmod(n, 2)
+                target = held.at[k, pl.ds(which * halves[0], halves[which])]
+                copies.append(pltpu.make_async_copy(ref, target, sems.at[n]))
+            for copy in copies:
+                copy.start()
+            for copy in copies:
+                copy.wait()
+
+        d = first = 0
+        for width in widths:
+            for k in range(ROW_GROUP):
+                for t in range(width):
+                    j = first + t
+                    slot = table_ref[c * tile_rows + i, (r ^ k) * tile_cols + j]
+                    if k == 0:
+                        tile = x_ref[:, j * TILE : (j + 1) * TILE]
+                    else:
+                        tile = held[k - 1, jnp.maximum(slot, 0)]
+                    out[:, d * TILE : (d + 1) * TILE] = jnp.where(slot >= 0, tile, jnp.zeros_like(tile))
+                    d += 1
+            first += width
+
+    return pl.pallas_call(
+        kernel,
+        grid=(tile_rows,),
+        out_shape=jax.ShapeDtypeStruct((nrows, n_tiles * TILE), jnp.bfloat16),
+        in_specs=[SMEM, SMEM, pl.BlockSpec((TILE, ncols), lambda i: (i, 0))] + [ANY] * len(flat),
+        out_specs=pl.BlockSpec((TILE, n_tiles * TILE), lambda i: (i, 0)),
+        scratch_shapes=[
+            pltpu.VMEM((len(pieces), sum(halves), TILE, TILE), jnp.bfloat16),
+            pltpu.SemaphoreType.DMA((len(flat),)),
+        ],
+        compiler_params=pltpu.CompilerParams(vmem_limit_bytes=VMEM_BYTES),
+        name="row_unpack",
+    )(table, place, density, *flat)
+
+
+def square_group(table, place, row_panel, chunks, spans, h, widths, shape):
+    tile_rows, tile_cols = shape
+    nrows, depth = row_panel.shape
+    n = widths[h] * TILE
+    blocks = depth // DEPTH
+    block_tiles = DEPTH // TILE
+    first_h = sum(widths[:h])
+    order = []
+    first = 0
+    for width in widths:
+        order += [(k, first + t) for k in range(ROW_GROUP) for t in range(width)]
+        first += width
+
+    def kernel(table_ref, place_ref, a_ref, *refs):
+        ins, (panel_out, square, top, bottom, a, panel, a_sems, sems, out_sem) = refs[: len(chunks)], refs[len(chunks) :]
+        c, r = place_ref[0], place_ref[1]
+
+        def a_copy(b):
+            lanes = pl.ds(pl.multiple_of(b * DEPTH, DEPTH), DEPTH)
+            return pltpu.make_async_copy(a_ref.at[:, lanes], a.at[:, lanes], a_sems.at[b])
+
+        def out_copy(b):
+            rows = pl.ds(pl.multiple_of(b * DEPTH, DEPTH), DEPTH)
+            return pltpu.make_async_copy(panel.at[rows], panel_out.at[rows], out_sem)
+
+        for b in range(blocks):
+            a_copy(b).start()
+        panel[...] = jnp.zeros_like(panel)
+        for b in range(blocks):
+            for d in range(b * block_tiles, (b + 1) * block_tiles):
+                k, t = order[d]
+                i = (r ^ k) * tile_cols + t
+                owner = i // tile_rows
+                for j in range(widths[h]):
+                    slot = table_ref[i, r * tile_cols + first_h + j]
+                    target = panel.at[d * TILE : (d + 1) * TILE, j * TILE : (j + 1) * TILE]
+                    for q, (lo, hi) in enumerate(spans[: h + 1]):
+                        @pl.when((slot >= lo) & (slot < hi))
+                        def _():
+                            source = ins[q].at[owner * (hi - lo) + slot - lo]
+                            pltpu.make_async_copy(source, target, sems.at[b]).start()
+        for b in range(blocks):
+            for d in range(b * block_tiles, (b + 1) * block_tiles):
+                k, t = order[d]
+                for j in range(widths[h]):
+                    target = panel.at[d * TILE : (d + 1) * TILE, j * TILE : (j + 1) * TILE]
+
+                    @pl.when(table_ref[(r ^ k) * tile_cols + t, r * tile_cols + first_h + j] >= 0)
+                    def _():
+                        pltpu.make_async_copy(target, target, sems.at[b]).wait()
+
+        def step(b, z):
+            a_copy(b).wait()
+            out_copy(b).start()
+            at = pl.ds(pl.multiple_of(b * DEPTH, DEPTH), DEPTH)
+            part = jnp.dot(a[:, at], panel[at, :], preferred_element_type=jnp.float32)
+
+            @pl.when(b == 0)
+            def _():
+                square[...] = part
+
+            @pl.when(b > 0)
+            def _():
+                square[...] += part
+
+            return z
+
+        lax.fori_loop(0, blocks, step, 0)
+        top[...] = square[: nrows // 2].astype(jnp.bfloat16)
+        bottom[...] = square[nrows // 2 :].astype(jnp.bfloat16)
+        for b in range(blocks):
+            out_copy(b).wait()
+
+    half = jax.ShapeDtypeStruct((nrows // 2, n), jnp.bfloat16)
+    return pl.pallas_call(
+        kernel,
+        out_shape=[
+            jax.ShapeDtypeStruct((depth, n), jnp.bfloat16), jax.ShapeDtypeStruct((nrows, n), jnp.float32), half, half,
+        ],
+        in_specs=[SMEM, SMEM, ANY] + [ANY] * len(chunks),
+        out_specs=[ANY, VMEM, VMEM, VMEM],
+        scratch_shapes=[
+            pltpu.VMEM((nrows, depth), jnp.bfloat16),
+            pltpu.VMEM((depth, n), jnp.bfloat16),
+            pltpu.SemaphoreType.DMA((blocks,)),
+            pltpu.SemaphoreType.DMA((blocks,)),
+            pltpu.SemaphoreType.DMA,
+        ],
+        compiler_params=pltpu.CompilerParams(vmem_limit_bytes=VMEM_BYTES),
+        cost_estimate=pl.CostEstimate(
+            flops=2 * nrows * depth * n, bytes_accessed=2 * depth * (nrows + 2 * n) + 6 * nrows * n, transcendentals=0
+        ),
+        name="square_group",
+    )(table, place, row_panel, *chunks)
+
+
+def cube_part(strips, panels, lo, widths, before=None, finish=None):
+    half = strips[0][0][0].shape[0]
+    nrows = 2 * half
+    sizes = [group[0][0].shape[1] for group in strips]
+    depth = ROW_GROUP * sum(sizes)
+    blocks = depth // DEPTH
+    total = sum(widths) * TILE
+    lefts, at = [], 0
+    for group, size in zip(strips, sizes):
+        for pair in group:
+            lefts += [(pair[0], 0, at, size), (pair[1], half, at, size)]
+            at += size
+    widest = max(widths) * TILE
+    firsts = [sum(widths[:h]) for h in range(len(widths))]
+    n_left, n_panels = len(lefts), len(panels)
+    operands = [x for x, *_ in lefts] + list(panels)
+    specs = [ANY] * len(operands)
+    if before is not None:
+        operands.append(before)
+        specs.append(ANY)
+    if finish is not None:
+        place, pattern_square, pattern_cube, squares = finish
+        operands += [place, pattern_square, pattern_cube, *squares]
+        specs += [SMEM] * 3 + [ANY] * len(squares)
+
+    def kernel(*refs):
+        left_refs, refs = refs[:n_left], refs[n_left:]
+        panel_refs, refs = refs[:n_panels], refs[n_panels:]
+        if before is not None:
+            before_ref, refs = refs[0], refs[1:]
+        if finish is not None:
+            (place_ref, keep_square, keep_cube), refs = refs[:3], refs[3:]
+            square_refs, refs = refs[:n_panels], refs[n_panels:]
+        out, left, right, acc, held, left_sem, right_sems, acc_sems, held_sems, out_sems = refs
+
+        def loads(h):
+            s, n = h % 2, widths[h] * TILE
+            copies = [pltpu.make_async_copy(panel_refs[h].at[pl.ds(lo, depth)], right.at[s, :, :n], right_sems.at[s])]
+            if before is not None:
+                lanes = pl.ds(firsts[h] * TILE, n)
+                copies.append(pltpu.make_async_copy(before_ref.at[:, lanes], acc.at[s, :, :n], acc_sems.at[s]))
+            if finish is not None:
+                copies.append(pltpu.make_async_copy(square_refs[h], held.at[s, :, :n], held_sems.at[s]))
+            return copies
+
+        def store(h):
+            s, n = h % 2, widths[h] * TILE
+            lanes = pl.ds(firsts[h] * TILE, n)
+            source = held if finish is not None else acc
+            return pltpu.make_async_copy(source.at[s, :, :n], out.at[:, lanes], out_sems.at[s])
+
+        left_copies = [
+            pltpu.make_async_copy(ref, left.at[pl.ds(row, half), pl.ds(col, size)], left_sem.at[0])
+            for ref, (_, row, col, size) in zip(left_refs, lefts)
+        ]
+        for copy in left_copies + loads(0):
+            copy.start()
+        for copy in left_copies:
+            copy.wait()
+        for h in range(n_panels):
+            s, n = h % 2, widths[h] * TILE
+            if h >= 1:
+                store(h - 1).wait()
+            if h + 1 < n_panels:
+                for copy in loads(h + 1):
+                    copy.start()
+            for copy in loads(h):
+                copy.wait()
+
+            def step(b, z):
+                at = pl.ds(pl.multiple_of(b * DEPTH, DEPTH), DEPTH)
+                part = jnp.dot(left[:, at], right[s, at, :n], preferred_element_type=jnp.float32)
+                if before is None:
+                    @pl.when(b == 0)
+                    def _():
+                        acc[s, :, :n] = part
+
+                    @pl.when(b > 0)
+                    def _():
+                        acc[s, :, :n] += part
+                else:
+                    acc[s, :, :n] += part
+                return z
+
+            lax.fori_loop(0, blocks, step, 0)
+            if finish is not None:
+                tile_rows, tile_cols = nrows // TILE, total // TILE
+                row, col = place_ref[0] * tile_rows, place_ref[1] * tile_cols + firsts[h]
+
+                def combine(i, z):
+                    rows = pl.ds(pl.multiple_of(i * TILE, TILE), TILE)
+                    for j in range(widths[h]):
+                        lanes = slice(j * TILE, (j + 1) * TILE)
+                        a = 3.0 * keep_square[row + i, col + j].astype(jnp.float32)
+                        b = 2.0 * keep_cube[row + i, col + j].astype(jnp.float32)
+                        held[s, rows, lanes] = a * held[s, rows, lanes] - b * acc[s, rows, lanes]
+                    return z
+
+                lax.fori_loop(0, tile_rows, combine, 0)
+            store(h).start()
+        store(n_panels - 1).wait()
+
+    return pl.pallas_call(
+        kernel,
+        out_shape=jax.ShapeDtypeStruct((nrows, total), jnp.float32),
+        in_specs=specs,
+        out_specs=ANY,
+        scratch_shapes=[
+            pltpu.VMEM((nrows, depth), jnp.bfloat16),
+            pltpu.VMEM((2, depth, widest), jnp.bfloat16),
+            pltpu.VMEM((2, nrows, widest), jnp.float32),
+            pltpu.VMEM((2, nrows, widest) if finish is not None else (2, 8, TILE), jnp.float32),
+            pltpu.SemaphoreType.DMA((1,)),
+            pltpu.SemaphoreType.DMA((2,)),
+            pltpu.SemaphoreType.DMA((2,)),
+            pltpu.SemaphoreType.DMA((2,)),
+            pltpu.SemaphoreType.DMA((2,)),
+        ],
+        compiler_params=pltpu.CompilerParams(vmem_limit_bytes=VMEM_BYTES),
+        cost_estimate=pl.CostEstimate(
+            flops=2 * nrows * depth * total, bytes_accessed=2 * depth * total + 8 * nrows * total, transcendentals=0
+        ),
+        name="cube_part",
+    )(*operands)
+
+
+def packed_step(density, table, place, pattern_square, pattern_cube, packed, spans, widths):
+    shape = density.shape[0] // TILE, density.shape[1] // TILE
+    *halves, first_chunk = packed
+
+    def swap(x, k):
+        return lax.ppermute(x, "row", [(i, i ^ k) for i in range(ROW_GROUP)])
+
+    def exchange(top, bottom):
+        by_x = swap(top, 1), swap(bottom, 1)
+        by_y = swap(top, 2), swap(bottom, 2)
+        far = swap(by_x[0], 2), swap(by_y[1], 1)
+        return by_x, by_y, far
+
+    def gather(x):
+        return lax.all_gather(x, "col", axis=0, tiled=True)
+
+    pieces = exchange(*halves)
+    chunks = [gather(first_chunk)]
+    chunks.append(gather(stage(halves, *spans[1], pieces[0][0])))
+    chunks.append(gather(stage(halves, *spans[2], pieces[2][0])))
+    row_panel = row_unpack(table, place, density, pieces, widths)
+
+    panels, squares, strips = [], [], []
+    for h in range(len(widths)):
+        if h == 1:
+            chunks.append(gather(stage(halves, *spans[3], strips[0][0][0])))
+        panel, square, top, bottom = square_group(
+            table, place, row_panel, chunks[: h + 1], spans, h, widths, shape
+        )
+        panels.append(panel)
+        squares.append(square)
+        strips.append([(top, bottom), *exchange(top, bottom)])
+
+    lo = ROW_GROUP * sum(widths[:-1]) * TILE
+    cube = cube_part(strips[:-1], panels, 0, widths)
+    return cube_part(strips[-1:], panels, lo, widths, cube, (place, pattern_square, pattern_cube, squares))
+
+
+def local(density, pattern_p, pattern_square, pattern_cube):
+    tile_rows, tile_cols = density.shape[0] // TILE, density.shape[1] // TILE
+    if lax.axis_size("row") != ROW_GROUP or tile_cols != sum(WIDTHS):
+        return dense_step(density, pattern_p, pattern_square, pattern_cube)
+    bounds = chunk_bounds(tile_rows, WIDTHS)
+    table = slot_table(pattern_p, tile_rows, tile_cols)
+    limit = np.tile(np.repeat(bounds, WIDTHS), table.shape[1] // tile_cols)
+    fits = jnp.all(table < jnp.asarray(limit, jnp.int32)[None, :])
+    place = jnp.stack([lax.axis_index("col"), lax.axis_index("row")]).astype(jnp.int32)
+    spans = list(zip([0, *bounds[:-1]], bounds))
+    cut = bounds[-1] // 2
+    packed = pack(table, place, density, [(0, cut), (cut, bounds[-1]), spans[0]])
+    return lax.cond(
+        fits,
+        lambda: packed_step(density, table, place, pattern_square, pattern_cube, packed, spans, WIDTHS),
+        lambda: dense_step(density, pattern_p, pattern_square, pattern_cube),
+    )
+
+
 def solution(mesh):
     placed = (P("col", "row"), P(), P(), P())
     return jax.shard_map(

time: 724 us -> 430 us (0.59)
  waiting for transfers between devices: 575 us -> 175 us
  Pallas kernels: 0 us -> 181 us
  matrix products: 91.3 us -> 2.63 us
  starting transfers between devices: 0.08 us -> 38.2 us
  local copies, waits for them, and re-layouts: 39.6 us -> 5.13 us
  loops' own time: 0 us -> 7.91 us
    all_gather x3 -> x4, waiting for transfers between devices: 574 us -> 0.03 us  [gather(): return lax.all_gather(x, 'col', axis=0, tiled=True)]
    pallas_call x0 -> x11, Pallas kernels: none -> 181 us  [the longest x4 87.2 us: square_group(): pl.pallas_call(kernel, out_shape=[jax.ShapeDtypeStruct((depth, n), jnp.bf...]
    ppermute x0 -> x30, waiting for transfers between devices: none -> 175 us  [swap(): return lax.ppermute(x, 'row', [(i, i ^ k) for i in range(ROW_GROUP)])]
    dot_general x2, matrix products: 91.3 us -> 2.63 us  [the longest x1 1.73 us: slot_table(): before = dot(column, jnp.asarray(left, jnp.bfloat16))]
    ppermute x0 -> x30, starting transfers between devices: none -> 38 us  [swap(): return lax.ppermute(x, 'row', [(i, i ^ k) for i in range(ROW_GROUP)])]
    unnamed x14 -> x0, local copies, waits for them, and re-layouts: 26 us -> none
    dynamic_slice x7 -> x0, local copies, waits for them, and re-layouts: 10.9 us -> none  [the longest x2 9.68 us: tile_mask(): lax.dynamic_slice(spread, (row_start % TILE, col_start % TILE), (nrows, n...]
    another operation x0 -> x1, loops' own time: none -> 7.91 us  [local(): lax.cond(fits, lambda: packed_step(density, table, place, pattern_square,...]
  transfers between devices with their start and end apart: 3 -> 34, of which waited for: 3 -> 15; matrix products, arithmetic and copies ran while one was open for 4% -> 0% of each run, Pallas kernels for 0% -> 36%
where the time goes in v1:
time: 430 us; the launch traced here: 425 us
  Pallas kernels  181 us (42%)
  waiting for transfers between devices  175 us (41%)
  starting transfers between devices  38.2 us (9%)
  between operations  14.1 us (3%)
  loops' own time  7.91 us (2%)
  local copies, waits for them, and re-layouts  5.13 us (1%)
    ppermute x30, waiting for transfers between devices, swap(): return lax.ppermute(x, 'row', [(i, i ^ k) for i in range(ROW_GROUP)])  175 us
    pallas_call x4, Pallas kernels, square_group(): pl.pallas_call(kernel, out_shape=[jax.ShapeDtypeStruct((depth, n), jnp.bf...  87.2 us
    pallas_call x2, Pallas kernels, cube_part(): pl.pallas_call(kernel, out_shape=jax.ShapeDtypeStruct((nrows, total), jnp...  69 us
    ppermute x30, starting transfers between devices, swap(): return lax.ppermute(x, 'row', [(i, i ^ k) for i in range(ROW_GROUP)])  38 us
    pallas_call x1, Pallas kernels, row_unpack(): pl.pallas_call(kernel, grid=(tile_rows,), out_shape=jax.ShapeDtypeStruct(...  14.3 us
  transfers between devices with their start and end apart: 34, of which 15 were waited for; matrix products, arithmetic and copies ran while one was open for 0% of the time, Pallas kernels for 36%

profile of v1, /device:TPU:0, one launch (start us, length us, event | category | flops | bytes accessed | tf_op | source)
XLA Modules:
  0.0 424.9 jit_solution(2068356921821554773)
XLA Ops:
  6.5 0.9 fusion.5
  7.4 1.7 compare_reduce_fusion
  9.9 7.6 %pack.1 = (bf16[43,128,128]{2,1,0:T(8,128)(2,1)S(1)}, bf16[43,128,128]{2,1,0:T(8,128)(2,1)S(1)}, bf16[28,128,128]{2,1,0:T(8,128)(2,1)}) custom-call(s32[64,64]{1,0:T(8,128)S(1)} %get-tuple-element.84.table_ref, s32[2]{0:T(128)S(1)} %pad_add_fusion.place_ref, bf16[1024,2048]{1,0:T(8,128)(2,1)} %x_ref.1), custom_call_target="tpu_custom_call" | custom-call | tf_op jit(solution)/shard_map/pack/pallas_call | solution.py:113
  17.5 400.6 %conditional.1 = (f32[1024,2048]{1,0:T(8,128)}) conditional(s32[]{:T(128)} %convert_element_type.27, (s32[64,64]{1,0:T(8,128)}, s32[64,64]{1,0:T(8,128)}, bf16[1024,2048]{1,0:T(8,128)(2,1)}, s32[64,64]{1,0:T(8,128)}) %tuple.11, (bf16[43,128,128]{2,1,0:T(8,128)(2,1)S(1)}, bf16[43,128,128]{2,1,0:T(8,128)(2,1)S(1)}, s32[64,64]{1,0:T(8,128)S(1)}, ...), branch_computations={%region_1.2_spmd, %region_2.3_spmd} | conditional | flops 68740448256 | bytes 515693568 | solution.py:477
  24.8 0.7 all-gather.14.cloned.1.call-update
  25.6 3.1 collective-permute-start
  28.7 30.9 %collective-permute-done.refs_0_.after_ref = bf16[43,128,128]{2,1,0:T(8,128)(2,1)S(1)} collective-permute-done((bf16[43,128,128]{2,1,0:T(8,128)(2,1)S(1)}, bf16[43,128,128]{2,1,0:T(8,128)(2,1)S(1)}, u32[]{:S(2)}, u32[]{:S(2)}) %collective-permute-start) | collective-permute-done | bytes 1409056 | tf_op jit(solution)/shard_map/cond/branch_1_fun/ppermute | solution.py:432
  59.6 1.1 copy-done
  60.7 1.5 stage.3
  62.2 1.7 collective-permute-start.4
  63.9 30.9 %collective-permute-done.4.refs_4_.after_ref = bf16[43,128,128]{2,1,0:T(8,128)(2,1)} collective-permute-done((bf16[43,128,128]{2,1,0:T(8,128)(2,1)}, bf16[43,128,128]{2,1,0:T(8,128)(2,1)}, u32[]{:S(2)}, u32[]{:S(2)}) %collective-permute-start.4) | collective-permute-done | bytes 1409056 | tf_op jit(solution)/shard_map/cond/branch_1_fun/ppermute | solution.py:432
  94.8 1.1 stage.4
  95.9 1.3 collective-permute-start.3
  97.2 1.6 collective-permute-start.1
  98.8 0.6 collective-permute-start.2
  99.4 30.4 %collective-permute-done.3.refs_3_ = bf16[43,128,128]{2,1,0:T(8,128)(2,1)S(1)} collective-permute-done((bf16[43,128,128]{2,1,0:T(8,128)(2,1)S(1)}, bf16[43,128,128]{2,1,0:T(8,128)(2,1)S(1)}, u32[]{:S(2)}, u32[]{:S(2)}) %collective-permute-start.3) | collective-permute-done | bytes 1409056 | tf_op jit(solution)/shard_map/cond/branch_1_fun/ppermute | solution.py:432
  129.8 1.4 collective-permute-start.5
  131.2 26.2 %collective-permute-done.2.refs_2_ = bf16[43,128,128]{2,1,0:T(8,128)(2,1)S(1)} collective-permute-done((bf16[43,128,128]{2,1,0:T(8,128)(2,1)S(1)}, bf16[43,128,128]{2,1,0:T(8,128)(2,1)S(1)}, u32[]{:S(2)}, u32[]{:S(2)}) %collective-permute-start.2) | collective-permute-done | bytes 1409056 | tf_op jit(solution)/shard_map/cond/branch_1_fun/ppermute | solution.py:432
  157.5 0.5 collective-permute-done.5.refs_5_
  158.0 0.6 copy-done.3
  158.6 0.5 copy-done.4
  159.1 14.3 %row_unpack.1.a_ref = bf16[1024,8192]{1,0:T(8,128)(2,1)} custom-call(s32[64,64]{1,0:T(8,128)S(1)} %get-tuple-element.36.table_ref, s32[2]{0:T(128)S(1)} %get-tuple-element.37.place_ref.refs_13_, bf16[1024,2048]{1,0:T(8,128)(2,1)} %get-tuple-element.38.x_ref, bf16[43,128,128]{2,1,0:T(8,128)(2,1)} %copy-done, bf16[43,128,128]{2,1,0:T(8,128)(2,1)} %copy-done.2, ...), custom_call_target="tpu_custom_call" | custom-call | tf_op jit(solution)/shard_map/cond/branch_1_fun/row_unpack/pallas_call | solution.py:190
  173.4 22.3 %square_group.4 = (bf16[8192,512]{1,0:T(8,128)(2,1)}, f32[1024,512]{1,0:T(8,128)}, bf16[512,512]{1,0:T(8,128)(2,1)}, bf16[512,512]{1,0:T(8,128)(2,1)}) custom-call(s32[64,64]{1,0:T(8,128)S(1)} %get-tuple-element.36.table_ref, s32[2]{0:T(128)S(1)} %get-tuple-element.37.place_ref.refs_13_, bf16[1024,8192]{1,0:T(8,128)(2,1)} %row_unpack.1.a_ref, ...), custom_call_target="tpu_custom_call" | custom-call | flops 8589934592 | bytes 36700160 | tf_op jit(solution)/shard_map/cond/branch_1_fun/square_group/pallas_call | solution.py:279
  195.7 0.9 stage.5
  196.7 2.3 collective-permute-start.14
  199.0 0.9 collective-permute-start.13
  199.9 0.8 collective-permute-start.15
  200.7 20.5 %square_group.6 = (bf16[8192,512]{1,0:T(8,128)(2,1)}, f32[1024,512]{1,0:T(8,128)}, bf16[512,512]{1,0:T(8,128)(2,1)}, bf16[512,512]{1,0:T(8,128)(2,1)}) custom-call(s32[64,64]{1,0:T(8,128)S(1)} %get-tuple-element.36.table_ref, s32[2]{0:T(128)S(1)} %get-tuple-element.37.place_ref.refs_13_, bf16[1024,8192]{1,0:T(8,128)(2,1)} %row_unpack.1.a_ref, ...), custom_call_target="tpu_custom_call" | custom-call | flops 8589934592 | bytes 36700160 | tf_op jit(solution)/shard_map/cond/branch_1_fun/square_group/pallas_call | solution.py:279
  221.3 2.9 collective-permute-start.18
  224.2 23.2 %square_group.7 = (bf16[8192,512]{1,0:T(8,128)(2,1)}, f32[1024,512]{1,0:T(8,128)}, bf16[512,512]{1,0:T(8,128)(2,1)}, bf16[512,512]{1,0:T(8,128)(2,1)}) custom-call(s32[64,64]{1,0:T(8,128)S(1)} %get-tuple-element.36.table_ref, s32[2]{0:T(128)S(1)} %get-tuple-element.37.place_ref.refs_13_, bf16[1024,8192]{1,0:T(8,128)(2,1)} %row_unpack.1.a_ref, ...), custom_call_target="tpu_custom_call" | custom-call | flops 8589934592 | bytes 36700160 | tf_op jit(solution)/shard_map/cond/branch_1_fun/square_group/pallas_call | solution.py:279
  247.4 2.0 collective-permute-start.20
  249.5 0.3 collective-permute-start.19
  249.8 1.7 collective-permute-start.24
  251.6 0.3 collective-permute-start.25
  251.9 12.7 %collective-permute-done.19.refs_11_ = bf16[512,512]{1,0:T(8,128)(2,1)S(1)} collective-permute-done((bf16[512,512]{1,0:T(8,128)(2,1)}, bf16[512,512]{1,0:T(8,128)(2,1)S(1)}, u32[]{:S(2)}, u32[]{:S(2)}) %collective-permute-start.19) | collective-permute-done | bytes 524320 | tf_op jit(solution)/shard_map/cond/branch_1_fun/ppermute | solution.py:432
  264.6 1.9 collective-permute-start.27
  266.6 7.0 %collective-permute-done.21.refs_13_ = bf16[512,512]{1,0:T(8,128)(2,1)S(1)} collective-permute-done((bf16[512,512]{1,0:T(8,128)(2,1)}, bf16[512,512]{1,0:T(8,128)(2,1)S(1)}, u32[]{:S(2)}, u32[]{:S(2)}) %collective-permute-start.21) | collective-permute-done | bytes 524320 | tf_op jit(solution)/shard_map/cond/branch_1_fun/ppermute | solution.py:432
  273.6 2.0 collective-permute-start.16
  275.5 0.3 collective-permute-done.24.refs_18_
  275.9 0.3 collective-permute-start.17
  276.1 10.9 %collective-permute-done.25.refs_19_ = bf16[512,512]{1,0:T(8,128)(2,1)S(1)} collective-permute-done((bf16[512,512]{1,0:T(8,128)(2,1)}, bf16[512,512]{1,0:T(8,128)(2,1)S(1)}, u32[]{:S(2)}, u32[]{:S(2)}) %collective-permute-start.25) | collective-permute-done | bytes 524320 | tf_op jit(solution)/shard_map/cond/branch_1_fun/ppermute | solution.py:432
  287.0 0.8 copy-done.25
  287.9 21.2 %square_group.5 = (bf16[8192,512]{1,0:T(8,128)(2,1)}, f32[1024,512]{1,0:T(8,128)}, bf16[512,512]{1,0:T(8,128)(2,1)}, bf16[512,512]{1,0:T(8,128)(2,1)}) custom-call(s32[64,64]{1,0:T(8,128)S(1)} %get-tuple-element.36.table_ref, s32[2]{0:T(128)S(1)} %get-tuple-element.37.place_ref.refs_13_, bf16[1024,8192]{1,0:T(8,128)(2,1)} %row_unpack.1.a_ref, ...), custom_call_target="tpu_custom_call" | custom-call | flops 8589934592 | bytes 36700160 | tf_op jit(solution)/shard_map/cond/branch_1_fun/square_group/pallas_call | solution.py:279
  309.2 0.3 collective-permute-start.23
  309.5 4.3 %collective-permute-start.28 = (bf16[512,512]{1,0:T(8,128)(2,1)}, bf16[512,512]{1,0:T(8,128)(2,1)S(1)}, u32[]{:S(2)}, u32[]{:S(2)}) collective-permute-start(bf16[512,512]{1,0:T(8,128)(2,1)} %collective-permute-done.24.refs_18_), channel_id=1, source_target_pairs={{0,16},{8,24},{16,0},{24,8},{1,17},{9,25},{17,1},{25,9},{2,18},{10... | collective-permute-start | bytes 1572872 | tf_op jit(solution)/shard_map/cond/branch_1_fun/ppermute | solution.py:432
  313.9 1.2 collective-permute-start.6
  315.1 3.5 collective-permute-done.22.refs_14_
  318.6 0.3 collective-permute-start.29
  318.9 5.3 %collective-permute-done.23.refs_15_ = bf16[512,512]{1,0:T(8,128)(2,1)} collective-permute-done((bf16[512,512]{1,0:T(8,128)(2,1)S(1)}, bf16[512,512]{1,0:T(8,128)(2,1)}, u32[]{:S(2)}, u32[]{:S(2)}) %collective-permute-start.23) | collective-permute-done | bytes 524320 | tf_op jit(solution)/shard_map/cond/branch_1_fun/ppermute | solution.py:432
  324.2 0.3 collective-permute-start.7
  324.5 5.2 %collective-permute-done.28.refs_22_ = bf16[512,512]{1,0:T(8,128)(2,1)S(1)} collective-permute-done((bf16[512,512]{1,0:T(8,128)(2,1)}, bf16[512,512]{1,0:T(8,128)(2,1)S(1)}, u32[]{:S(2)}, u32[]{:S(2)}) %collective-permute-start.28) | collective-permute-done | bytes 524320 | tf_op jit(solution)/shard_map/cond/branch_1_fun/ppermute | solution.py:432
  329.8 2.0 collective-permute-start.8
  331.7 3.6 collective-permute-done.6.refs_2_
  335.4 3.7 collective-permute-start.10
  339.1 1.9 collective-permute-done.9.refs_5_
  341.0 0.3 collective-permute-start.11
  341.3 5.3 %collective-permute-done.29.refs_23_ = bf16[512,512]{1,0:T(8,128)(2,1)S(1)} collective-permute-done((bf16[512,512]{1,0:T(8,128)(2,1)}, bf16[512,512]{1,0:T(8,128)(2,1)S(1)}, u32[]{:S(2)}, u32[]{:S(2)}) %collective-permute-start.29) | collective-permute-done | bytes 524320 | tf_op jit(solution)/shard_map/cond/branch_1_fun/ppermute | solution.py:432
  346.6 0.8 copy-done.27
  347.4 46.5 %cube_part.2.refs_12_ = f32[1024,2048]{1,0:T(8,128)} custom-call(bf16[512,512]{1,0:T(8,128)(2,1)} %get-tuple-element.42.after_ref.refs_0_, bf16[512,512]{1,0:T(8,128)(2,1)} %get-tuple-element.49.refs_1_, bf16[512,512]{1,0:T(8,128)(2,1)} %copy-done.16, bf16[512,512]{1,0:T(8,128)(2,1)} %copy-done.18, bf16[512,512]{1,0:T(8,128)(2,1)} %copy-done.17, ...), custom_call_target="tpu_custom_call" | custom-call | flops 25769803776 | bytes 41943040 | tf_op jit(solution)/shard_map/cond/branch_1_fun/cube_part/pallas_call | solution.py:403
  394.0 0.7 copy-done.7
  394.7 0.2 copy-done.8
  394.9 0.1 copy-done.9
  395.0 0.2 copy-done.10
  395.2 22.5 %cube_part.3 = f32[1024,2048]{1,0:T(8,128)} custom-call(bf16[512,512]{1,0:T(8,128)(2,1)} %get-tuple-element.43.refs_0_, bf16[512,512]{1,0:T(8,128)(2,1)} %get-tuple-element.44.refs_1_, bf16[512,512]{1,0:T(8,128)(2,1)} %copy-done.5, bf16[512,512]{1,0:T(8,128)(2,1)} %copy-done.7, bf16[512,512]{1,0:T(8,128)(2,1)} %copy-done.8, bf16[512,512]{1,0:T(8,128)(2,1)} %copy-done.6, ...), custom_call_target="tpu_custom_call" | custom-call | flops 8589934592 | bytes 25165824 | tf_op jit(solution)/shard_map/cond/branch_1_fun/cube_part/pallas_call | solution.py:403
  (77 shorter events, 0.9 us)
Async XLA Ops:
  24.8 263.1 %copy-start.14 = (s32[2]{0:T(128)}, s32[2]{0:T(128)S(1)}, u32[]{:S(2)}) copy-start(s32[2]{0:T(128)S(1)} %get-tuple-element.37.place_ref.refs_13_) | copy-start | bytes 28 | tf_op jit(solution)/shard_map/cond
  24.8 148.6 %all-gather.14.cloned.1.call-start = ((), (), s32[]{:S(2)}) async-start(), calls=%async_computation.3 | async-start | bytes 8257536 | tf_op jit(solution)/shard_map/cond/branch_1_fun/all_gather | solution.py:441
  25.5 175.2 %all-gather.16.cloned.1.call-start = ((), (), s32[]{:S(2)}) async-start(), calls=%async_computation.4 | async-start | bytes 6488064 | tf_op jit(solution)/shard_map/cond/branch_1_fun/all_gather | solution.py:441
  25.6 34.0 %collective-permute-start = (bf16[43,128,128]{2,1,0:T(8,128)(2,1)S(1)}, bf16[43,128,128]{2,1,0:T(8,128)(2,1)S(1)}, u32[]{:S(2)}, u32[]{:S(2)}) collective-permute-start(bf16[43,128,128]{2,1,0:T(8,128)(2,1)S(1)} %get-tuple-element.39.h0), channel_id=1, source_target_pairs={{0,8},{8,0},{16,24},{24,16},{1,9},{9,1},{17,25},{25,17},{2,10},{10... | collective-permute-start | bytes 4227080 | tf_op jit(solution)/shard_map/cond/branch_1_fun/ppermute | solution.py:432
  59.6 1.1 copy-start
  62.2 162.1 %all-gather.18.cloned.1.call-start = ((), (), s32[]{:S(2)}) async-start(), calls=%async_computation.5 | async-start | bytes 5898240 | tf_op jit(solution)/shard_map/cond/branch_1_fun/all_gather | solution.py:441
  62.2 32.6 %collective-permute-start.4 = (bf16[43,128,128]{2,1,0:T(8,128)(2,1)}, bf16[43,128,128]{2,1,0:T(8,128)(2,1)}, u32[]{:S(2)}, u32[]{:S(2)}) collective-permute-start(bf16[43,128,128]{2,1,0:T(8,128)(2,1)} %copy-done), channel_id=1, source_target_pairs={{0,16},{8,24},{16,0},{24,8},{1,17},{9,25},{17,1},{25,9},{2,18},{10... | collective-permute-start | bytes 4227080 | tf_op jit(solution)/shard_map/cond/branch_1_fun/ppermute | solution.py:432
  95.9 192.0 %all-gather.20.cloned.1.call-start = ((), (), s32[]{:S(2)}) async-start(), calls=%async_computation.6 | async-start | bytes 4718592 | tf_op jit(solution)/shard_map/cond/branch_1_fun/all_gather | solution.py:441
  95.9 33.9 %collective-permute-start.3 = (bf16[43,128,128]{2,1,0:T(8,128)(2,1)S(1)}, bf16[43,128,128]{2,1,0:T(8,128)(2,1)S(1)}, u32[]{:S(2)}, u32[]{:S(2)}) collective-permute-start(bf16[43,128,128]{2,1,0:T(8,128)(2,1)S(1)} %get-tuple-element.40.h1), channel_id=1, source_target_pairs={{0,16},{8,24},{16,0},{24,8},{1,17},{9,25},{17,1},{25,9},{2,18},{10... | collective-permute-start | bytes 4227080 | tf_op jit(solution)/shard_map/cond/branch_1_fun/ppermute | solution.py:432
  97.2 34.0 %collective-permute-start.1 = (bf16[43,128,128]{2,1,0:T(8,128)(2,1)S(1)}, bf16[43,128,128]{2,1,0:T(8,128)(2,1)S(1)}, u32[]{:S(2)}, u32[]{:S(2)}) collective-permute-start(bf16[43,128,128]{2,1,0:T(8,128)(2,1)S(1)} %get-tuple-element.40.h1), channel_id=1, source_target_pairs={{0,8},{8,0},{16,24},{24,16},{1,9},{9,1},{17,25},{25,17},{2,10},{10... | collective-permute-start | bytes 4227080 | tf_op jit(solution)/shard_map/cond/branch_1_fun/ppermute | solution.py:432
  98.8 58.6 %collective-permute-start.2 = (bf16[43,128,128]{2,1,0:T(8,128)(2,1)S(1)}, bf16[43,128,128]{2,1,0:T(8,128)(2,1)S(1)}, u32[]{:S(2)}, u32[]{:S(2)}) collective-permute-start(bf16[43,128,128]{2,1,0:T(8,128)(2,1)S(1)} %get-tuple-element.39.h0), channel_id=1, source_target_pairs={{0,16},{8,24},{16,0},{24,8},{1,17},{9,25},{17,1},{25,9},{2,18},{10... | collective-permute-start | bytes 4227080 | tf_op jit(solution)/shard_map/cond/branch_1_fun/ppermute | solution.py:432
  129.8 27.6 %copy-start.1 = (bf16[43,128,128]{2,1,0:T(8,128)(2,1)}, bf16[43,128,128]{2,1,0:T(8,128)(2,1)S(1)}, u32[]{:S(2)}) copy-start(bf16[43,128,128]{2,1,0:T(8,128)(2,1)S(1)} %collective-permute-done.3.refs_3_) | copy-start | bytes 4227076 | tf_op jit(solution)/shard_map/cond
  129.8 28.2 %collective-permute-start.5 = (bf16[43,128,128]{2,1,0:T(8,128)(2,1)S(1)}, bf16[43,128,128]{2,1,0:T(8,128)(2,1)S(1)}, u32[]{:S(2)}, u32[]{:S(2)}) collective-permute-start(bf16[43,128,128]{2,1,0:T(8,128)(2,1)S(1)} %collective-permute-done.3.refs_3_), channel_id=1, source_target_pairs={{0,8},{8,0},{16,24},{24,16},{1,9},{9,1},{17,25},{25,17},{2,10},{10... | collective-permute-start | bytes 4227080 | tf_op jit(solution)/shard_map/cond/branch_1_fun/ppermute | solution.py:432
  131.2 26.7 %copy-start.2 = (bf16[43,128,128]{2,1,0:T(8,128)(2,1)}, bf16[43,128,128]{2,1,0:T(8,128)(2,1)S(1)}, u32[]{:S(2)}) copy-start(bf16[43,128,128]{2,1,0:T(8,128)(2,1)S(1)} %collective-permute-done.1.refs_1_) | copy-start | bytes 4227076 | tf_op jit(solution)/shard_map/cond
  157.5 1.1 copy-start.3
  158.0 1.1 copy-start.4
  196.6 50.8 %collective-permute-start.12 = (bf16[512,512]{1,0:T(8,128)(2,1)}, bf16[512,512]{1,0:T(8,128)(2,1)S(1)}, u32[]{:S(2)}, u32[]{:S(2)}) collective-permute-start(bf16[512,512]{1,0:T(8,128)(2,1)} %get-tuple-element.42.after_ref.refs_0_), channel_id=1, source_target_pairs={{0,8},{8,0},{16,24},{24,16},{1,9},{9,1},{17,25},{25,17},{2,10},{10... | collective-permute-start | bytes 1572872 | tf_op jit(solution)/shard_map/cond/branch_1_fun/ppermute | solution.py:432
  196.7 53.0 %collective-permute-start.14 = (bf16[512,512]{1,0:T(8,128)(2,1)}, bf16[512,512]{1,0:T(8,128)(2,1)S(1)}, u32[]{:S(2)}, u32[]{:S(2)}) collective-permute-start(bf16[512,512]{1,0:T(8,128)(2,1)} %get-tuple-element.42.after_ref.refs_0_), channel_id=1, source_target_pairs={{0,16},{8,24},{16,0},{24,8},{1,17},{9,25},{17,1},{25,9},{2,18},{10... | collective-permute-start | bytes 1572872 | tf_op jit(solution)/shard_map/cond/branch_1_fun/ppermute | solution.py:432
  199.0 50.4 %collective-permute-start.13 = (bf16[512,512]{1,0:T(8,128)(2,1)}, bf16[512,512]{1,0:T(8,128)(2,1)S(1)}, u32[]{:S(2)}, u32[]{:S(2)}) collective-permute-start(bf16[512,512]{1,0:T(8,128)(2,1)} %get-tuple-element.49.refs_1_), channel_id=1, source_target_pairs={{0,8},{8,0},{16,24},{24,16},{1,9},{9,1},{17,25},{25,17},{2,10},{10... | collective-permute-start | bytes 1572872 | tf_op jit(solution)/shard_map/cond/branch_1_fun/ppermute | solution.py:432
  199.9 50.0 %collective-permute-start.15 = (bf16[512,512]{1,0:T(8,128)(2,1)}, bf16[512,512]{1,0:T(8,128)(2,1)S(1)}, u32[]{:S(2)}, u32[]{:S(2)}) collective-permute-start(bf16[512,512]{1,0:T(8,128)(2,1)} %get-tuple-element.49.refs_1_), channel_id=1, source_target_pairs={{0,16},{8,24},{16,0},{24,8},{1,17},{9,25},{17,1},{25,9},{2,18},{10... | collective-permute-start | bytes 1572872 | tf_op jit(solution)/shard_map/cond/branch_1_fun/ppermute | solution.py:432
  221.3 26.1 %copy-start.20 = (bf16[512,512]{1,0:T(8,128)(2,1)S(1)}, bf16[512,512]{1,0:T(8,128)(2,1)}, u32[]{:S(2)}) copy-start(bf16[512,512]{1,0:T(8,128)(2,1)} %get-tuple-element.50.refs_8_) | copy-start | bytes 1572868 | tf_op jit(solution)/shard_map/cond
  221.3 30.3 %collective-permute-start.18 = (bf16[512,512]{1,0:T(8,128)(2,1)}, bf16[512,512]{1,0:T(8,128)(2,1)}, u32[]{:S(2)}, u32[]{:S(2)}) collective-permute-start(bf16[512,512]{1,0:T(8,128)(2,1)} %get-tuple-element.50.refs_8_), channel_id=1, source_target_pairs={{0,8},{8,0},{16,24},{24,16},{1,9},{9,1},{17,25},{25,17},{2,10},{10... | collective-permute-start | bytes 1572872 | tf_op jit(solution)/shard_map/cond/branch_1_fun/ppermute | solution.py:432
  247.4 61.8 %copy-start.16 = (bf16[512,512]{1,0:T(8,128)(2,1)}, bf16[512,512]{1,0:T(8,128)(2,1)S(1)}, u32[]{:S(2)}) copy-start(bf16[512,512]{1,0:T(8,128)(2,1)S(1)} %collective-permute-done.12.refs_2_) | copy-start | bytes 1572868 | tf_op jit(solution)/shard_map/cond
  247.4 17.2 %collective-permute-start.20 = (bf16[512,512]{1,0:T(8,128)(2,1)S(1)}, bf16[512,512]{1,0:T(8,128)(2,1)S(1)}, u32[]{:S(2)}, u32[]{:S(2)}) collective-permute-start(bf16[512,512]{1,0:T(8,128)(2,1)S(1)} %copy-done.20), channel_id=1, source_target_pairs={{0,16},{8,24},{16,0},{24,8},{1,17},{9,25},{17,1},{25,9},{2,18},{10... | collective-permute-start | bytes 1572872 | tf_op jit(solution)/shard_map/cond/branch_1_fun/ppermute | solution.py:432
  249.4 59.7 %copy-start.18 = (bf16[512,512]{1,0:T(8,128)(2,1)}, bf16[512,512]{1,0:T(8,128)(2,1)S(1)}, u32[]{:S(2)}) copy-start(bf16[512,512]{1,0:T(8,128)(2,1)S(1)} %collective-permute-done.13.refs_3_) | copy-start | bytes 1572868 | tf_op jit(solution)/shard_map/cond
  249.5 15.1 %collective-permute-start.19 = (bf16[512,512]{1,0:T(8,128)(2,1)}, bf16[512,512]{1,0:T(8,128)(2,1)S(1)}, u32[]{:S(2)}, u32[]{:S(2)}) collective-permute-start(bf16[512,512]{1,0:T(8,128)(2,1)} %get-tuple-element.51.refs_9_), channel_id=1, source_target_pairs={{0,8},{8,0},{16,24},{24,16},{1,9},{9,1},{17,25},{25,17},{2,10},{10... | collective-permute-start | bytes 1572872 | tf_op jit(solution)/shard_map/cond/branch_1_fun/ppermute | solution.py:432
  249.7 59.5 %copy-start.17 = (bf16[512,512]{1,0:T(8,128)(2,1)}, bf16[512,512]{1,0:T(8,128)(2,1)S(1)}, u32[]{:S(2)}) copy-start(bf16[512,512]{1,0:T(8,128)(2,1)S(1)} %collective-permute-done.14.refs_4_) | copy-start | bytes 1572868 | tf_op jit(solution)/shard_map/cond
  249.7 23.9 %collective-permute-start.21 = (bf16[512,512]{1,0:T(8,128)(2,1)}, bf16[512,512]{1,0:T(8,128)(2,1)S(1)}, u32[]{:S(2)}, u32[]{:S(2)}) collective-permute-start(bf16[512,512]{1,0:T(8,128)(2,1)} %get-tuple-element.51.refs_9_), channel_id=1, source_target_pairs={{0,16},{8,24},{16,0},{24,8},{1,17},{9,25},{17,1},{25,9},{2,18},{10... | collective-permute-start | bytes 1572872 | tf_op jit(solution)/shard_map/cond/branch_1_fun/ppermute | solution.py:432
  249.8 59.3 %copy-start.19 = (bf16[512,512]{1,0:T(8,128)(2,1)}, bf16[512,512]{1,0:T(8,128)(2,1)S(1)}, u32[]{:S(2)}) copy-start(bf16[512,512]{1,0:T(8,128)(2,1)S(1)} %collective-permute-done.15.refs_5_) | copy-start | bytes 1572868 | tf_op jit(solution)/shard_map/cond
  249.8 26.0 %collective-permute-start.24 = (bf16[512,512]{1,0:T(8,128)(2,1)}, bf16[512,512]{1,0:T(8,128)(2,1)}, u32[]{:S(2)}, u32[]{:S(2)}) collective-permute-start(bf16[512,512]{1,0:T(8,128)(2,1)} %get-tuple-element.52.refs_16_), channel_id=1, source_target_pairs={{0,8},{8,0},{16,24},{24,16},{1,9},{9,1},{17,25},{25,17},{2,10},{10... | collective-permute-start | bytes 1572872 | tf_op jit(solution)/shard_map/cond/branch_1_fun/ppermute | solution.py:432
  251.6 35.4 %collective-permute-start.25 = (bf16[512,512]{1,0:T(8,128)(2,1)}, bf16[512,512]{1,0:T(8,128)(2,1)S(1)}, u32[]{:S(2)}, u32[]{:S(2)}) collective-permute-start(bf16[512,512]{1,0:T(8,128)(2,1)} %get-tuple-element.53.refs_17_), channel_id=1, source_target_pairs={{0,8},{8,0},{16,24},{24,16},{1,9},{9,1},{17,25},{25,17},{2,10},{10... | collective-permute-start | bytes 1572872 | tf_op jit(solution)/shard_map/cond/branch_1_fun/ppermute | solution.py:432
  264.5 11.3 %copy-start.22 = (bf16[512,512]{1,0:T(8,128)(2,1)}, bf16[512,512]{1,0:T(8,128)(2,1)S(1)}, u32[]{:S(2)}) copy-start(bf16[512,512]{1,0:T(8,128)(2,1)S(1)} %collective-permute-done.19.refs_11_) | copy-start | bytes 1572868 | tf_op jit(solution)/shard_map/cond
  264.5 44.7 %collective-permute-start.26 = (bf16[512,512]{1,0:T(8,128)(2,1)}, bf16[512,512]{1,0:T(8,128)(2,1)}, u32[]{:S(2)}, u32[]{:S(2)}) collective-permute-start(bf16[512,512]{1,0:T(8,128)(2,1)} %get-tuple-element.52.refs_16_), channel_id=1, source_target_pairs={{0,16},{8,24},{16,0},{24,8},{1,17},{9,25},{17,1},{25,9},{2,18},{10... | collective-permute-start | bytes 1572872 | tf_op jit(solution)/shard_map/cond/branch_1_fun/ppermute | solution.py:432
  264.6 10.9 %copy-start.21 = (bf16[512,512]{1,0:T(8,128)(2,1)}, bf16[512,512]{1,0:T(8,128)(2,1)S(1)}, u32[]{:S(2)}) copy-start(bf16[512,512]{1,0:T(8,128)(2,1)S(1)} %collective-permute-done.20.refs_12_) | copy-start | bytes 1572868 | tf_op jit(solution)/shard_map/cond
  264.6 44.9 %collective-permute-start.27 = (bf16[512,512]{1,0:T(8,128)(2,1)}, bf16[512,512]{1,0:T(8,128)(2,1)}, u32[]{:S(2)}, u32[]{:S(2)}) collective-permute-start(bf16[512,512]{1,0:T(8,128)(2,1)} %get-tuple-element.53.refs_17_), channel_id=1, source_target_pairs={{0,16},{8,24},{16,0},{24,8},{1,17},{9,25},{17,1},{25,9},{2,18},{10... | collective-permute-start | bytes 1572872 | tf_op jit(solution)/shard_map/cond/branch_1_fun/ppermute | solution.py:432
  273.6 2.6 copy-start.23
  273.6 40.3 %collective-permute-start.16 = (bf16[512,512]{1,0:T(8,128)(2,1)S(1)}, bf16[512,512]{1,0:T(8,128)(2,1)}, u32[]{:S(2)}, u32[]{:S(2)}) collective-permute-start(bf16[512,512]{1,0:T(8,128)(2,1)S(1)} %collective-permute-done.12.refs_2_), channel_id=1, source_target_pairs={{0,16},{8,24},{16,0},{24,8},{1,17},{9,25},{17,1},{25,9},{2,18},{10... | collective-permute-start | bytes 1572872 | tf_op jit(solution)/shard_map/cond/branch_1_fun/ppermute | solution.py:432
  275.9 39.2 %collective-permute-start.17 = (bf16[512,512]{1,0:T(8,128)(2,1)S(1)}, bf16[512,512]{1,0:T(8,128)(2,1)}, u32[]{:S(2)}, u32[]{:S(2)}) collective-permute-start(bf16[512,512]{1,0:T(8,128)(2,1)S(1)} %collective-permute-done.15.refs_5_), channel_id=1, source_target_pairs={{0,8},{8,0},{16,24},{24,16},{1,9},{9,1},{17,25},{25,17},{2,10},{10... | collective-permute-start | bytes 1572872 | tf_op jit(solution)/shard_map/cond/branch_1_fun/ppermute | solution.py:432
  287.0 0.8 copy-start.25
  287.8 21.4 %copy-start.24 = (bf16[512,512]{1,0:T(8,128)(2,1)S(1)}, bf16[512,512]{1,0:T(8,128)(2,1)}, u32[]{:S(2)}) copy-start(bf16[512,512]{1,0:T(8,128)(2,1)} %copy-done.23) | copy-start | bytes 1572868 | tf_op jit(solution)/shard_map/cond
  287.8 30.8 %collective-permute-start.22 = (bf16[512,512]{1,0:T(8,128)(2,1)}, bf16[512,512]{1,0:T(8,128)(2,1)}, u32[]{:S(2)}, u32[]{:S(2)}) collective-permute-start(bf16[512,512]{1,0:T(8,128)(2,1)} %collective-permute-done.18.refs_10_), channel_id=1, source_target_pairs={{0,16},{8,24},{16,0},{24,8},{1,17},{9,25},{17,1},{25,9},{2,18},{10... | collective-permute-start | bytes 1572872 | tf_op jit(solution)/shard_map/cond/branch_1_fun/ppermute | solution.py:432
  309.2 15.0 %collective-permute-start.23 = (bf16[512,512]{1,0:T(8,128)(2,1)S(1)}, bf16[512,512]{1,0:T(8,128)(2,1)}, u32[]{:S(2)}, u32[]{:S(2)}) collective-permute-start(bf16[512,512]{1,0:T(8,128)(2,1)S(1)} %copy-done.24), channel_id=1, source_target_pairs={{0,8},{8,0},{16,24},{24,16},{1,9},{9,1},{17,25},{25,17},{2,10},{10... | collective-permute-start | bytes 1572872 | tf_op jit(solution)/shard_map/cond/branch_1_fun/ppermute | solution.py:432
  309.5 20.2 %collective-permute-start.28 = (bf16[512,512]{1,0:T(8,128)(2,1)}, bf16[512,512]{1,0:T(8,128)(2,1)S(1)}, u32[]{:S(2)}, u32[]{:S(2)}) collective-permute-start(bf16[512,512]{1,0:T(8,128)(2,1)} %collective-permute-done.24.refs_18_), channel_id=1, source_target_pairs={{0,16},{8,24},{16,0},{24,8},{1,17},{9,25},{17,1},{25,9},{2,18},{10... | collective-permute-start | bytes 1572872 | tf_op jit(solution)/shard_map/cond/branch_1_fun/ppermute | solution.py:432
  313.9 21.5 %collective-permute-start.6 = (bf16[512,512]{1,0:T(8,128)(2,1)}, bf16[512,512]{1,0:T(8,128)(2,1)S(1)}, u32[]{:S(2)}, u32[]{:S(2)}) collective-permute-start(bf16[512,512]{1,0:T(8,128)(2,1)} %get-tuple-element.43.refs_0_), channel_id=1, source_target_pairs={{0,8},{8,0},{16,24},{24,16},{1,9},{9,1},{17,25},{25,17},{2,10},{10... | collective-permute-start | bytes 1572872 | tf_op jit(solution)/shard_map/cond/branch_1_fun/ppermute | solution.py:432
  315.0 25.9 %collective-permute-start.9 = (bf16[512,512]{1,0:T(8,128)(2,1)}, bf16[512,512]{1,0:T(8,128)(2,1)S(1)}, u32[]{:S(2)}, u32[]{:S(2)}) collective-permute-start(bf16[512,512]{1,0:T(8,128)(2,1)} %get-tuple-element.44.refs_1_), channel_id=1, source_target_pairs={{0,16},{8,24},{16,0},{24,8},{1,17},{9,25},{17,1},{25,9},{2,18},{10... | collective-permute-start | bytes 1572872 | tf_op jit(solution)/shard_map/cond/branch_1_fun/ppermute | solution.py:432
  318.6 28.0 %collective-permute-start.29 = (bf16[512,512]{1,0:T(8,128)(2,1)}, bf16[512,512]{1,0:T(8,128)(2,1)S(1)}, u32[]{:S(2)}, u32[]{:S(2)}) collective-permute-start(bf16[512,512]{1,0:T(8,128)(2,1)} %collective-permute-done.27.refs_21_), channel_id=1, source_target_pairs={{0,8},{8,0},{16,24},{24,16},{1,9},{9,1},{17,25},{25,17},{2,10},{10... | collective-permute-start | bytes 1572872 | tf_op jit(solution)/shard_map/cond/branch_1_fun/ppermute | solution.py:432
  324.2 69.6 %collective-permute-start.7 = (bf16[512,512]{1,0:T(8,128)(2,1)}, bf16[512,512]{1,0:T(8,128)(2,1)S(1)}, u32[]{:S(2)}, u32[]{:S(2)}) collective-permute-start(bf16[512,512]{1,0:T(8,128)(2,1)} %get-tuple-element.44.refs_1_), channel_id=1, source_target_pairs={{0,8},{8,0},{16,24},{24,16},{1,9},{9,1},{17,25},{25,17},{2,10},{10... | collective-permute-start | bytes 1572872 | tf_op jit(solution)/shard_map/cond/branch_1_fun/ppermute | solution.py:432
  329.8 16.9 %copy-start.26 = (bf16[512,512]{1,0:T(8,128)(2,1)}, bf16[512,512]{1,0:T(8,128)(2,1)S(1)}, u32[]{:S(2)}) copy-start(bf16[512,512]{1,0:T(8,128)(2,1)S(1)} %collective-permute-done.28.refs_22_) | copy-start | bytes 1572868 | tf_op jit(solution)/shard_map/cond
  329.8 64.2 %collective-permute-start.8 = (bf16[512,512]{1,0:T(8,128)(2,1)}, bf16[512,512]{1,0:T(8,128)(2,1)S(1)}, u32[]{:S(2)}, u32[]{:S(2)}) collective-permute-start(bf16[512,512]{1,0:T(8,128)(2,1)} %get-tuple-element.43.refs_0_), channel_id=1, source_target_pairs={{0,16},{8,24},{16,0},{24,8},{1,17},{9,25},{17,1},{25,9},{2,18},{10... | collective-permute-start | bytes 1572872 | tf_op jit(solution)/shard_map/cond/branch_1_fun/ppermute | solution.py:432
  335.4 58.5 %copy-start.5 = (bf16[512,512]{1,0:T(8,128)(2,1)}, bf16[512,512]{1,0:T(8,128)(2,1)S(1)}, u32[]{:S(2)}) copy-start(bf16[512,512]{1,0:T(8,128)(2,1)S(1)} %collective-permute-done.6.refs_2_) | copy-start | bytes 1572868 | tf_op jit(solution)/shard_map/cond
  335.4 58.6 %collective-permute-start.10 = (bf16[512,512]{1,0:T(8,128)(2,1)S(1)}, bf16[512,512]{1,0:T(8,128)(2,1)S(1)}, u32[]{:S(2)}, u32[]{:S(2)}) collective-permute-start(bf16[512,512]{1,0:T(8,128)(2,1)S(1)} %collective-permute-done.6.refs_2_), channel_id=1, source_target_pairs={{0,16},{8,24},{16,0},{24,8},{1,17},{9,25},{17,1},{25,9},{2,18},{10... | collective-permute-start | bytes 1572872 | tf_op jit(solution)/shard_map/cond/branch_1_fun/ppermute | solution.py:432
  341.0 52.9 %copy-start.6 = (bf16[512,512]{1,0:T(8,128)(2,1)}, bf16[512,512]{1,0:T(8,128)(2,1)S(1)}, u32[]{:S(2)}) copy-start(bf16[512,512]{1,0:T(8,128)(2,1)S(1)} %collective-permute-done.9.refs_5_) | copy-start | bytes 1572868 | tf_op jit(solution)/shard_map/cond
  341.0 53.0 %collective-permute-start.11 = (bf16[512,512]{1,0:T(8,128)(2,1)S(1)}, bf16[512,512]{1,0:T(8,128)(2,1)S(1)}, u32[]{:S(2)}, u32[]{:S(2)}) collective-permute-start(bf16[512,512]{1,0:T(8,128)(2,1)S(1)} %collective-permute-done.9.refs_5_), channel_id=1, source_target_pairs={{0,8},{8,0},{16,24},{24,16},{1,9},{9,1},{17,25},{25,17},{2,10},{10... | collective-permute-start | bytes 1572872 | tf_op jit(solution)/shard_map/cond/branch_1_fun/ppermute | solution.py:432
  346.6 0.8 copy-start.27
  347.4 47.9 %copy-start.12 = (s32[64,64]{1,0:T(8,128)S(1)}, s32[64,64]{1,0:T(8,128)}, u32[]{:S(2)}) copy-start(s32[64,64]{1,0:T(8,128)} %get-tuple-element.54.refs_14_) | copy-start | bytes 49156 | tf_op jit(solution)/shard_map/cond
  347.4 47.9 %copy-start.13 = (s32[64,64]{1,0:T(8,128)S(1)}, s32[64,64]{1,0:T(8,128)}, u32[]{:S(2)}) copy-start(s32[64,64]{1,0:T(8,128)} %get-tuple-element.55.refs_15_) | copy-start | bytes 49156 | tf_op jit(solution)/shard_map/cond
  347.4 47.9 %copy-start.15 = (s32[2]{0:T(128)S(1)}, s32[2]{0:T(128)}, u32[]{:S(2)}) copy-start(s32[2]{0:T(128)} %copy-done.14) | copy-start | bytes 28 | tf_op jit(solution)/shard_map/cond
  393.9 0.8 copy-start.7
  393.9 1.0 copy-start.8
  393.9 1.1 copy-start.9
  394.0 1.3 copy-start.10
Sparse Core Ops, SparseCore 0:
  27.2 76.1 all-gather.13
  105.1 59.0 all-gather.15
  165.8 54.7 all-gather.17
  222.0 45.9 all-gather.19

commit v2 on v0

--- a/solution.py
+++ b/solution.py
@@ -1,9 +1,23 @@
+import functools
+import math
+
 import jax
 import jax.numpy as jnp
+import numpy as np
 from jax import lax
+from jax.experimental import pallas as pl
+from jax.experimental.pallas import tpu as pltpu
 from jax.sharding import PartitionSpec as P
 
 TILE = 128
+ROW_GROUP = 4
+WIDTHS = (4, 4, 4, 4)
+SIGMAS = ((3.2, 2.1), (4.2, 3.9))
+DEPTH = 1024
+VMEM_BYTES = 60 * 2**20
+SMEM = pl.BlockSpec(memory_space=pltpu.SMEM)
+VMEM = pl.BlockSpec(memory_space=pltpu.VMEM)
+ANY = pl.BlockSpec(memory_space=pl.ANY)
 
 
 def tile_mask(pattern, row_start, col_start, nrows, ncols):
@@ -17,7 +31,7 @@
     return lax.dynamic_slice(spread, (row_start % TILE, col_start % TILE), (nrows, ncols))
 
 
-def local(density, pattern_p, pattern_square, pattern_cube):
+def dense_step(density, pattern_p, pattern_square, pattern_cube):
     nrows, ncols = density.shape
     row_start = lax.axis_index("col") * nrows
     col_start = lax.axis_index("row") * ncols
@@ -34,6 +48,548 @@
     return 3.0 * keep_square * square - 2.0 * keep_cube * cube
 
 
+def chunk_bounds(tile_rows, widths, part_sigmas, sigmas):
+    bounds, cols = [], 0
+    for width in widths:
+        cols += width
+        tiles = tile_rows * cols
+        more = (sigmas if cols == sum(widths) else part_sigmas) * math.sqrt(tiles)
+        bounds.append(min(tiles, 2 * math.ceil((tiles + more) / 4)))
+    return [min(b, bounds[-1]) for b in bounds]
+
+
+def slot_table(pattern, tile_rows, tile_cols):
+    n = pattern.shape[0]
+    at = np.arange(n)
+    same_rows = at[:, None] // tile_rows == at[None, :] // tile_rows
+    above = (same_rows & (at[None, :] < at[:, None])).astype(np.float32)
+    same_cols = at[:, None] // tile_cols == at[None, :] // tile_cols
+    left = (same_cols & (at[:, None] < at[None, :])).astype(np.float32)
+    kept = pattern.astype(jnp.bfloat16)
+    dot = functools.partial(jnp.dot, preferred_element_type=jnp.float32)
+    in_column = dot(jnp.asarray(above, jnp.bfloat16), kept)
+    column = dot(jnp.asarray(same_rows, jnp.bfloat16), kept).astype(jnp.bfloat16)
+    before = dot(column, jnp.asarray(left, jnp.bfloat16))
+    return jnp.where(pattern != 0, (in_column + before).astype(jnp.int32), -1)
+
+
+def column_lists(table, place, tile_rows, tile_cols):
+    n = table.shape[0]
+    blocks = n // tile_rows
+    tiles = tile_rows * tile_cols
+    mine = lax.dynamic_slice(table, (0, place[1] * tile_cols), (n, tile_cols)).reshape(blocks, tile_rows, tile_cols)
+    order = mine.transpose(0, 2, 1).reshape(blocks, tiles, 1)
+    which = lax.broadcasted_iota(jnp.int32, (blocks, tiles, tiles), 1)
+    slot = lax.broadcasted_iota(jnp.int32, (blocks, tiles, tiles), 2)
+    lists = jnp.sum(jnp.where(order == slot, which, 0), 1)
+    column = lax.broadcasted_iota(jnp.int32, (blocks, tiles, tile_cols + 1), 1) // tile_rows
+    limit = lax.broadcasted_iota(jnp.int32, (blocks, tiles, tile_cols + 1), 2)
+    counts = jnp.sum(jnp.where((order >= 0) & (column < limit), 1, 0), 1)
+    return lists, counts
+
+
+def tile_at(ref, i, j):
+    return ref.at[pl.ds(pl.multiple_of(i * TILE, TILE), TILE), pl.ds(pl.multiple_of(j * TILE, TILE), TILE)]
+
+
+def send_kept(table_ref, place_ref, x_ref, outs, sems, spans, shape):
+    tile_rows, tile_cols = shape
+    c, r = place_ref[0], place_ref[1]
+
+    def send(i, j, slot):
+        for q, (lo, hi) in enumerate(spans):
+            @pl.when((slot >= lo) & (slot < hi))
+            def _():
+                pltpu.make_async_copy(tile_at(x_ref, i, j), outs[q].at[slot - lo], sems.at[q]).start()
+
+    def step(n, used):
+        j, i = n // tile_rows, n % tile_rows
+        slot = table_ref[c * tile_rows + i, r * tile_cols + j]
+        send(i, j, slot)
+        return used + (slot >= 0).astype(jnp.int32)
+
+    used = lax.fori_loop(0, tile_rows * tile_cols, step, jnp.int32(0))
+    top = max(hi for _, hi in spans)
+
+    def fill(slot, z):
+        send(0, 0, slot)
+        return z
+
+    lax.fori_loop(used, jnp.int32(top), fill, 0)
+    for q, out in enumerate(outs):
+        pltpu.make_async_copy(out, out, sems.at[q]).wait()
+
+
+def pack(table, place, density, spans):
+    shape = density.shape[0] // TILE, density.shape[1] // TILE
+
+    def kernel(table_ref, place_ref, x_ref, *refs):
+        send_kept(table_ref, place_ref, x_ref, refs[:-1], refs[-1], spans, shape)
+
+    return pl.pallas_call(
+        kernel,
+        out_shape=[jax.ShapeDtypeStruct((hi - lo, TILE, TILE), density.dtype) for lo, hi in spans],
+        in_specs=[SMEM, SMEM, VMEM],
+        out_specs=[ANY] * len(spans),
+        scratch_shapes=[pltpu.SemaphoreType.DMA((len(spans),))],
+        name="pack",
+    )(table, place, density)
+
+
+def stage(halves, lo, hi, after):
+    cut = halves[0].shape[0]
+    parts = []
+    if lo < cut:
+        parts.append((0, lo, min(hi, cut)))
+    if hi > cut:
+        parts.append((1, max(lo, cut) - cut, hi - cut))
+
+    def kernel(h0, h1, *refs):
+        out, sem = refs[-2:]
+        at, copies = 0, []
+        for which, first, end in parts:
+            src = (h0, h1)[which].at[pl.ds(first, end - first)]
+            copies.append(pltpu.make_async_copy(src, out.at[pl.ds(at, end - first)], sem.at[which]))
+            at += end - first
+        for copy in copies:
+            copy.start()
+        for copy in copies:
+            copy.wait()
+
+    return pl.pallas_call(
+        kernel,
+        out_shape=jax.ShapeDtypeStruct((hi - lo, TILE, TILE), halves[0].dtype),
+        in_specs=[ANY] * (2 + len(after)),
+        out_specs=VMEM,
+        scratch_shapes=[pltpu.SemaphoreType.DMA((2,))],
+        name="stage",
+    )(*halves, *after)
+
+
+def split(x, y, after):
+    nrows, ncols = x.shape
+    half = jax.ShapeDtypeStruct((nrows // 2, ncols), x.dtype)
+
+    def kernel(x_ref, y_ref, *refs):
+        top, bottom, sem = refs[-3:]
+        copies = [
+            pltpu.make_async_copy(x_ref.at[pl.ds(0, nrows // 2)], top, sem.at[0]),
+            pltpu.make_async_copy(y_ref.at[pl.ds(nrows // 2, nrows // 2)], bottom, sem.at[1]),
+        ]
+        for copy in copies:
+            copy.start()
+        for copy in copies:
+            copy.wait()
+
+    return pl.pallas_call(
+        kernel,
+        out_shape=[half, half],
+        in_specs=[ANY] * (2 + len(after)),
+        out_specs=[VMEM, VMEM],
+        scratch_shapes=[pltpu.SemaphoreType.DMA((2,))],
+        name="split",
+    )(x, y, *after)
+
+
+def row_unpack(table, place, density, pieces, ks, after=()):
+    nrows, ncols = density.shape
+    tile_rows, tile_cols = nrows // TILE, ncols // TILE
+    flat = [x for piece in pieces if piece is not None for x in piece]
+    sizes = [x.shape[0] for x in flat[:2]]
+
+    def kernel(table_ref, place_ref, x_ref, *refs):
+        ins, (out, held, sems) = refs[: len(flat)], refs[-3:]
+        i = pl.program_id(0)
+        c, r = place_ref[0], place_ref[1]
+
+        @pl.when(i == 0)
+        def _():
+            copies = []
+            for n, ref in enumerate(ins):
+                which = n % 2
+                target = held.at[n // 2, pl.ds(which * sizes[0], sizes[which])]
+                copies.append(pltpu.make_async_copy(ref, target, sems.at[n]))
+            for copy in copies:
+                copy.start()
+            for copy in copies:
+                copy.wait()
+
+        at = 0
+        for n, (k, piece) in enumerate(zip(ks, pieces)):
+            for j in range(tile_cols):
+                slot = table_ref[c * tile_rows + i, (r ^ k) * tile_cols + j]
+                if piece is None:
+                    tile = x_ref[:, j * TILE : (j + 1) * TILE]
+                else:
+                    tile = held[at, jnp.maximum(slot, 0)]
+                d = n * tile_cols + j
+                out[:, d * TILE : (d + 1) * TILE] = jnp.where(slot >= 0, tile, jnp.zeros_like(tile))
+            at += piece is not None
+
+    return pl.pallas_call(
+        kernel,
+        grid=(tile_rows,),
+        out_shape=jax.ShapeDtypeStruct((nrows, len(ks) * ncols), jnp.bfloat16),
+        in_specs=[SMEM, SMEM, pl.BlockSpec((TILE, ncols), lambda i: (i, 0))] + [ANY] * (len(flat) + len(after)),
+        out_specs=pl.BlockSpec((TILE, len(ks) * ncols), lambda i: (i, 0)),
+        scratch_shapes=[
+            pltpu.VMEM((len(flat) // 2, sum(sizes), TILE, TILE), jnp.bfloat16),
+            pltpu.SemaphoreType.DMA((len(flat),)),
+        ],
+        compiler_params=pltpu.CompilerParams(vmem_limit_bytes=VMEM_BYTES),
+        cost_estimate=pl.CostEstimate(flops=0, bytes_accessed=8 * len(ks) * nrows * ncols, transcendentals=0),
+        name="row_unpack",
+    )(table, place, density, *flat, *after)
+
+
+def square_group(lists, counts, place, row_parts, chunks, spans, first, width, shape, ks, partial=None, after=()):
+    tile_rows, tile_cols = shape
+    nrows = row_parts[0].shape[0]
+    span = tile_cols * TILE
+    count = len(ks)
+    depth = count * span
+    n = width * TILE
+    bits = (tile_cols * width).bit_length()
+    step_rows = nrows // 2
+
+    def kernel(lists_ref, counts_ref, place_ref, *refs):
+        a_refs, refs = refs[: len(row_parts)], refs[len(row_parts) :]
+        ins, refs = refs[: len(chunks)], refs[len(chunks) :]
+        if partial is not None:
+            partial_ref, refs = refs[0], refs[1:]
+        panel_out, square, low, a, panel, kept, a_sems, sems, out_sem, partial_sem = refs[len(after) :]
+        r = place_ref[1]
+        owners = tile_cols // tile_rows
+
+        part = at = 0
+        for k in range(count):
+            source = a_refs[part].at[:, pl.ds(at, span)]
+            pltpu.make_async_copy(source, a.at[k], a_sems.at[k]).start()
+            at += span
+            if at == row_parts[part].shape[1]:
+                part, at = part + 1, 0
+        if partial is not None:
+            before = pltpu.make_async_copy(partial_ref, square, partial_sem)
+            before.start()
+
+        def fetch(k, z):
+            rows = pl.ds(pl.multiple_of(k * span, span), span)
+            panel[:, rows] = jnp.zeros((width, span, TILE), panel.dtype)
+            total = jnp.int32(0)
+            for o in range(owners):
+                owner = (r ^ (k + ks[0])) * owners + o
+                begin, end = counts_ref[owner, first], counts_ref[owner, first + width]
+                total += end - begin
+                top = k * span + o * tile_rows * TILE
+                for q, (lo, hi) in enumerate(spans[: len(chunks)]):
+                    shift = owner * (hi - lo) - lo
+
+                    def one(slot, z):
+                        tile = lists_ref[owner, slot]
+                        j, i = tile // tile_rows - first, tile % tile_rows
+                        here = pl.ds(pl.multiple_of(top + i * TILE, TILE), TILE)
+                        pltpu.make_async_copy(ins[q].at[shift + slot], panel.at[j, here], sems.at[k]).start()
+                        return z
+
+                    lax.fori_loop(jnp.maximum(begin, lo), jnp.minimum(end, hi), one, 0)
+            kept[k] = total
+            return z
+
+        lax.fori_loop(0, count, fetch, 0)
+
+        def out_copy(k):
+            rows = pl.ds(pl.multiple_of(k * span, span), span)
+            return pltpu.make_async_copy(panel.at[:, rows], panel_out.at[:, rows], out_sem)
+
+        def multiply(k, z):
+            for bit in range(bits):
+                some = ins[0].at[pl.ds(0, 1 << bit)]
+
+                @pl.when((kept[k] >> bit) & 1 == 1)
+                def _():
+                    pltpu.make_async_copy(some, some, sems.at[k]).wait()
+
+            pltpu.make_async_copy(a.at[k], a.at[k], a_sems.at[k]).wait()
+            out_copy(k).start()
+            rows = pl.ds(pl.multiple_of(k * span, span), span)
+
+            def step(m, z):
+                here = pl.ds(pl.multiple_of(m * step_rows, step_rows), step_rows)
+                right = jnp.concatenate([panel[j, rows] for j in range(width)], 1)
+                square[here] += jnp.dot(a[k, here], right, preferred_element_type=jnp.float32)
+                return z
+
+            return lax.fori_loop(0, nrows // step_rows, step, z)
+
+        if partial is not None:
+            before.wait()
+        else:
+            square[...] = jnp.zeros_like(square)
+        lax.fori_loop(0, count, multiply, 0)
+        low[...] = square[...].astype(jnp.bfloat16)
+        for k in range(count):
+            out_copy(k).wait()
+
+    operands = [*row_parts, *chunks, *([] if partial is None else [partial]), *after]
+    return pl.pallas_call(
+        kernel,
+        out_shape=[
+            jax.ShapeDtypeStruct((width, depth, TILE), jnp.bfloat16),
+            jax.ShapeDtypeStruct((nrows, n), jnp.float32),
+            jax.ShapeDtypeStruct((nrows, n), jnp.bfloat16),
+        ],
+        in_specs=[SMEM] * 3 + [ANY] * len(operands),
+        out_specs=[ANY, VMEM, VMEM],
+        scratch_shapes=[
+            pltpu.VMEM((count, nrows, span), jnp.bfloat16),
+            pltpu.VMEM((width, depth, TILE), jnp.bfloat16),
+            pltpu.SMEM((count,), jnp.int32),
+            pltpu.SemaphoreType.DMA((count,)),
+            pltpu.SemaphoreType.DMA((count,)),
+            pltpu.SemaphoreType.DMA,
+            pltpu.SemaphoreType.DMA,
+        ],
+        compiler_params=pltpu.CompilerParams(vmem_limit_bytes=VMEM_BYTES),
+        cost_estimate=pl.CostEstimate(
+            flops=2 * nrows * depth * n, bytes_accessed=2 * depth * (nrows + 2 * n) + 6 * nrows * n, transcendentals=0
+        ),
+        name="square_group",
+    )(lists, counts, place, *operands)
+
+
+def cube_part(strips, panels, jobs, widths, before, finish=None, after=()):
+    groups = sorted({g for job in jobs.values() for g in job})
+    firsts = [sum(widths[:h]) for h in range(len(widths))]
+    span = sum(widths) * TILE
+    nrows = strips[groups[0]][0][0][0].shape[0]
+    lefts, start = [], {}
+    at = 0
+    for g in groups:
+        start[g] = at
+        for pieces in strips[g]:
+            lefts += [(x, row, at) for x, row in pieces]
+            at += widths[g] * TILE
+    total = at
+    hs = list(jobs)
+    deepest = max(ROW_GROUP * TILE * sum(widths[g] for g in job) for job in jobs.values())
+    widest = max(widths[h] for h in hs)
+    panel_arrays = [x for h in hs for x, _ in panels[h]]
+    operands = [x for x, *_ in lefts] + panel_arrays + [before[h] for h in hs if h in before]
+    with_before = [h for h in hs if h in before]
+    specs = [ANY] * len(operands)
+    if finish is not None:
+        place, pattern_square, pattern_cube, squares = finish
+        operands += [place, pattern_square, pattern_cube, *squares]
+        specs += [SMEM] * 3 + [ANY] * len(squares)
+        out_shape = [jax.ShapeDtypeStruct((nrows, span), jnp.float32)]
+    else:
+        out_shape = [jax.ShapeDtypeStruct((nrows, widths[h] * TILE), jnp.float32) for h in hs]
+    operands += after
+    specs += [ANY] * len(after)
+    step_rows = nrows // 2
+
+    def kernel(*refs):
+        refs = list(refs)
+
+        def take(count):
+            taken = refs[:count]
+            del refs[:count]
+            return taken
+
+        left_refs = take(len(lefts))
+        panel_refs = {h: take(ROW_GROUP) for h in hs}
+        before_refs = dict(zip(with_before, take(len(with_before))))
+        if finish is not None:
+            place_ref, keep_square, keep_cube = take(3)
+            square_refs = take(len(hs))
+        take(len(after))
+        outs = take(len(out_shape))
+        left, right, acc, held, left_sems, right_sems, acc_sems, held_sems, out_sems = refs
+
+        def loads(n):
+            h, s, t = hs[n], n % 2, n % 3
+            lanes = pl.ds(0, widths[h] * TILE)
+            copies, at = [], 0
+            for g in jobs[h]:
+                rows = widths[g] * TILE
+                for k, (ref, (_, shift)) in enumerate(zip(panel_refs[h], panels[h])):
+                    source = ref.at[:, pl.ds(shift + firsts[g] * TILE, rows)]
+                    target = right.at[s, pl.ds(0, widths[h]), pl.ds(at, rows)]
+                    copies.append(pltpu.make_async_copy(source, target, right_sems.at[s]))
+                    at += rows
+            if h in before_refs:
+                copies.append(pltpu.make_async_copy(before_refs[h], acc.at[t, :, lanes], acc_sems.at[t]))
+            if finish is not None:
+                copies.append(pltpu.make_async_copy(square_refs[n], held.at[t, :, lanes], held_sems.at[t]))
+            return copies
+
+        def store(n):
+            h, t = hs[n], n % 3
+            lanes = pl.ds(0, widths[h] * TILE)
+            if finish is None:
+                return pltpu.make_async_copy(acc.at[t, :, lanes], outs[n], out_sems.at[t])
+            target = outs[0].at[:, pl.ds(firsts[h] * TILE, widths[h] * TILE)]
+            return pltpu.make_async_copy(held.at[t, :, lanes], target, out_sems.at[t])
+
+        left_copies = [
+            pltpu.make_async_copy(ref, left.at[pl.ds(row, x.shape[0]), pl.ds(col, x.shape[1])], left_sems.at[0])
+            for ref, (x, row, col) in zip(left_refs, lefts)
+        ]
+        for copy in left_copies + loads(0):
+            copy.start()
+        for copy in left_copies:
+            copy.wait()
+        for n, h in enumerate(hs):
+            s, t, wide = n % 2, n % 3, widths[h] * TILE
+            if n >= 2:
+                store(n - 2).wait()
+            if n + 1 < len(hs):
+                for copy in loads(n + 1):
+                    copy.start()
+            for copy in loads(n):
+                copy.wait()
+            if h not in before_refs:
+                acc[t, :, :wide] = jnp.zeros((nrows, wide), jnp.float32)
+            shift = start[jobs[h][0]]
+            blocks = ROW_GROUP * TILE * sum(widths[g] for g in jobs[h]) // DEPTH
+
+            def step(b, z):
+                here = pl.ds(pl.multiple_of(b * DEPTH, DEPTH), DEPTH)
+                there = pl.ds(pl.multiple_of(shift + b * DEPTH, DEPTH), DEPTH)
+
+                def rows_step(m, z):
+                    rows = pl.ds(pl.multiple_of(m * step_rows, step_rows), step_rows)
+                    other = jnp.concatenate([right[s, j, here] for j in range(widths[h])], 1)
+                    part = jnp.dot(left[rows, there], other, preferred_element_type=jnp.float32)
+                    acc[t, rows, :wide] += part
+                    return z
+
+                return lax.fori_loop(0, nrows // step_rows, rows_step, z)
+
+            lax.fori_loop(0, blocks, step, 0)
+            if finish is not None:
+                tile_rows, tile_cols = nrows // TILE, span // TILE
+                row, col = place_ref[0] * tile_rows, place_ref[1] * tile_cols + firsts[h]
+
+                def combine(i, z):
+                    rows = pl.ds(pl.multiple_of(i * TILE, TILE), TILE)
+                    for j in range(widths[h]):
+                        lanes = slice(j * TILE, (j + 1) * TILE)
+                        a = 3.0 * keep_square[row + i, col + j].astype(jnp.float32)
+                        b = 2.0 * keep_cube[row + i, col + j].astype(jnp.float32)
+                        held[t, rows, lanes] = a * held[t, rows, lanes] - b * acc[t, rows, lanes]
+                    return z
+
+                lax.fori_loop(0, tile_rows, combine, 0)
+            store(n).start()
+        for n in range(max(len(hs) - 2, 0), len(hs)):
+            store(n).wait()
+
+    flops = sum(2 * nrows * ROW_GROUP * TILE * widths[g] * widths[h] * TILE for h in hs for g in jobs[h])
+    return pl.pallas_call(
+        kernel,
+        out_shape=out_shape,
+        in_specs=specs,
+        out_specs=[ANY] * len(out_shape),
+        scratch_shapes=[
+            pltpu.VMEM((nrows, total), jnp.bfloat16),
+            pltpu.VMEM((2, widest, deepest, TILE), jnp.bfloat16),
+            pltpu.VMEM((3, nrows, widest * TILE), jnp.float32),
+            pltpu.VMEM((3, nrows, widest * TILE) if finish is not None else (3, 8, TILE), jnp.float32),
+            pltpu.SemaphoreType.DMA((1,)),
+            pltpu.SemaphoreType.DMA((2,)),
+            pltpu.SemaphoreType.DMA((3,)),
+            pltpu.SemaphoreType.DMA((3,)),
+            pltpu.SemaphoreType.DMA((3,)),
+        ],
+        compiler_params=pltpu.CompilerParams(vmem_limit_bytes=VMEM_BYTES),
+        cost_estimate=pl.CostEstimate(flops=flops, bytes_accessed=8 * nrows * span, transcendentals=0),
+        name="cube_part",
+    )(*operands)
+
+
+def packed_step(density, table, place, pattern_square, pattern_cube, spans):
+    nrows, ncols = density.shape
+    shape = nrows // TILE, ncols // TILE
+    widths = WIDTHS
+    cap = spans[-1][1]
+    *halves, first_chunk = pack(table, place, density, [(0, cap // 2), (cap // 2, cap), spans[0]])
+
+    def swap(x, k):
+        return lax.ppermute(x, "row", [(i, i ^ k) for i in range(ROW_GROUP)])
+
+    def gather(x):
+        return lax.all_gather(x, "col", axis=0, tiled=True)
+
+    chunks = [gather(first_chunk)]
+    by_x, by_y = [swap(x, 1) for x in halves], [swap(x, 2) for x in halves]
+    chunks.append(gather(stage(halves, *spans[1], by_x + by_y)))
+    far = [swap(by_x[0], 2), swap(by_y[1], 1)]
+    near_part = row_unpack(table, place, density, [None, by_x, by_y], [0, 1, 2])
+
+    lists, counts = column_lists(table, place, *shape)
+    group = functools.partial(square_group, lists, counts, place)
+    panels, squares, strips = [], [], []
+
+    def send(square, low):
+        squares.append(square)
+        strips.append([[(low, 0)], [(swap(low, 1), 0)], [(swap(low, 2), 0)]])
+
+    def forward(h, after=()):
+        (x, _), (y, _) = strips[h][1][0], strips[h][2][0]
+        top, bottom = split(x, y, after)
+        strips[h].append([(swap(top, 2), 0), (swap(bottom, 1), nrows // 2)])
+        return top
+
+    near_panel, partial, _ = group([near_part], chunks[:1], spans, 0, widths[0], shape, [0, 1, 2])
+    far_part = row_unpack(table, place, density, [far], [3], [partial])
+    chunks.append(gather(stage(halves, *spans[2], [far_part])))
+    far_panel, square, low = group([far_part], chunks[:1], spans, 0, widths[0], shape, [3], partial)
+    panels.append([(near_panel, k * ncols) for k in range(3)] + [(far_panel, 0)])
+    send(square, low)
+
+    def next_group(h, after):
+        parts = [near_part, far_part]
+        panel, square, low = group(
+            parts, chunks[: h + 1], spans, sum(widths[:h]), widths[h], shape, [0, 1, 2, 3], None, after
+        )
+        panels.append([(panel, k * ncols) for k in range(ROW_GROUP)])
+        send(square, low)
+
+    next_group(1, [])
+    forward(0)
+    chunks.append(gather(stage(halves, *spans[3], [low])))
+    next_group(2, [forward(1)])
+    cubes = dict(enumerate(cube_part(strips, panels, {0: [0, 1], 1: [0, 1]}, widths, {}, after=[squares[2]])))
+    next_group(3, [forward(2), cubes[0]])
+    jobs = {0: [2], 1: [2], 2: [0, 1, 2], 3: [0, 1, 2]}
+    cubes = dict(enumerate(cube_part(strips, panels, jobs, widths, cubes)))
+    forward(3, [cubes[0]])
+    finish = place, pattern_square, pattern_cube, squares
+    return cube_part(strips, panels, {h: [3] for h in range(4)}, widths, cubes, finish)[0]
+
+
+def local(density, pattern_p, pattern_square, pattern_cube):
+    tile_rows, tile_cols = density.shape[0] // TILE, density.shape[1] // TILE
+    if lax.axis_size("row") != ROW_GROUP or tile_cols != sum(WIDTHS):
+        return dense_step(density, pattern_p, pattern_square, pattern_cube)
+    widths = WIDTHS
+    table = slot_table(pattern_p, tile_rows, tile_cols)
+    place = jnp.stack([lax.axis_index("col"), lax.axis_index("row")]).astype(jnp.int32)
+    level, ways = len(SIGMAS), []
+    for n, sigmas in reversed(list(enumerate(SIGMAS))):
+        bounds = chunk_bounds(tile_rows, widths, *sigmas)
+        limit = np.tile(np.repeat(bounds, widths), table.shape[1] // tile_cols)
+        fits = jnp.all(table < jnp.asarray(limit, jnp.int32)[None, :])
+        level = jnp.where(fits, n, level)
+        spans = list(zip([0, *bounds[:-1]], bounds))
+        ways.insert(0, functools.partial(
+            packed_step, density, table, place, pattern_square, pattern_cube, spans
+        ))
+    ways.append(lambda: dense_step(density, pattern_p, pattern_square, pattern_cube))
+    return lax.switch(level, ways)
+
+
 def solution(mesh):
     placed = (P("col", "row"), P(), P(), P())
     return jax.shard_map(

time: 724 us -> 366 us (0.51)
  waiting for transfers between devices: 575 us -> 116 us
  Pallas kernels: 0 us -> 192 us
  matrix products: 91.3 us -> 2.63 us
  local copies, waits for them, and re-layouts: 39.6 us -> 9.11 us
  starting transfers between devices: 0.08 us -> 25.2 us
    all_gather x3 -> x4, waiting for transfers between devices: 574 us -> 15.4 us  [gather(): return lax.all_gather(x, 'col', axis=0, tiled=True)]
    pallas_call x0 -> x18, Pallas kernels: none -> 192 us  [the longest x5 80.2 us: square_group(): pl.pallas_call(kernel, out_shape=[jax.ShapeDtypeStruct((width, depth, TIL...]
    ppermute x0 -> x22, waiting for transfers between devices: none -> 101 us  [swap(): return lax.ppermute(x, 'row', [(i, i ^ k) for i in range(ROW_GROUP)])]
    dot_general x2, matrix products: 91.3 us -> 2.63 us  [the longest x1 1.74 us: slot_table(): before = dot(column, jnp.asarray(left, jnp.bfloat16))]
    unnamed x14 -> x0, local copies, waits for them, and re-layouts: 26 us -> none
    ppermute x0 -> x22, starting transfers between devices: none -> 25 us  [swap(): return lax.ppermute(x, 'row', [(i, i ^ k) for i in range(ROW_GROUP)])]
    dynamic_slice x7 -> x0, local copies, waits for them, and re-layouts: 10.9 us -> none  [the longest x2 9.68 us: tile_mask(): lax.dynamic_slice(spread, (row_start % TILE, col_start % TILE), (nrows, n...]
    cond x0 -> x38, local copies, waits for them, and re-layouts: none -> 8.18 us
  transfers between devices with their start and end apart: 3 -> 26, of which waited for: 3 -> 15; matrix products, arithmetic and copies ran while one was open for 4% -> 1% of each run, Pallas kernels for 0% -> 44%
where the time goes in v2:
time: 366 us; the launch traced here: 368 us
  Pallas kernels  192 us (52%)
  waiting for transfers between devices  116 us (32%)
  starting transfers between devices  25.2 us (7%)
  between operations  14.6 us (4%)
  local copies, waits for them, and re-layouts  9.11 us (2%)
  loops' own time  6.59 us (2%)
    ppermute x22, waiting for transfers between devices, swap(): return lax.ppermute(x, 'row', [(i, i ^ k) for i in range(ROW_GROUP)])  101 us
    pallas_call x5, Pallas kernels, square_group(): pl.pallas_call(kernel, out_shape=[jax.ShapeDtypeStruct((width, depth, TIL...  80.2 us
    pallas_call x3, Pallas kernels, cube_part(): pl.pallas_call(kernel, out_shape=out_shape, in_specs=specs, out_specs=[AN...  69.3 us
    ppermute x22, starting transfers between devices, swap(): return lax.ppermute(x, 'row', [(i, i ^ k) for i in range(ROW_GROUP)])  25 us
    pallas_call x2, Pallas kernels, row_unpack(): pl.pallas_call(kernel, grid=(tile_rows,), out_shape=jax.ShapeDtypeStruct(...  21.6 us
    all_gather x4, waiting for transfers between devices, gather(): return lax.all_gather(x, 'col', axis=0, tiled=True)  15.4 us
    pallas_call x4, Pallas kernels, split(): pl.pallas_call(kernel, out_shape=[half, half], in_specs=[ANY] * (2 + len(...  8.88 us
    cond x38, local copies, waits for them, and re-layouts  8.18 us
  transfers between devices with their start and end apart: 26, of which 15 were waited for; matrix products, arithmetic and copies ran while one was open for 1% of the time, Pallas kernels for 44%

profile of v2, /device:TPU:0, one launch (start us, length us, event | category | flops | bytes accessed | tf_op | source)
XLA Modules:
  0.0 367.6 jit_solution(14075143296547306709)
XLA Ops:
  6.6 0.9 fusion.7
  7.5 1.7 compare_reduce_fusion
  10.4 350.4 %conditional.1 = (f32[1024,2048]{1,0:T(8,128)}) conditional(s32[]{:T(128)} %clamp.3, (s32[]{:T(128)}, s32[64,64]{1,0:T(8,128)S(1)}, s32[2]{0:T(128)S(1)}, bf16[1024,2048]{1,0:T(8,128)(2,1)}, s32[64,64]{1,0:T(8,128)}, /*index=5*/s32[64,64]{1,0:T(8,128)}) %tuple.14, (s32[]{:T(128)}, s32[64,64]{1,0:T(8,128)S(1)}, s32[2]{0:T(128)S(1)}, ...), branch_computations={%region_2.5_spmd, %region_5.8_spmd, %region_8.9_spmd} | conditional | flops 68740448256 | bytes 515693568 | solution.py:590
  10.7 6.0 %pack.3 = (bf16[44,128,128]{2,1,0:T(8,128)(2,1)}, bf16[44,128,128]{2,1,0:T(8,128)(2,1)}, bf16[28,128,128]{2,1,0:T(8,128)(2,1)}) custom-call(s32[64,64]{1,0:T(8,128)S(1)} %get-tuple-element.78.table_ref, s32[2]{0:T(128)S(1)} %get-tuple-element.80.place_ref.refs_25_, bf16[1024,2048]{1,0:T(8,128)(2,1)} %get-tuple-element.81.x_ref), custom_call_target="tpu_custom_call" | custom-call | tf_op jit(solution)/shard_map/cond/branch_1_fun/pack/pallas_call | solution.py:129
  16.8 2.9 collective-permute-start.22
  19.7 1.5 collective-permute-start.25
  21.2 0.7 collective-permute-start.23
  21.9 30.4 %collective-permute-done.22.refs_0_ = bf16[44,128,128]{2,1,0:T(8,128)(2,1)S(1)} collective-permute-done((bf16[44,128,128]{2,1,0:T(8,128)(2,1)}, bf16[44,128,128]{2,1,0:T(8,128)(2,1)S(1)}, u32[]{:S(2)}, u32[]{:S(2)}) %collective-permute-start.22) | collective-permute-done | bytes 1441824 | tf_op jit(solution)/shard_map/cond/branch_1_fun/ppermute | solution.py:519
  52.3 2.1 collective-permute-done.25.refs_3_
  54.4 28.2 %collective-permute-done.23.refs_1_ = bf16[44,128,128]{2,1,0:T(8,128)(2,1)} collective-permute-done((bf16[44,128,128]{2,1,0:T(8,128)(2,1)}, bf16[44,128,128]{2,1,0:T(8,128)(2,1)}, u32[]{:S(2)}, u32[]{:S(2)}) %collective-permute-start.23) | collective-permute-done | bytes 1441824 | tf_op jit(solution)/shard_map/cond/branch_1_fun/ppermute | solution.py:519
  82.6 1.5 collective-permute-done.24.refs_2_
  84.0 2.0 stage.9
  86.1 1.4 collective-permute-start.26
  87.5 0.6 collective-permute-start.27
  88.8 0.7 copy.46.counts_ref
  89.5 0.8 select_reduce_fusion.2.lists_ref
  90.3 12.6 %row_unpack.6.refs_0_ = bf16[1024,6144]{1,0:T(8,128)(2,1)} custom-call(s32[64,64]{1,0:T(8,128)S(1)} %get-tuple-element.78.table_ref, s32[2]{0:T(128)S(1)} %get-tuple-element.80.place_ref.refs_25_, bf16[1024,2048]{1,0:T(8,128)(2,1)} %get-tuple-element.81.x_ref, bf16[44,128,128]{2,1,0:T(8,128)(2,1)} %copy-done.6, ...), custom_call_target="tpu_custom_call" | custom-call | bytes 50331648 | tf_op jit(solution)/shard_map/cond/branch_1_fun/row_unpack/pallas_call | solution.py:229
  102.9 15.1 %square_group.15 = (bf16[4,6144,128]{2,1,0:T(8,128)(2,1)}, f32[1024,512]{1,0:T(8,128)}, bf16[1024,512]{1,0:T(8,128)(2,1)}) custom-call(s32[8,128]{1,0:T(8,128)} %select_reduce_fusion.2.lists_ref, s32[8,17]{1,0:T(8,128)} %copy.46.counts_ref, s32[2]{0:T(128)S(1)} %get-tuple-element.80.place_ref.refs_25_, bf16[1024,6144]{1,0:T(8,128)(2,1)} %row_unpack.6.refs_0_, ...), custom_call_target="tpu_custom_call" | custom-call | flops 6442450944 | bytes 28311552 | tf_op jit(solution)/shard_map/cond/branch_1_fun/square_group/pallas_call | solution.py:334
  118.0 0.6 collective-permute-done.26.refs_0_
  118.6 0.9 collective-permute-done.27.refs_1_
  119.7 1.0 copy-done.23
  120.6 9.1 %row_unpack.7.refs_0_.refs_1_ = bf16[1024,2048]{1,0:T(8,128)(2,1)} custom-call(s32[64,64]{1,0:T(8,128)S(1)} %get-tuple-element.78.table_ref, s32[2]{0:T(128)S(1)} %get-tuple-element.80.place_ref.refs_25_, bf16[1024,2048]{1,0:T(8,128)(2,1)} %get-tuple-element.81.x_ref, bf16[44,128,128]{2,1,0:T(8,128)(2,1)} %copy-done.22, bf16[44,128,128]{2,1,0:T(8,128)(2,1)} %copy-done.23, ...), custom_call_target="tpu_custom_call" | custom-call | bytes 16777216 | tf_op jit(solution)/shard_map/cond/branch_1_fun/row_unpack/pallas_call | solution.py:229
  129.7 2.0 stage.10
  131.8 8.4 %square_group.16 = (bf16[4,2048,128]{2,1,0:T(8,128)(2,1)}, f32[1024,512]{1,0:T(8,128)}, bf16[1024,512]{1,0:T(8,128)(2,1)}) custom-call(s32[8,128]{1,0:T(8,128)} %select_reduce_fusion.2.lists_ref, s32[8,17]{1,0:T(8,128)} %copy.46.counts_ref, s32[2]{0:T(128)S(1)} %get-tuple-element.80.place_ref.refs_25_, bf16[1024,2048]{1,0:T(8,128)(2,1)} %row_unpack.7.refs_0_.refs_1_, ...), custom_call_target="tpu_custom_call" | custom-call | flops 2147483648 | bytes 11534336 | tf_op jit(solution)/shard_map/cond/branch_1_fun/square_group/pallas_call | solution.py:334
  140.2 1.9 stage.11
  142.2 0.6 collective-permute-start.32
  142.8 0.6 collective-permute-start.33
  143.4 10.2 %all-gather.22.cloned.1.call-done.refs_3_ = bf16[176,128,128]{2,1,0:T(8,128)(2,1)} async-done(((bf16[22,128,128]{2,1,0:T(8,128)(2,1)}), bf16[176,128,128]{2,1,0:T(8,128)(2,1)}) %all-gather.22.cloned.1.call-update) | async-done | bytes 5767184 | tf_op jit(solution)/shard_map/cond/branch_1_fun/all_gather | solution.py:522
  153.6 18.9 %square_group.17 = (bf16[4,8192,128]{2,1,0:T(8,128)(2,1)}, f32[1024,512]{1,0:T(8,128)}, bf16[1024,512]{1,0:T(8,128)(2,1)}) custom-call(s32[8,128]{1,0:T(8,128)} %select_reduce_fusion.2.lists_ref, s32[8,17]{1,0:T(8,128)} %copy.46.counts_ref, s32[2]{0:T(128)S(1)} %get-tuple-element.80.place_ref.refs_25_, bf16[1024,6144]{1,0:T(8,128)(2,1)} %row_unpack.6.refs_0_, ...), custom_call_target="tpu_custom_call" | custom-call | flops 8589934592 | bytes 36700160 | tf_op jit(solution)/shard_map/cond/branch_1_fun/square_group/pallas_call | solution.py:334
  172.5 1.5 collective-permute-start.28
  174.1 1.5 collective-permute-start.29
  175.5 1.0 copy-done.1
  176.5 1.0 copy-done.3
  177.5 2.3 split.14
  179.8 0.6 collective-permute-start.34
  180.4 0.6 collective-permute-start.35
  180.9 17.9 %collective-permute-done.28.x_ref.refs_6_ = bf16[1024,512]{1,0:T(8,128)(2,1)S(1)} collective-permute-done((bf16[1024,512]{1,0:T(8,128)(2,1)}, bf16[1024,512]{1,0:T(8,128)(2,1)S(1)}, u32[]{:S(2)}, u32[]{:S(2)}) %collective-permute-start.28) | collective-permute-done | bytes 1048608 | tf_op jit(solution)/shard_map/cond/branch_1_fun/ppermute | solution.py:519
  198.8 1.6 collective-permute-done.29.y_ref.refs_7_
  200.4 2.2 split.12
  202.6 1.5 collective-permute-start.36
  204.1 0.9 collective-permute-start.37
  205.0 5.0 %all-gather.24.cloned.1.call-done.refs_4_ = bf16[160,128,128]{2,1,0:T(8,128)(2,1)} async-done(((bf16[20,128,128]{2,1,0:T(8,128)(2,1)}), bf16[160,128,128]{2,1,0:T(8,128)(2,1)}) %all-gather.24.cloned.1.call-update) | async-done | bytes 5242896 | tf_op jit(solution)/shard_map/cond/branch_1_fun/all_gather | solution.py:522
  210.0 18.9 %square_group.18 = (bf16[4,8192,128]{2,1,0:T(8,128)(2,1)}, f32[1024,512]{1,0:T(8,128)}, bf16[1024,512]{1,0:T(8,128)(2,1)}) custom-call(s32[8,128]{1,0:T(8,128)} %select_reduce_fusion.2.lists_ref, s32[8,17]{1,0:T(8,128)} %copy.46.counts_ref, s32[2]{0:T(128)S(1)} %get-tuple-element.80.place_ref.refs_25_, bf16[1024,6144]{1,0:T(8,128)(2,1)} %row_unpack.6.refs_0_, ...), custom_call_target="tpu_custom_call" | custom-call | flops 8589934592 | bytes 36700160 | tf_op jit(solution)/shard_map/cond/branch_1_fun/square_group/pallas_call | solution.py:334
  228.9 1.5 collective-permute-start.30
  230.4 1.5 collective-permute-start.31
  231.9 0.8 copy-done.19
  232.9 17.8 %cube_part.9 = (f32[1024,512]{1,0:T(8,128)}, f32[1024,512]{1,0:T(8,128)}) custom-call(bf16[1024,512]{1,0:T(8,128)(2,1)} %get-tuple-element.86.refs_0_, bf16[1024,512]{1,0:T(8,128)(2,1)} %copy-done.1, bf16[1024,512]{1,0:T(8,128)(2,1)} %copy-done.3, bf16[512,512]{1,0:T(8,128)(2,1)} %collective-permute-done.34.refs_3_, ...), custom_call_target="tpu_custom_call" | custom-call | flops 8589934592 | bytes 16777216 | tf_op jit(solution)/shard_map/cond/branch_1_fun/cube_part/pallas_call | solution.py:489
  250.7 3.7 %collective-permute-done.30.x_ref.refs_11_ = bf16[1024,512]{1,0:T(8,128)(2,1)S(1)} collective-permute-done((bf16[1024,512]{1,0:T(8,128)(2,1)}, bf16[1024,512]{1,0:T(8,128)(2,1)S(1)}, u32[]{:S(2)}, u32[]{:S(2)}) %collective-permute-start.30) | collective-permute-done | bytes 1048608 | tf_op jit(solution)/shard_map/cond/branch_1_fun/ppermute | solution.py:519
  254.4 1.2 collective-permute-done.31.y_ref.refs_12_
  255.7 1.0 copy-done.13
  256.6 2.3 split.13
  258.9 1.5 collective-permute-start.40
  260.5 1.3 collective-permute-start.41
  262.0 18.9 %square_group.19 = (bf16[4,8192,128]{2,1,0:T(8,128)(2,1)}, f32[1024,512]{1,0:T(8,128)}, bf16[1024,512]{1,0:T(8,128)(2,1)}) custom-call(s32[8,128]{1,0:T(8,128)} %select_reduce_fusion.2.lists_ref, s32[8,17]{1,0:T(8,128)} %copy.46.counts_ref, s32[2]{0:T(128)S(1)} %get-tuple-element.80.place_ref.refs_25_, bf16[1024,6144]{1,0:T(8,128)(2,1)} %row_unpack.6.refs_0_, ...), custom_call_target="tpu_custom_call" | custom-call | flops 8589934592 | bytes 36700160 | tf_op jit(solution)/shard_map/cond/branch_1_fun/square_group/pallas_call | solution.py:334
  280.9 1.5 collective-permute-start.38
  282.4 1.5 collective-permute-start.39
  284.0 0.8 copy-done.27
  284.9 31.0 %cube_part.10 = (f32[1024,512]{1,0:T(8,128)}, f32[1024,512]{1,0:T(8,128)}, f32[1024,512]{1,0:T(8,128)}, f32[1024,512]{1,0:T(8,128)}) custom-call(bf16[1024,512]{1,0:T(8,128)(2,1)} %get-tuple-element.86.refs_0_, bf16[1024,512]{1,0:T(8,128)(2,1)} %copy-done.1, bf16[1024,512]{1,0:T(8,128)(2,1)} %copy-done.3, bf16[512,512]{1,0:T(8,128)(2,1)} %collective-permute-done.34.refs_3_, ...), custom_call_target="tpu_custom_call" | custom-call | flops 17179869184 | bytes 16777216 | tf_op jit(solution)/shard_map/cond/branch_1_fun/cube_part/pallas_call | solution.py:489
  316.0 0.9 copy-done.15
  317.3 2.2 split.15
  319.5 0.6 collective-permute-start.42
  320.6 12.7 %collective-permute-done.42.refs_3_ = bf16[512,512]{1,0:T(8,128)(2,1)S(1)} collective-permute-done((bf16[512,512]{1,0:T(8,128)(2,1)}, bf16[512,512]{1,0:T(8,128)(2,1)S(1)}, u32[]{:S(2)}, u32[]{:S(2)}) %collective-permute-start.42) | collective-permute-done | bytes 524320 | tf_op jit(solution)/shard_map/cond/branch_1_fun/ppermute | solution.py:519
  333.5 0.6 copy-done.31
  334.3 20.5 %cube_part.11 = f32[1024,2048]{1,0:T(8,128)} custom-call(bf16[1024,512]{1,0:T(8,128)(2,1)} %get-tuple-element.99.refs_0_, bf16[1024,512]{1,0:T(8,128)(2,1)} %copy-done.15, bf16[1024,512]{1,0:T(8,128)(2,1)} %copy-done.17, bf16[512,512]{1,0:T(8,128)(2,1)} %copy-done.31, bf16[512,512]{1,0:T(8,128)(2,1)} %copy-done.33, ...), custom_call_target="tpu_custom_call" | custom-call | flops 8589934592 | bytes 16777216 | tf_op jit(solution)/shard_map/cond/branch_1_fun/cube_part/pallas_call | solution.py:489
  (61 shorter events, 3.3 us)
Async XLA Ops:
  10.7 92.2 %all-gather.20.cloned.1.call-start = ((), (), s32[]{:S(2)}) async-start(), calls=%async_computation.4 | async-start | bytes 8257536 | tf_op jit(solution)/shard_map/cond/branch_1_fun/all_gather | solution.py:522
  16.7 136.8 %all-gather.22.cloned.1.call-start = ((), (), s32[]{:S(2)}) async-start(), calls=%async_computation.5 | async-start | bytes 6488064 | tf_op jit(solution)/shard_map/cond/branch_1_fun/all_gather | solution.py:522
  16.8 35.5 %collective-permute-start.22 = (bf16[44,128,128]{2,1,0:T(8,128)(2,1)}, bf16[44,128,128]{2,1,0:T(8,128)(2,1)S(1)}, u32[]{:S(2)}, u32[]{:S(2)}) collective-permute-start(bf16[44,128,128]{2,1,0:T(8,128)(2,1)} %get-tuple-element.82.h0), channel_id=1, source_target_pairs={{0,8},{8,0},{16,24},{24,16},{1,9},{9,1},{17,25},{25,17},{2,10},{10... | collective-permute-start | bytes 4325384 | tf_op jit(solution)/shard_map/cond/branch_1_fun/ppermute | solution.py:519
  19.7 34.7 %collective-permute-start.25 = (bf16[44,128,128]{2,1,0:T(8,128)(2,1)}, bf16[44,128,128]{2,1,0:T(8,128)(2,1)S(1)}, u32[]{:S(2)}, u32[]{:S(2)}) collective-permute-start(bf16[44,128,128]{2,1,0:T(8,128)(2,1)} %get-tuple-element.83.h1), channel_id=1, source_target_pairs={{0,16},{8,24},{16,0},{24,8},{1,17},{9,25},{17,1},{25,9},{2,18},{10... | collective-permute-start | bytes 4325384 | tf_op jit(solution)/shard_map/cond/branch_1_fun/ppermute | solution.py:519
  21.2 61.3 %collective-permute-start.23 = (bf16[44,128,128]{2,1,0:T(8,128)(2,1)}, bf16[44,128,128]{2,1,0:T(8,128)(2,1)}, u32[]{:S(2)}, u32[]{:S(2)}) collective-permute-start(bf16[44,128,128]{2,1,0:T(8,128)(2,1)} %get-tuple-element.83.h1), channel_id=1, source_target_pairs={{0,8},{8,0},{16,24},{24,16},{1,9},{9,1},{17,25},{25,17},{2,10},{10... | collective-permute-start | bytes 4325384 | tf_op jit(solution)/shard_map/cond/branch_1_fun/ppermute | solution.py:519
  21.9 62.1 %collective-permute-start.24 = (bf16[44,128,128]{2,1,0:T(8,128)(2,1)}, bf16[44,128,128]{2,1,0:T(8,128)(2,1)}, u32[]{:S(2)}, u32[]{:S(2)}) collective-permute-start(bf16[44,128,128]{2,1,0:T(8,128)(2,1)} %get-tuple-element.82.h0), channel_id=1, source_target_pairs={{0,16},{8,24},{16,0},{24,8},{1,17},{9,25},{17,1},{25,9},{2,18},{10... | collective-permute-start | bytes 4325384 | tf_op jit(solution)/shard_map/cond/branch_1_fun/ppermute | solution.py:519
  52.3 31.7 %copy-start.6 = (bf16[44,128,128]{2,1,0:T(8,128)(2,1)}, bf16[44,128,128]{2,1,0:T(8,128)(2,1)S(1)}, u32[]{:S(2)}) copy-start(bf16[44,128,128]{2,1,0:T(8,128)(2,1)S(1)} %collective-permute-done.22.refs_0_) | copy-start | bytes 4325380 | tf_op jit(solution)/shard_map/cond
  54.4 29.6 %copy-start.7 = (bf16[44,128,128]{2,1,0:T(8,128)(2,1)}, bf16[44,128,128]{2,1,0:T(8,128)(2,1)S(1)}, u32[]{:S(2)}) copy-start(bf16[44,128,128]{2,1,0:T(8,128)(2,1)S(1)} %collective-permute-done.25.refs_3_) | copy-start | bytes 4325380 | tf_op jit(solution)/shard_map/cond
  86.0 124.0 %all-gather.24.cloned.1.call-start = ((), (), s32[]{:S(2)}) async-start(), calls=%async_computation.6 | async-start | bytes 5898240 | tf_op jit(solution)/shard_map/cond/branch_1_fun/all_gather | solution.py:522
  86.1 32.5 %collective-permute-start.26 = (bf16[44,128,128]{2,1,0:T(8,128)(2,1)}, bf16[44,128,128]{2,1,0:T(8,128)(2,1)S(1)}, u32[]{:S(2)}, u32[]{:S(2)}) collective-permute-start(bf16[44,128,128]{2,1,0:T(8,128)(2,1)} %copy-done.6), channel_id=1, source_target_pairs={{0,16},{8,24},{16,0},{24,8},{1,17},{9,25},{17,1},{25,9},{2,18},{10... | collective-permute-start | bytes 4325384 | tf_op jit(solution)/shard_map/cond/branch_1_fun/ppermute | solution.py:519
  87.5 32.0 %collective-permute-start.27 = (bf16[44,128,128]{2,1,0:T(8,128)(2,1)}, bf16[44,128,128]{2,1,0:T(8,128)(2,1)S(1)}, u32[]{:S(2)}, u32[]{:S(2)}) collective-permute-start(bf16[44,128,128]{2,1,0:T(8,128)(2,1)} %copy-done.7), channel_id=1, source_target_pairs={{0,8},{8,0},{16,24},{24,16},{1,9},{9,1},{17,25},{25,17},{2,10},{10... | collective-permute-start | bytes 4325384 | tf_op jit(solution)/shard_map/cond/branch_1_fun/ppermute | solution.py:519
  118.6 1.1 copy-start.22
  119.5 1.1 copy-start.23
  131.7 130.3 %all-gather.26.cloned.1.call-start = ((), (), s32[]{:S(2)}) async-start(), calls=%async_computation.7 | async-start | bytes 5308416 | tf_op jit(solution)/shard_map/cond/branch_1_fun/all_gather | solution.py:522
  142.2 33.4 %collective-permute-start.32 = (bf16[1024,512]{1,0:T(8,128)(2,1)}, bf16[1024,512]{1,0:T(8,128)(2,1)S(1)}, u32[]{:S(2)}, u32[]{:S(2)}) collective-permute-start(bf16[1024,512]{1,0:T(8,128)(2,1)} %get-tuple-element.86.refs_0_), channel_id=1, source_target_pairs={{0,8},{8,0},{16,24},{24,16},{1,9},{9,1},{17,25},{25,17},{2,10},{10... | collective-permute-start | bytes 3145736 | tf_op jit(solution)/shard_map/cond/branch_1_fun/ppermute | solution.py:519
  142.8 32.7 %collective-permute-start.33 = (bf16[1024,512]{1,0:T(8,128)(2,1)}, bf16[1024,512]{1,0:T(8,128)(2,1)S(1)}, u32[]{:S(2)}, u32[]{:S(2)}) collective-permute-start(bf16[1024,512]{1,0:T(8,128)(2,1)} %get-tuple-element.86.refs_0_), channel_id=1, source_target_pairs={{0,16},{8,24},{16,0},{24,8},{1,17},{9,25},{17,1},{25,9},{2,18},{10... | collective-permute-start | bytes 3145736 | tf_op jit(solution)/shard_map/cond/branch_1_fun/ppermute | solution.py:519
  172.5 26.3 %collective-permute-start.28 = (bf16[1024,512]{1,0:T(8,128)(2,1)}, bf16[1024,512]{1,0:T(8,128)(2,1)S(1)}, u32[]{:S(2)}, u32[]{:S(2)}) collective-permute-start(bf16[1024,512]{1,0:T(8,128)(2,1)} %get-tuple-element.87.refs_5_), channel_id=1, source_target_pairs={{0,8},{8,0},{16,24},{24,16},{1,9},{9,1},{17,25},{25,17},{2,10},{10... | collective-permute-start | bytes 3145736 | tf_op jit(solution)/shard_map/cond/branch_1_fun/ppermute | solution.py:519
  174.1 26.4 %collective-permute-start.29 = (bf16[1024,512]{1,0:T(8,128)(2,1)}, bf16[1024,512]{1,0:T(8,128)(2,1)}, u32[]{:S(2)}, u32[]{:S(2)}) collective-permute-start(bf16[1024,512]{1,0:T(8,128)(2,1)} %get-tuple-element.87.refs_5_), channel_id=1, source_target_pairs={{0,16},{8,24},{16,0},{24,8},{1,17},{9,25},{17,1},{25,9},{2,18},{10... | collective-permute-start | bytes 3145736 | tf_op jit(solution)/shard_map/cond/branch_1_fun/ppermute | solution.py:519
  175.5 1.0 copy-start.1
  176.5 1.0 copy-start.3
  179.8 50.7 %collective-permute-start.34 = (bf16[512,512]{1,0:T(8,128)(2,1)}, bf16[512,512]{1,0:T(8,128)(2,1)}, u32[]{:S(2)}, u32[]{:S(2)}) collective-permute-start(bf16[512,512]{1,0:T(8,128)(2,1)} %get-tuple-element.91), channel_id=1, source_target_pairs={{0,16},{8,24},{16,0},{24,8},{1,17},{9,25},{17,1},{25,9},{2,18},{10... | collective-permute-start | bytes 1572872 | tf_op jit(solution)/shard_map/cond/branch_1_fun/ppermute | solution.py:519
  180.4 51.5 %collective-permute-start.35 = (bf16[512,512]{1,0:T(8,128)(2,1)}, bf16[512,512]{1,0:T(8,128)(2,1)}, u32[]{:S(2)}, u32[]{:S(2)}) collective-permute-start(bf16[512,512]{1,0:T(8,128)(2,1)} %get-tuple-element.92), channel_id=1, source_target_pairs={{0,8},{8,0},{16,24},{24,16},{1,9},{9,1},{17,25},{25,17},{2,10},{10... | collective-permute-start | bytes 1572872 | tf_op jit(solution)/shard_map/cond/branch_1_fun/ppermute | solution.py:519
  198.8 1.6 copy-start.5
  202.6 29.3 %collective-permute-start.36 = (bf16[512,512]{1,0:T(8,128)(2,1)}, bf16[512,512]{1,0:T(8,128)(2,1)S(1)}, u32[]{:S(2)}, u32[]{:S(2)}) collective-permute-start(bf16[512,512]{1,0:T(8,128)(2,1)} %get-tuple-element.88.refs_5_), channel_id=1, source_target_pairs={{0,16},{8,24},{16,0},{24,8},{1,17},{9,25},{17,1},{25,9},{2,18},{10... | collective-permute-start | bytes 1572872 | tf_op jit(solution)/shard_map/cond/branch_1_fun/ppermute | solution.py:519
  204.1 27.8 %collective-permute-start.37 = (bf16[512,512]{1,0:T(8,128)(2,1)}, bf16[512,512]{1,0:T(8,128)(2,1)S(1)}, u32[]{:S(2)}, u32[]{:S(2)}) collective-permute-start(bf16[512,512]{1,0:T(8,128)(2,1)} %get-tuple-element.93), channel_id=1, source_target_pairs={{0,8},{8,0},{16,24},{24,16},{1,9},{9,1},{17,25},{25,17},{2,10},{10... | collective-permute-start | bytes 1572872 | tf_op jit(solution)/shard_map/cond/branch_1_fun/ppermute | solution.py:519
  228.9 25.5 %collective-permute-start.30 = (bf16[1024,512]{1,0:T(8,128)(2,1)}, bf16[1024,512]{1,0:T(8,128)(2,1)S(1)}, u32[]{:S(2)}, u32[]{:S(2)}) collective-permute-start(bf16[1024,512]{1,0:T(8,128)(2,1)} %get-tuple-element.89.refs_10_), channel_id=1, source_target_pairs={{0,8},{8,0},{16,24},{24,16},{1,9},{9,1},{17,25},{25,17},{2,10},{10... | collective-permute-start | bytes 3145736 | tf_op jit(solution)/shard_map/cond/branch_1_fun/ppermute | solution.py:519
  230.4 25.2 %collective-permute-start.31 = (bf16[1024,512]{1,0:T(8,128)(2,1)}, bf16[1024,512]{1,0:T(8,128)(2,1)S(1)}, u32[]{:S(2)}, u32[]{:S(2)}) collective-permute-start(bf16[1024,512]{1,0:T(8,128)(2,1)} %get-tuple-element.89.refs_10_), channel_id=1, source_target_pairs={{0,16},{8,24},{16,0},{24,8},{1,17},{9,25},{17,1},{25,9},{2,18},{10... | collective-permute-start | bytes 3145736 | tf_op jit(solution)/shard_map/cond/branch_1_fun/ppermute | solution.py:519
  231.9 0.8 copy-start.19
  231.9 1.0 copy-start.21
  254.4 1.2 copy-start.11
  255.7 1.0 copy-start.13
  258.9 25.0 %collective-permute-start.40 = (bf16[512,512]{1,0:T(8,128)(2,1)}, bf16[512,512]{1,0:T(8,128)(2,1)S(1)}, u32[]{:S(2)}, u32[]{:S(2)}) collective-permute-start(bf16[512,512]{1,0:T(8,128)(2,1)} %get-tuple-element.90.refs_6_), channel_id=1, source_target_pairs={{0,16},{8,24},{16,0},{24,8},{1,17},{9,25},{17,1},{25,9},{2,18},{10... | collective-permute-start | bytes 1572872 | tf_op jit(solution)/shard_map/cond/branch_1_fun/ppermute | solution.py:519
  260.5 23.5 %collective-permute-start.41 = (bf16[512,512]{1,0:T(8,128)(2,1)}, bf16[512,512]{1,0:T(8,128)(2,1)S(1)}, u32[]{:S(2)}, u32[]{:S(2)}) collective-permute-start(bf16[512,512]{1,0:T(8,128)(2,1)} %get-tuple-element.100), channel_id=1, source_target_pairs={{0,8},{8,0},{16,24},{24,16},{1,9},{9,1},{17,25},{25,17},{2,10},{10... | collective-permute-start | bytes 1572872 | tf_op jit(solution)/shard_map/cond/branch_1_fun/ppermute | solution.py:519
  280.9 35.1 %collective-permute-start.38 = (bf16[1024,512]{1,0:T(8,128)(2,1)}, bf16[1024,512]{1,0:T(8,128)(2,1)S(1)}, u32[]{:S(2)}, u32[]{:S(2)}) collective-permute-start(bf16[1024,512]{1,0:T(8,128)(2,1)} %get-tuple-element.99.refs_0_), channel_id=1, source_target_pairs={{0,8},{8,0},{16,24},{24,16},{1,9},{9,1},{17,25},{25,17},{2,10},{10... | collective-permute-start | bytes 3145736 | tf_op jit(solution)/shard_map/cond/branch_1_fun/ppermute | solution.py:519
  282.4 33.6 %collective-permute-start.39 = (bf16[1024,512]{1,0:T(8,128)(2,1)}, bf16[1024,512]{1,0:T(8,128)(2,1)S(1)}, u32[]{:S(2)}, u32[]{:S(2)}) collective-permute-start(bf16[1024,512]{1,0:T(8,128)(2,1)} %get-tuple-element.99.refs_0_), channel_id=1, source_target_pairs={{0,16},{8,24},{16,0},{24,8},{1,17},{9,25},{17,1},{25,9},{2,18},{10... | collective-permute-start | bytes 3145736 | tf_op jit(solution)/shard_map/cond/branch_1_fun/ppermute | solution.py:519
  283.9 0.8 copy-start.27
  283.9 1.0 copy-start.29
  284.9 49.4 %copy-start.35 = (s32[64,64]{1,0:T(8,128)S(1)}, s32[64,64]{1,0:T(8,128)}, u32[]{:S(2)}) copy-start(s32[64,64]{1,0:T(8,128)} %get-tuple-element.110.refs_26_) | copy-start | bytes 49156 | tf_op jit(solution)/shard_map/cond
  284.9 49.4 %copy-start.38 = (s32[64,64]{1,0:T(8,128)S(1)}, s32[64,64]{1,0:T(8,128)}, u32[]{:S(2)}) copy-start(s32[64,64]{1,0:T(8,128)} %get-tuple-element.111.refs_27_) | copy-start | bytes 49156 | tf_op jit(solution)/shard_map/cond
  315.9 1.0 copy-start.15
  316.0 1.4 copy-start.17
  319.5 13.8 %collective-permute-start.42 = (bf16[512,512]{1,0:T(8,128)(2,1)}, bf16[512,512]{1,0:T(8,128)(2,1)S(1)}, u32[]{:S(2)}, u32[]{:S(2)}) collective-permute-start(bf16[512,512]{1,0:T(8,128)(2,1)} %get-tuple-element.105), channel_id=1, source_target_pairs={{0,16},{8,24},{16,0},{24,8},{1,17},{9,25},{17,1},{25,9},{2,18},{10... | collective-permute-start | bytes 1572872 | tf_op jit(solution)/shard_map/cond/branch_1_fun/ppermute | solution.py:519
  320.1 13.4 %collective-permute-start.43 = (bf16[512,512]{1,0:T(8,128)(2,1)}, bf16[512,512]{1,0:T(8,128)(2,1)S(1)}, u32[]{:S(2)}, u32[]{:S(2)}) collective-permute-start(bf16[512,512]{1,0:T(8,128)(2,1)} %get-tuple-element.106), channel_id=1, source_target_pairs={{0,8},{8,0},{16,24},{24,16},{1,9},{9,1},{17,25},{25,17},{2,10},{10... | collective-permute-start | bytes 1572872 | tf_op jit(solution)/shard_map/cond/branch_1_fun/ppermute | solution.py:519
  333.3 0.8 copy-start.31
  333.5 0.8 copy-start.33
Sparse Core Ops, SparseCore 0:
  16.9 75.9 all-gather.19
  94.5 59.0 all-gather.21
  155.2 54.7 all-gather.23
  211.5 50.4 all-gather.25

commit v3 on v2

--- a/solution.py
+++ b/solution.py
@@ -12,8 +12,8 @@
 TILE = 128
 ROW_GROUP = 4
 WIDTHS = (4, 4, 4, 4)
-SIGMAS = ((3.2, 2.1), (4.2, 3.9))
-DEPTH = 1024
+SIGMAS = ((3.2, 2.1), (4.2, 3.5))
+SMALL = pl.CostEstimate(flops=1, bytes_accessed=1, transcendentals=0)
 VMEM_BYTES = 60 * 2**20
 SMEM = pl.BlockSpec(memory_space=pltpu.SMEM)
 VMEM = pl.BlockSpec(memory_space=pltpu.VMEM)
@@ -81,7 +81,8 @@
     order = mine.transpose(0, 2, 1).reshape(blocks, tiles, 1)
     which = lax.broadcasted_iota(jnp.int32, (blocks, tiles, tiles), 1)
     slot = lax.broadcasted_iota(jnp.int32, (blocks, tiles, tiles), 2)
-    lists = jnp.sum(jnp.where(order == slot, which, 0), 1)
+    spot = which // tile_rows * n + which % tile_rows
+    lists = jnp.sum(jnp.where(order == slot, spot, 0), 1)
     column = lax.broadcasted_iota(jnp.int32, (blocks, tiles, tile_cols + 1), 1) // tile_rows
     limit = lax.broadcasted_iota(jnp.int32, (blocks, tiles, tile_cols + 1), 2)
     counts = jnp.sum(jnp.where((order >= 0) & (column < limit), 1, 0), 1)
@@ -237,7 +238,7 @@
             pltpu.SemaphoreType.DMA((len(flat),)),
         ],
         compiler_params=pltpu.CompilerParams(vmem_limit_bytes=VMEM_BYTES),
-        cost_estimate=pl.CostEstimate(flops=0, bytes_accessed=8 * len(ks) * nrows * ncols, transcendentals=0),
+        cost_estimate=SMALL,
         name="row_unpack",
     )(table, place, density, *flat, *after)
 
@@ -249,8 +250,8 @@
     count = len(ks)
     depth = count * span
     n = width * TILE
+    n_tiles = ROW_GROUP * tile_cols
     bits = (tile_cols * width).bit_length()
-    step_rows = nrows // 2
 
     def kernel(lists_ref, counts_ref, place_ref, *refs):
         a_refs, refs = refs[: len(row_parts)], refs[len(row_parts) :]
@@ -273,22 +274,21 @@
             before.start()
 
         def fetch(k, z):
-            rows = pl.ds(pl.multiple_of(k * span, span), span)
-            panel[:, rows] = jnp.zeros((width, span, TILE), panel.dtype)
+            for j in range(width):
+                at = pl.ds(j * n_tiles + k * tile_cols, tile_cols)
+                panel[at] = jnp.zeros((tile_cols, TILE, TILE), panel.dtype)
             total = jnp.int32(0)
             for o in range(owners):
                 owner = (r ^ (k + ks[0])) * owners + o
                 begin, end = counts_ref[owner, first], counts_ref[owner, first + width]
                 total += end - begin
-                top = k * span + o * tile_rows * TILE
+                base = k * tile_cols + o * tile_rows - first * n_tiles
                 for q, (lo, hi) in enumerate(spans[: len(chunks)]):
                     shift = owner * (hi - lo) - lo
 
                     def one(slot, z):
-                        tile = lists_ref[owner, slot]
-                        j, i = tile // tile_rows - first, tile % tile_rows
-                        here = pl.ds(pl.multiple_of(top + i * TILE, TILE), TILE)
-                        pltpu.make_async_copy(ins[q].at[shift + slot], panel.at[j, here], sems.at[k]).start()
+                        target = panel.at[base + lists_ref[owner, slot]]
+                        pltpu.make_async_copy(ins[q].at[shift + slot], target, sems.at[k]).start()
                         return z
 
                     lax.fori_loop(jnp.maximum(begin, lo), jnp.minimum(end, hi), one, 0)
@@ -297,9 +297,12 @@
 
         lax.fori_loop(0, count, fetch, 0)
 
-        def out_copy(k):
-            rows = pl.ds(pl.multiple_of(k * span, span), span)
-            return pltpu.make_async_copy(panel.at[:, rows], panel_out.at[:, rows], out_sem)
+        def out_copies(k):
+            rows = pl.ds(k * tile_cols, tile_cols)
+            return [
+                pltpu.make_async_copy(panel.at[pl.ds(j * n_tiles + k * tile_cols, tile_cols)], panel_out.at[j, rows], out_sem)
+                for j in range(width)
+            ]
 
         def multiply(k, z):
             for bit in range(bits):
@@ -310,16 +313,13 @@
                     pltpu.make_async_copy(some, some, sems.at[k]).wait()
 
             pltpu.make_async_copy(a.at[k], a.at[k], a_sems.at[k]).wait()
-            out_copy(k).start()
-            rows = pl.ds(pl.multiple_of(k * span, span), span)
-
-            def step(m, z):
-                here = pl.ds(pl.multiple_of(m * step_rows, step_rows), step_rows)
-                right = jnp.concatenate([panel[j, rows] for j in range(width)], 1)
-                square[here] += jnp.dot(a[k, here], right, preferred_element_type=jnp.float32)
-                return z
-
-            return lax.fori_loop(0, nrows // step_rows, step, z)
+            for copy in out_copies(k):
+                copy.start()
+            right = jnp.concatenate([
+                panel[pl.ds(j * n_tiles + k * tile_cols, tile_cols)].reshape(span, TILE) for j in range(width)
+            ], 1)
+            square[...] += jnp.dot(a[k], right, preferred_element_type=jnp.float32)
+            return z
 
         if partial is not None:
             before.wait()
@@ -328,13 +328,14 @@
         lax.fori_loop(0, count, multiply, 0)
         low[...] = square[...].astype(jnp.bfloat16)
         for k in range(count):
-            out_copy(k).wait()
+            for copy in out_copies(k):
+                copy.wait()
 
     operands = [*row_parts, *chunks, *([] if partial is None else [partial]), *after]
     return pl.pallas_call(
         kernel,
         out_shape=[
-            jax.ShapeDtypeStruct((width, depth, TILE), jnp.bfloat16),
+            jax.ShapeDtypeStruct((width, count * tile_cols, TILE, TILE), jnp.bfloat16),
             jax.ShapeDtypeStruct((nrows, n), jnp.float32),
             jax.ShapeDtypeStruct((nrows, n), jnp.bfloat16),
         ],
@@ -342,7 +343,7 @@
         out_specs=[ANY, VMEM, VMEM],
         scratch_shapes=[
             pltpu.VMEM((count, nrows, span), jnp.bfloat16),
-            pltpu.VMEM((width, depth, TILE), jnp.bfloat16),
+            pltpu.VMEM((width * n_tiles, TILE, TILE), jnp.bfloat16),
             pltpu.SMEM((count,), jnp.int32),
             pltpu.SemaphoreType.DMA((count,)),
             pltpu.SemaphoreType.DMA((count,)),
@@ -350,43 +351,43 @@
             pltpu.SemaphoreType.DMA,
         ],
         compiler_params=pltpu.CompilerParams(vmem_limit_bytes=VMEM_BYTES),
-        cost_estimate=pl.CostEstimate(
-            flops=2 * nrows * depth * n, bytes_accessed=2 * depth * (nrows + 2 * n) + 6 * nrows * n, transcendentals=0
-        ),
+        cost_estimate=SMALL,
         name="square_group",
     )(lists, counts, place, *operands)
 
 
-def cube_part(strips, panels, jobs, widths, before, finish=None, after=()):
+def cube_part(strips, panels, jobs, widths, before, keep=None, squares=None, base=None, joined=False, after=()):
     groups = sorted({g for job in jobs.values() for g in job})
     firsts = [sum(widths[:h]) for h in range(len(widths))]
-    span = sum(widths) * TILE
-    nrows = strips[groups[0]][0][0][0].shape[0]
+    tile_cols = sum(widths)
+    span = tile_cols * TILE
+    nrows = strips[0][0][0][0].shape[0]
+    tile_rows = nrows // TILE
     lefts, start = [], {}
     at = 0
-    for g in groups:
-        start[g] = at
-        for pieces in strips[g]:
-            lefts += [(x, row, at) for x, row in pieces]
+    for group in groups:
+        g, ks = group
+        start[group] = at
+        for k in ks:
+            lefts += [(x, row, at, group) for x, row in strips[g][k]]
             at += widths[g] * TILE
     total = at
     hs = list(jobs)
-    deepest = max(ROW_GROUP * TILE * sum(widths[g] for g in job) for job in jobs.values())
+    deepest = max(sum(len(ks) * widths[g] for g, ks in job) for job in jobs.values())
     widest = max(widths[h] for h in hs)
-    panel_arrays = [x for h in hs for x, _ in panels[h]]
-    operands = [x for x, *_ in lefts] + panel_arrays + [before[h] for h in hs if h in before]
     with_before = [h for h in hs if h in before]
+    held_from = base if base is not None else squares
+    operands = [x for x, *_ in lefts] + [x for h in hs for x, _ in panels[h]] + [before[h] for h in with_before]
     specs = [ANY] * len(operands)
-    if finish is not None:
-        place, pattern_square, pattern_cube, squares = finish
-        operands += [place, pattern_square, pattern_cube, *squares]
-        specs += [SMEM] * 3 + [ANY] * len(squares)
+    if keep is not None:
+        operands += [*keep, *(held_from[h] for h in hs)]
+        specs += [SMEM] * 3 + [ANY] * len(hs)
+    operands += after
+    specs += [ANY] * len(after)
+    if joined:
         out_shape = [jax.ShapeDtypeStruct((nrows, span), jnp.float32)]
     else:
         out_shape = [jax.ShapeDtypeStruct((nrows, widths[h] * TILE), jnp.float32) for h in hs]
-    operands += after
-    specs += [ANY] * len(after)
-    step_rows = nrows // 2
 
     def kernel(*refs):
         refs = list(refs)
@@ -399,46 +400,80 @@
         left_refs = take(len(lefts))
         panel_refs = {h: take(ROW_GROUP) for h in hs}
         before_refs = dict(zip(with_before, take(len(with_before))))
-        if finish is not None:
+        if keep is not None:
             place_ref, keep_square, keep_cube = take(3)
-            square_refs = take(len(hs))
+            held_refs = dict(zip(hs, take(len(hs))))
         take(len(after))
         outs = take(len(out_shape))
         left, right, acc, held, left_sems, right_sems, acc_sems, held_sems, out_sems = refs
 
-        def loads(n):
-            h, s, t = hs[n], n % 2, n % 3
+        def left_copies(g):
+            return [
+                pltpu.make_async_copy(
+                    ref, left.at[pl.ds(row, x.shape[0]), pl.ds(at, x.shape[1])], left_sems.at[groups.index(g)]
+                )
+                for ref, (x, row, at, group) in zip(left_refs, lefts)
+                if group == g
+            ]
+
+        def right_copies(n, at, group):
+            h, s = hs[n], n % 2
+            g, ks = group
+            copies = []
+            for m, k in enumerate(ks):
+                ref, shift = panel_refs[h][k], panels[h][k][1]
+                copies.append(pltpu.make_async_copy(
+                    ref.at[:, pl.ds(shift + firsts[g], widths[g])],
+                    right.at[s, pl.ds(0, widths[h]), pl.ds(at + m * widths[g], widths[g])],
+                    right_sems.at[s, jobs[h].index(group)],
+                ))
+            return copies
+
+        def acc_copies(n):
+            h, t = hs[n], n % 3
             lanes = pl.ds(0, widths[h] * TILE)
-            copies, at = [], 0
-            for g in jobs[h]:
-                rows = widths[g] * TILE
-                for k, (ref, (_, shift)) in enumerate(zip(panel_refs[h], panels[h])):
-                    source = ref.at[:, pl.ds(shift + firsts[g] * TILE, rows)]
-                    target = right.at[s, pl.ds(0, widths[h]), pl.ds(at, rows)]
-                    copies.append(pltpu.make_async_copy(source, target, right_sems.at[s]))
-                    at += rows
+            copies = []
             if h in before_refs:
                 copies.append(pltpu.make_async_copy(before_refs[h], acc.at[t, :, lanes], acc_sems.at[t]))
-            if finish is not None:
-                copies.append(pltpu.make_async_copy(square_refs[n], held.at[t, :, lanes], held_sems.at[t]))
             return copies
+
+        def held_copies(n):
+            h, t = hs[n], n % 3
+            lanes = pl.ds(0, widths[h] * TILE)
+            copies = []
+            if keep is not None:
+                copies.append(pltpu.make_async_copy(held_refs[h], held.at[t, :, lanes], held_sems.at[t]))
+            return copies
+
+        def steps(h):
+            at, found = 0, []
+            for g in jobs[h]:
+                found.append((at, g))
+                at += len(g[1]) * widths[g[0]]
+            return found
+
+        def loads(n):
+            copies = []
+            for m, (at, g) in enumerate(steps(hs[n])):
+                if n == 0:
+                    copies += left_copies(g)
+                copies += right_copies(n, at, g)
+                if m == 0:
+                    copies += acc_copies(n)
+            if n == 0:
+                copies += [copy for g in groups if g not in jobs[hs[0]] for copy in left_copies(g)]
+            return copies + held_copies(n)
 
         def store(n):
             h, t = hs[n], n % 3
             lanes = pl.ds(0, widths[h] * TILE)
-            if finish is None:
-                return pltpu.make_async_copy(acc.at[t, :, lanes], outs[n], out_sems.at[t])
-            target = outs[0].at[:, pl.ds(firsts[h] * TILE, widths[h] * TILE)]
-            return pltpu.make_async_copy(held.at[t, :, lanes], target, out_sems.at[t])
-
-        left_copies = [
-            pltpu.make_async_copy(ref, left.at[pl.ds(row, x.shape[0]), pl.ds(col, x.shape[1])], left_sems.at[0])
-            for ref, (x, row, col) in zip(left_refs, lefts)
-        ]
-        for copy in left_copies + loads(0):
+            source = (acc if keep is None else held).at[t, :, lanes]
+            target = outs[n] if not joined else outs[0].at[:, pl.ds(firsts[h] * TILE, widths[h] * TILE)]
+            return pltpu.make_async_copy(source, target, out_sems.at[t])
+
+        for copy in loads(0):
             copy.start()
-        for copy in left_copies:
-            copy.wait()
+        arrived = set()
         for n, h in enumerate(hs):
             s, t, wide = n % 2, n % 3, widths[h] * TILE
             if n >= 2:
@@ -446,46 +481,45 @@
             if n + 1 < len(hs):
                 for copy in loads(n + 1):
                     copy.start()
-            for copy in loads(n):
+            row, col = (place_ref[0] * tile_rows, place_ref[1] * tile_cols + firsts[h]) if keep is not None else (0, 0)
+            for copy in acc_copies(n):
                 copy.wait()
-            if h not in before_refs:
-                acc[t, :, :wide] = jnp.zeros((nrows, wide), jnp.float32)
-            shift = start[jobs[h][0]]
-            blocks = ROW_GROUP * TILE * sum(widths[g] for g in jobs[h]) // DEPTH
-
-            def step(b, z):
-                here = pl.ds(pl.multiple_of(b * DEPTH, DEPTH), DEPTH)
-                there = pl.ds(pl.multiple_of(shift + b * DEPTH, DEPTH), DEPTH)
-
-                def rows_step(m, z):
-                    rows = pl.ds(pl.multiple_of(m * step_rows, step_rows), step_rows)
-                    other = jnp.concatenate([right[s, j, here] for j in range(widths[h])], 1)
-                    part = jnp.dot(left[rows, there], other, preferred_element_type=jnp.float32)
-                    acc[t, rows, :wide] += part
-                    return z
-
-                return lax.fori_loop(0, nrows // step_rows, rows_step, z)
-
-            lax.fori_loop(0, blocks, step, 0)
-            if finish is not None:
-                tile_rows, tile_cols = nrows // TILE, span // TILE
-                row, col = place_ref[0] * tile_rows, place_ref[1] * tile_cols + firsts[h]
-
-                def combine(i, z):
-                    rows = pl.ds(pl.multiple_of(i * TILE, TILE), TILE)
+            found = steps(h)
+            for m, (at, g) in enumerate(found):
+                if g not in arrived:
+                    arrived.add(g)
+                    for copy in left_copies(g):
+                        copy.wait()
+                for copy in right_copies(n, at, g):
+                    copy.wait()
+                last = m == len(found) - 1
+                if last:
+                    for copy in held_copies(n):
+                        copy.wait()
+                depth = len(g[1]) * widths[g[0]]
+                other = jnp.concatenate(
+                    [right[s, j, at : at + depth].reshape(depth * TILE, TILE) for j in range(widths[h])], 1
+                )
+                lanes = slice(start[g], start[g] + depth * TILE)
+                part = jnp.dot(left[:, lanes], other, preferred_element_type=jnp.float32)
+                if m > 0 or h in before_refs:
+                    part += acc[t, :, :wide]
+                if keep is None or not last:
+                    acc[t, :, :wide] = part
+                    continue
+                for i in range(tile_rows):
+                    rows = slice(i * TILE, (i + 1) * TILE)
                     for j in range(widths[h]):
                         lanes = slice(j * TILE, (j + 1) * TILE)
-                        a = 3.0 * keep_square[row + i, col + j].astype(jnp.float32)
                         b = 2.0 * keep_cube[row + i, col + j].astype(jnp.float32)
-                        held[t, rows, lanes] = a * held[t, rows, lanes] - b * acc[t, rows, lanes]
-                    return z
-
-                lax.fori_loop(0, tile_rows, combine, 0)
+                        rest = held[t, rows, lanes]
+                        if base is None:
+                            rest = 3.0 * keep_square[row + i, col + j].astype(jnp.float32) * rest
+                        held[t, rows, lanes] = rest - b * part[rows, lanes]
             store(n).start()
         for n in range(max(len(hs) - 2, 0), len(hs)):
             store(n).wait()
 
-    flops = sum(2 * nrows * ROW_GROUP * TILE * widths[g] * widths[h] * TILE for h in hs for g in jobs[h])
     return pl.pallas_call(
         kernel,
         out_shape=out_shape,
@@ -493,17 +527,17 @@
         out_specs=[ANY] * len(out_shape),
         scratch_shapes=[
             pltpu.VMEM((nrows, total), jnp.bfloat16),
-            pltpu.VMEM((2, widest, deepest, TILE), jnp.bfloat16),
+            pltpu.VMEM((2, widest, deepest, TILE, TILE), jnp.bfloat16),
             pltpu.VMEM((3, nrows, widest * TILE), jnp.float32),
-            pltpu.VMEM((3, nrows, widest * TILE) if finish is not None else (3, 8, TILE), jnp.float32),
-            pltpu.SemaphoreType.DMA((1,)),
-            pltpu.SemaphoreType.DMA((2,)),
+            pltpu.VMEM((3, nrows, widest * TILE) if keep is not None else (3, 8, TILE), jnp.float32),
+            pltpu.SemaphoreType.DMA((len(groups),)),
+            pltpu.SemaphoreType.DMA((2, max(len(job) for job in jobs.values()))),
             pltpu.SemaphoreType.DMA((3,)),
             pltpu.SemaphoreType.DMA((3,)),
             pltpu.SemaphoreType.DMA((3,)),
         ],
         compiler_params=pltpu.CompilerParams(vmem_limit_bytes=VMEM_BYTES),
-        cost_estimate=pl.CostEstimate(flops=flops, bytes_accessed=8 * nrows * span, transcendentals=0),
+        cost_estimate=SMALL,
         name="cube_part",
     )(*operands)
 
@@ -531,9 +565,10 @@
     group = functools.partial(square_group, lists, counts, place)
     panels, squares, strips = [], [], []
 
-    def send(square, low):
+    def send(square, low, at_once):
         squares.append(square)
-        strips.append([[(low, 0)], [(swap(low, 1), 0)], [(swap(low, 2), 0)]])
+        others = (1, 2, 3) if at_once else (1, 2)
+        strips.append([[(low, 0)]] + [[(swap(low, k), 0)] for k in others])
 
     def forward(h, after=()):
         (x, _), (y, _) = strips[h][1][0], strips[h][2][0]
@@ -545,28 +580,37 @@
     far_part = row_unpack(table, place, density, [far], [3], [partial])
     chunks.append(gather(stage(halves, *spans[2], [far_part])))
     far_panel, square, low = group([far_part], chunks[:1], spans, 0, widths[0], shape, [3], partial)
-    panels.append([(near_panel, k * ncols) for k in range(3)] + [(far_panel, 0)])
-    send(square, low)
-
-    def next_group(h, after):
+    panels.append([(near_panel, k * shape[1]) for k in range(3)] + [(far_panel, 0)])
+    send(square, low, False)
+
+    def next_group(h, at_once, after):
         parts = [near_part, far_part]
         panel, square, low = group(
             parts, chunks[: h + 1], spans, sum(widths[:h]), widths[h], shape, [0, 1, 2, 3], None, after
         )
-        panels.append([(panel, k * ncols) for k in range(ROW_GROUP)])
-        send(square, low)
-
-    next_group(1, [])
+        panels.append([(panel, k * shape[1]) for k in range(ROW_GROUP)])
+        send(square, low, at_once)
+
+    next_group(1, False, [])
     forward(0)
     chunks.append(gather(stage(halves, *spans[3], [low])))
-    next_group(2, [forward(1)])
-    cubes = dict(enumerate(cube_part(strips, panels, {0: [0, 1], 1: [0, 1]}, widths, {}, after=[squares[2]])))
-    next_group(3, [forward(2), cubes[0]])
-    jobs = {0: [2], 1: [2], 2: [0, 1, 2], 3: [0, 1, 2]}
-    cubes = dict(enumerate(cube_part(strips, panels, jobs, widths, cubes)))
-    forward(3, [cubes[0]])
-    finish = place, pattern_square, pattern_cube, squares
-    return cube_part(strips, panels, {h: [3] for h in range(4)}, widths, cubes, finish)[0]
+    next_group(2, True, [forward(1)])
+    every = tuple(range(ROW_GROUP))
+    first, second, third = [(g, every) for g in range(3)]
+    keep = place, pattern_square, pattern_cube
+
+    def add(jobs, base=None, joined=False, after=()):
+        return dict(zip(jobs, cube_part(
+            strips, panels, jobs, widths, {}, keep, squares if base is None else None, base, joined, after
+        )))
+
+    parts = add({0: [first, second], 1: [first, second]}, after=[squares[2]])
+    next_group(3, False, [parts[0]])
+    parts.update(add({2: [first, second], 3: [first, second]}))
+    parts = add({h: [third] for h in range(4)}, parts)
+    forward(3, [parts[0]])
+    parts = add({h: [(3, every[:3])] for h in range(4)}, parts)
+    return add({h: [(3, every[3:])] for h in range(4)}, parts, True)[0]
 
 
 def local(density, pattern_p, pattern_square, pattern_cube):

time: 366 us -> 354 us (0.967)
  waiting for transfers between devices: 116 us -> 101 us
  loops' own time: 6.59 us -> 11.5 us
    ppermute x22 -> x21, waiting for transfers between devices: 101 us -> 79 us  [swap(): return lax.ppermute(x, 'row', [(i, i ^ k) for i in range(ROW_GROUP)])]
    all_gather x4, waiting for transfers between devices: 15.4 us -> 22.2 us  [gather(): return lax.all_gather(x, 'col', axis=0, tiled=True)]
    pallas_call x3 -> x5, Pallas kernels: 69.3 us -> 75.9 us  [cube_part(): pl.pallas_call(kernel, out_shape=out_shape, in_specs=specs, out_specs=[AN...]
    another operation x1, loops' own time: 6.59 us -> 11.5 us  [local(): return lax.switch(level, ways)]
    pallas_call x4 -> x3, Pallas kernels: 8.88 us -> 6.58 us  [split(): pl.pallas_call(kernel, out_shape=[half, half], in_specs=[ANY] * (2 + len(...]
    cond x38 -> x40, local copies, waits for them, and re-layouts: 8.18 us -> 6.67 us
    ppermute x22 -> x21, starting transfers between devices: 25 us -> 24.5 us  [swap(): return lax.ppermute(x, 'row', [(i, i ^ k) for i in range(ROW_GROUP)])]
  transfers between devices with their start and end apart: 26 -> 25, of which waited for: 15 -> 10; matrix products, arithmetic and copies ran while one was open for 1% -> 1% of each run, Pallas kernels for 44% -> 49%
where the time goes in v3:
time: 354 us; the launch traced here: 357 us
  Pallas kernels  193 us (55%)
  waiting for transfers between devices  101 us (29%)
  starting transfers between devices  24.7 us (7%)
  between operations  14.7 us (4%)
  loops' own time  11.5 us (3%)
  local copies, waits for them, and re-layouts  7.59 us (2%)
    ppermute x21, waiting for transfers between devices, swap(): return lax.ppermute(x, 'row', [(i, i ^ k) for i in range(ROW_GROUP)])  79 us
    pallas_call x5, Pallas kernels, square_group(): pl.pallas_call(kernel, out_shape=[jax.ShapeDtypeStruct((width, count * ti...  77.4 us
    pallas_call x5, Pallas kernels, cube_part(): pl.pallas_call(kernel, out_shape=out_shape, in_specs=specs, out_specs=[AN...  75.9 us
    ppermute x21, starting transfers between devices, swap(): return lax.ppermute(x, 'row', [(i, i ^ k) for i in range(ROW_GROUP)])  24.5 us
    all_gather x4, waiting for transfers between devices, gather(): return lax.all_gather(x, 'col', axis=0, tiled=True)  22.2 us
    pallas_call x2, Pallas kernels, row_unpack(): pl.pallas_call(kernel, grid=(tile_rows,), out_shape=jax.ShapeDtypeStruct(...  21.4 us
    another operation x1, loops' own time, local(): return lax.switch(level, ways)  11.5 us
  transfers between devices with their start and end apart: 25, of which 10 were waited for; matrix products, arithmetic and copies ran while one was open for 1% of the time, Pallas kernels for 49%

profile of v3, /device:TPU:0, one launch (start us, length us, event | category | flops | bytes accessed | tf_op | source)
XLA Modules:
  0.0 356.6 jit_solution(11410419524802743223)
XLA Ops:
  6.6 0.9 fusion.7
  7.5 1.8 compare_reduce_fusion
  10.7 339.1 %conditional.1 = (f32[1024,2048]{1,0:T(8,128)}) conditional(s32[]{:T(128)} %clamp.3, (s32[]{:T(128)}, s32[64,64]{1,0:T(8,128)S(1)}, s32[2]{0:T(128)S(1)}, bf16[1024,2048]{1,0:T(8,128)(2,1)}, s32[64,64]{1,0:T(8,128)}, /*index=5*/s32[64,64]{1,0:T(8,128)}) %tuple.14, (s32[]{:T(128)}, s32[64,64]{1,0:T(8,128)S(1)}, s32[2]{0:T(128)S(1)}, ...), branch_computations={%region_2.5_spmd, %region_5.8_spmd, %region_8.9_spmd} | conditional | flops 68740448256 | bytes 515693568 | solution.py:634
  15.8 5.8 %pack.3 = (bf16[42,128,128]{2,1,0:T(8,128)(2,1)}, bf16[42,128,128]{2,1,0:T(8,128)(2,1)}, bf16[28,128,128]{2,1,0:T(8,128)(2,1)}) custom-call(s32[64,64]{1,0:T(8,128)S(1)} %get-tuple-element.82.table_ref, s32[2]{0:T(128)S(1)} %get-tuple-element.84.place_ref.refs_18_.refs_20_.refs_19_, bf16[1024,2048]{1,0:T(8,128)(2,1)} %get-tuple-element.85.x_ref), custom_call_target="tpu_custom_call" | custom-call | tf_op jit(solution)/shard_map/cond/branch_1_fun/pack/pallas_call | solution.py:130
  21.7 3.1 collective-permute-start.23
  24.8 1.5 collective-permute-start.21
  26.3 0.5 collective-permute-start.24
  26.9 29.1 %collective-permute-done.23.refs_2_ = bf16[42,128,128]{2,1,0:T(8,128)(2,1)S(1)} collective-permute-done((bf16[42,128,128]{2,1,0:T(8,128)(2,1)}, bf16[42,128,128]{2,1,0:T(8,128)(2,1)S(1)}, u32[]{:S(2)}, u32[]{:S(2)}) %collective-permute-start.23) | collective-permute-done | bytes 1376288 | tf_op jit(solution)/shard_map/cond/branch_1_fun/ppermute | solution.py:553
  56.0 2.1 collective-permute-done.21.refs_0_
  58.1 26.6 %collective-permute-done.24.refs_3_ = bf16[42,128,128]{2,1,0:T(8,128)(2,1)S(1)} collective-permute-done((bf16[42,128,128]{2,1,0:T(8,128)(2,1)}, bf16[42,128,128]{2,1,0:T(8,128)(2,1)S(1)}, u32[]{:S(2)}, u32[]{:S(2)}) %collective-permute-start.24) | collective-permute-done | bytes 1376288 | tf_op jit(solution)/shard_map/cond/branch_1_fun/ppermute | solution.py:553
  84.7 1.6 collective-permute-done.22.refs_1_
  86.3 2.0 stage.9
  88.3 1.3 collective-permute-start.25
  89.6 1.5 collective-permute-start.26
  91.5 0.4 select_reduce_fusion.3
  91.9 0.7 copy.46.counts_ref
  92.5 0.9 select_reduce_fusion.2.lists_ref
  93.4 12.4 %row_unpack.6.refs_0_ = bf16[1024,6144]{1,0:T(8,128)(2,1)} custom-call(s32[64,64]{1,0:T(8,128)S(1)} %copy-done.22, s32[2]{0:T(128)S(1)} %get-tuple-element.84.place_ref.refs_18_.refs_20_.refs_19_, bf16[1024,2048]{1,0:T(8,128)(2,1)} %get-tuple-element.85.x_ref, bf16[42,128,128]{2,1,0:T(8,128)(2,1)} %copy-done.6, ...), custom_call_target="tpu_custom_call" | custom-call | flops 1 | bytes 1 | tf_op jit(solution)/shard_map/cond/branch_1_fun/row_unpack/pallas_call | solution.py:230
  105.8 14.7 %square_group.15 = (bf16[4,48,128,128]{3,2,1,0:T(8,128)(2,1)}, f32[1024,512]{1,0:T(8,128)}, bf16[1024,512]{1,0:T(8,128)(2,1)}) custom-call(s32[8,128]{1,0:T(8,128)} %select_reduce_fusion.2.lists_ref, s32[8,17]{1,0:T(8,128)} %copy.46.counts_ref, s32[2]{0:T(128)S(1)} %get-tuple-element.84.place_ref.refs_18_.refs_20_.refs_19_, ...), custom_call_target="tpu_custom_call" | custom-call | flops 1 | bytes 1 | tf_op jit(solution)/shard_map/cond/branch_1_fun/square_group/pallas_call | solution.py:335
  120.7 0.9 copy-done.31
  121.7 0.5 copy-done.32
  122.2 9.0 %row_unpack.7.refs_0_.refs_1_ = bf16[1024,2048]{1,0:T(8,128)(2,1)} custom-call(s32[64,64]{1,0:T(8,128)S(1)} %copy-done.22, s32[2]{0:T(128)S(1)} %get-tuple-element.84.place_ref.refs_18_.refs_20_.refs_19_, bf16[1024,2048]{1,0:T(8,128)(2,1)} %get-tuple-element.85.x_ref, bf16[42,128,128]{2,1,0:T(8,128)(2,1)} %copy-done.31, bf16[42,128,128]{2,1,0:T(8,128)(2,1)} %copy-done.32, ...), custom_call_target="tpu_custom_call" | custom-call | flops 1 | bytes 1 | tf_op jit(solution)/shard_map/cond/branch_1_fun/row_unpack/pallas_call | solution.py:230
  131.2 2.0 stage.10
  133.2 8.0 %square_group.16 = (bf16[4,16,128,128]{3,2,1,0:T(8,128)(2,1)}, f32[1024,512]{1,0:T(8,128)}, bf16[1024,512]{1,0:T(8,128)(2,1)}) custom-call(s32[8,128]{1,0:T(8,128)} %select_reduce_fusion.2.lists_ref, s32[8,17]{1,0:T(8,128)} %copy.46.counts_ref, s32[2]{0:T(128)S(1)} %get-tuple-element.84.place_ref.refs_18_.refs_20_.refs_19_, ...), custom_call_target="tpu_custom_call" | custom-call | flops 1 | bytes 1 | tf_op jit(solution)/shard_map/cond/branch_1_fun/square_group/pallas_call | solution.py:335
  141.3 1.8 stage.11
  143.1 1.1 collective-permute-start.28
  144.3 0.9 collective-permute-start.27
  145.2 13.4 %all-gather.22.cloned.1.call-done.refs_3_ = bf16[176,128,128]{2,1,0:T(8,128)(2,1)} async-done(((bf16[22,128,128]{2,1,0:T(8,128)(2,1)}), bf16[176,128,128]{2,1,0:T(8,128)(2,1)}) %all-gather.22.cloned.1.call-update) | async-done | bytes 5767184 | tf_op jit(solution)/shard_map/cond/branch_1_fun/all_gather | solution.py:556
  158.6 18.2 %square_group.17 = (bf16[4,64,128,128]{3,2,1,0:T(8,128)(2,1)}, f32[1024,512]{1,0:T(8,128)}, bf16[1024,512]{1,0:T(8,128)(2,1)}) custom-call(s32[8,128]{1,0:T(8,128)} %select_reduce_fusion.2.lists_ref, s32[8,17]{1,0:T(8,128)} %copy.46.counts_ref, s32[2]{0:T(128)S(1)} %get-tuple-element.84.place_ref.refs_18_.refs_20_.refs_19_, ...), custom_call_target="tpu_custom_call" | custom-call | flops 1 | bytes 1 | tf_op jit(solution)/shard_map/cond/branch_1_fun/square_group/pallas_call | solution.py:335
  176.8 1.4 collective-permute-start.32
  178.3 1.5 collective-permute-start.31
  179.7 1.0 copy-done.1
  180.7 1.0 copy-done.3
  181.7 2.2 split.9
  183.9 0.6 collective-permute-start.29
  184.5 0.7 collective-permute-start.30
  185.2 17.9 %collective-permute-done.32.y_ref.refs_7_ = bf16[1024,512]{1,0:T(8,128)(2,1)S(1)} collective-permute-done((bf16[1024,512]{1,0:T(8,128)(2,1)}, bf16[1024,512]{1,0:T(8,128)(2,1)S(1)}, u32[]{:S(2)}, u32[]{:S(2)}) %collective-permute-start.32) | collective-permute-done | bytes 1048608 | tf_op jit(solution)/shard_map/cond/branch_1_fun/ppermute | solution.py:553
  203.1 1.5 collective-permute-done.31.x_ref.refs_6_
  204.6 2.2 split.10
  206.8 1.5 collective-permute-start.34
  208.3 0.9 collective-permute-start.33
  209.3 5.7 %all-gather.24.cloned.1.call-done.refs_4_ = bf16[160,128,128]{2,1,0:T(8,128)(2,1)} async-done(((bf16[20,128,128]{2,1,0:T(8,128)(2,1)}), bf16[160,128,128]{2,1,0:T(8,128)(2,1)}) %all-gather.24.cloned.1.call-update) | async-done | bytes 5242896 | tf_op jit(solution)/shard_map/cond/branch_1_fun/all_gather | solution.py:556
  215.0 18.1 %square_group.18 = (bf16[4,64,128,128]{3,2,1,0:T(8,128)(2,1)}, f32[1024,512]{1,0:T(8,128)}, bf16[1024,512]{1,0:T(8,128)(2,1)}) custom-call(s32[8,128]{1,0:T(8,128)} %select_reduce_fusion.2.lists_ref, s32[8,17]{1,0:T(8,128)} %copy.46.counts_ref, s32[2]{0:T(128)S(1)} %get-tuple-element.84.place_ref.refs_18_.refs_20_.refs_19_, ...), custom_call_target="tpu_custom_call" | custom-call | flops 1 | bytes 1 | tf_op jit(solution)/shard_map/cond/branch_1_fun/square_group/pallas_call | solution.py:335
  233.1 2.5 collective-permute-start.39
  235.6 0.6 collective-permute-start.38
  236.2 0.5 collective-permute-start.37
  236.7 0.2 copy-done.26
  237.0 0.5 copy-done.28
  237.5 0.2 copy-done.30
  237.7 17.1 %cube_part.15 = (f32[1024,512]{1,0:T(8,128)}, f32[1024,512]{1,0:T(8,128)}) custom-call(bf16[1024,512]{1,0:T(8,128)(2,1)} %get-tuple-element.90.refs_0_, bf16[1024,512]{1,0:T(8,128)(2,1)} %copy-done.3, bf16[1024,512]{1,0:T(8,128)(2,1)} %copy-done.1, bf16[512,512]{1,0:T(8,128)(2,1)} %copy-done.24, bf16[512,512]{1,0:T(8,128)(2,1)} %copy-done.26, ...), custom_call_target="tpu_custom_call" | custom-call | flops 1 | bytes 1 | tf_op jit(solution)/shard_map/cond/branch_1_fun/cube_part/pallas_call | solution.py:523
  254.9 3.0 all-gather.26.cloned.1.call-done.refs_5_
  257.9 18.4 %square_group.19 = (bf16[4,64,128,128]{3,2,1,0:T(8,128)(2,1)}, f32[1024,512]{1,0:T(8,128)}, bf16[1024,512]{1,0:T(8,128)(2,1)}) custom-call(s32[8,128]{1,0:T(8,128)} %select_reduce_fusion.2.lists_ref, s32[8,17]{1,0:T(8,128)} %copy.46.counts_ref, s32[2]{0:T(128)S(1)} %get-tuple-element.84.place_ref.refs_18_.refs_20_.refs_19_, ...), custom_call_target="tpu_custom_call" | custom-call | flops 1 | bytes 1 | tf_op jit(solution)/shard_map/cond/branch_1_fun/square_group/pallas_call | solution.py:335
  276.3 1.5 collective-permute-start.36
  277.8 1.4 collective-permute-start.35
  279.2 16.1 %cube_part.16 = (f32[1024,512]{1,0:T(8,128)}, f32[1024,512]{1,0:T(8,128)}) custom-call(bf16[1024,512]{1,0:T(8,128)(2,1)} %get-tuple-element.90.refs_0_, bf16[1024,512]{1,0:T(8,128)(2,1)} %copy-done.3, bf16[1024,512]{1,0:T(8,128)(2,1)} %copy-done.1, bf16[512,512]{1,0:T(8,128)(2,1)} %copy-done.24, bf16[512,512]{1,0:T(8,128)(2,1)} %copy-done.26, ...), custom_call_target="tpu_custom_call" | custom-call | flops 1 | bytes 1 | tf_op jit(solution)/shard_map/cond/branch_1_fun/cube_part/pallas_call | solution.py:523
  295.4 17.0 %cube_part.17 = (f32[1024,512]{1,0:T(8,128)}, f32[1024,512]{1,0:T(8,128)}, f32[1024,512]{1,0:T(8,128)}, f32[1024,512]{1,0:T(8,128)}) custom-call(bf16[1024,512]{1,0:T(8,128)(2,1)} %get-tuple-element.106.refs_0_, bf16[1024,512]{1,0:T(8,128)(2,1)} %collective-permute-done.37.refs_1_, bf16[1024,512]{1,0:T(8,128)(2,1)} %collective-permute-done.38.refs_2_, ...), custom_call_target="tpu_custom_call" | custom-call | flops 1 | bytes 1 | tf_op jit(solution)/shard_map/cond/branch_1_fun/cube_part/pallas_call | solution.py:523
  312.5 0.9 copy-done.13
  313.4 0.4 copy-done.15
  313.8 2.2 split.11
  316.0 0.5 collective-permute-start.40
  316.5 0.7 collective-permute-start.41
  317.2 15.2 %cube_part.18 = (f32[1024,512]{1,0:T(8,128)}, f32[1024,512]{1,0:T(8,128)}, f32[1024,512]{1,0:T(8,128)}, f32[1024,512]{1,0:T(8,128)}) custom-call(bf16[1024,512]{1,0:T(8,128)(2,1)} %get-tuple-element.105.refs_0_, bf16[1024,512]{1,0:T(8,128)(2,1)} %copy-done.15, bf16[1024,512]{1,0:T(8,128)(2,1)} %copy-done.13, ...), custom_call_target="tpu_custom_call" | custom-call | flops 1 | bytes 1 | tf_op jit(solution)/shard_map/cond/branch_1_fun/cube_part/pallas_call | solution.py:523
  332.4 0.8 copy-done.36
  333.4 10.4 %cube_part.19 = f32[1024,2048]{1,0:T(8,128)} custom-call(bf16[512,512]{1,0:T(8,128)(2,1)} %copy-done.36, bf16[512,512]{1,0:T(8,128)(2,1)} %copy-done.38, bf16[4,48,128,128]{3,2,1,0:T(8,128)(2,1)} %get-tuple-element.96.refs_10_.refs_11_.refs_12_.refs_4_.refs_5_.refs_6_.refs_3_.refs_2_, ...), custom_call_target="tpu_custom_call" | custom-call | flops 1 | bytes 1 | tf_op jit(solution)/shard_map/cond/branch_1_fun/cube_part/pallas_call | solution.py:523
  (63 shorter events, 1.2 us)
Async XLA Ops:
  15.7 10.6 %copy-start.21 = (s32[64,64]{1,0:T(8,128)}, s32[64,64]{1,0:T(8,128)S(1)}, u32[]{:S(2)}) copy-start(s32[64,64]{1,0:T(8,128)S(1)} %get-tuple-element.82.table_ref) | copy-start | bytes 49156 | tf_op jit(solution)/shard_map/cond
  15.7 90.1 %all-gather.20.cloned.1.call-start = ((), (), s32[]{:S(2)}) async-start(), calls=%async_computation.4 | async-start | bytes 8257536 | tf_op jit(solution)/shard_map/cond/branch_1_fun/all_gather | solution.py:556
  21.6 136.9 %all-gather.22.cloned.1.call-start = ((), (), s32[]{:S(2)}) async-start(), calls=%async_computation.5 | async-start | bytes 6488064 | tf_op jit(solution)/shard_map/cond/branch_1_fun/all_gather | solution.py:556
  21.7 34.4 %collective-permute-start.23 = (bf16[42,128,128]{2,1,0:T(8,128)(2,1)}, bf16[42,128,128]{2,1,0:T(8,128)(2,1)S(1)}, u32[]{:S(2)}, u32[]{:S(2)}) collective-permute-start(bf16[42,128,128]{2,1,0:T(8,128)(2,1)} %get-tuple-element.86.h0), channel_id=1, source_target_pairs={{0,16},{8,24},{16,0},{24,8},{1,17},{9,25},{17,1},{25,9},{2,18},{10... | collective-permute-start | bytes 4128776 | tf_op jit(solution)/shard_map/cond/branch_1_fun/ppermute | solution.py:553
  24.8 33.3 %collective-permute-start.21 = (bf16[42,128,128]{2,1,0:T(8,128)(2,1)}, bf16[42,128,128]{2,1,0:T(8,128)(2,1)S(1)}, u32[]{:S(2)}, u32[]{:S(2)}) collective-permute-start(bf16[42,128,128]{2,1,0:T(8,128)(2,1)} %get-tuple-element.86.h0), channel_id=1, source_target_pairs={{0,8},{8,0},{16,24},{24,16},{1,9},{9,1},{17,25},{25,17},{2,10},{10... | collective-permute-start | bytes 4128776 | tf_op jit(solution)/shard_map/cond/branch_1_fun/ppermute | solution.py:553
  26.3 64.9 %copy-start.22 = (s32[64,64]{1,0:T(8,128)S(1)}, s32[64,64]{1,0:T(8,128)}, u32[]{:S(2)}) copy-start(s32[64,64]{1,0:T(8,128)} %copy-done.21) | copy-start | bytes 49156 | tf_op jit(solution)/shard_map/cond
  26.3 58.4 %collective-permute-start.24 = (bf16[42,128,128]{2,1,0:T(8,128)(2,1)}, bf16[42,128,128]{2,1,0:T(8,128)(2,1)S(1)}, u32[]{:S(2)}, u32[]{:S(2)}) collective-permute-start(bf16[42,128,128]{2,1,0:T(8,128)(2,1)} %get-tuple-element.87.h1), channel_id=1, source_target_pairs={{0,16},{8,24},{16,0},{24,8},{1,17},{9,25},{17,1},{25,9},{2,18},{10... | collective-permute-start | bytes 4128776 | tf_op jit(solution)/shard_map/cond/branch_1_fun/ppermute | solution.py:553
  26.8 59.5 %collective-permute-start.22 = (bf16[42,128,128]{2,1,0:T(8,128)(2,1)}, bf16[42,128,128]{2,1,0:T(8,128)(2,1)}, u32[]{:S(2)}, u32[]{:S(2)}) collective-permute-start(bf16[42,128,128]{2,1,0:T(8,128)(2,1)} %get-tuple-element.87.h1), channel_id=1, source_target_pairs={{0,8},{8,0},{16,24},{24,16},{1,9},{9,1},{17,25},{25,17},{2,10},{10... | collective-permute-start | bytes 4128776 | tf_op jit(solution)/shard_map/cond/branch_1_fun/ppermute | solution.py:553
  56.0 28.7 %copy-start.8 = (bf16[42,128,128]{2,1,0:T(8,128)(2,1)}, bf16[42,128,128]{2,1,0:T(8,128)(2,1)S(1)}, u32[]{:S(2)}) copy-start(bf16[42,128,128]{2,1,0:T(8,128)(2,1)S(1)} %collective-permute-done.23.refs_2_) | copy-start | bytes 4128772 | tf_op jit(solution)/shard_map/cond
  58.1 28.1 %copy-start.6 = (bf16[42,128,128]{2,1,0:T(8,128)(2,1)}, bf16[42,128,128]{2,1,0:T(8,128)(2,1)S(1)}, u32[]{:S(2)}) copy-start(bf16[42,128,128]{2,1,0:T(8,128)(2,1)S(1)} %collective-permute-done.21.refs_0_) | copy-start | bytes 4128772 | tf_op jit(solution)/shard_map/cond
  84.7 1.6 copy-start.7
  88.3 126.7 %all-gather.24.cloned.1.call-start = ((), (), s32[]{:S(2)}) async-start(), calls=%async_computation.6 | async-start | bytes 5898240 | tf_op jit(solution)/shard_map/cond/branch_1_fun/all_gather | solution.py:556
  88.3 32.2 %collective-permute-start.25 = (bf16[42,128,128]{2,1,0:T(8,128)(2,1)}, bf16[42,128,128]{2,1,0:T(8,128)(2,1)S(1)}, u32[]{:S(2)}, u32[]{:S(2)}) collective-permute-start(bf16[42,128,128]{2,1,0:T(8,128)(2,1)} %copy-done.6), channel_id=1, source_target_pairs={{0,16},{8,24},{16,0},{24,8},{1,17},{9,25},{17,1},{25,9},{2,18},{10... | collective-permute-start | bytes 4128776 | tf_op jit(solution)/shard_map/cond/branch_1_fun/ppermute | solution.py:553
  89.6 31.1 %collective-permute-start.26 = (bf16[42,128,128]{2,1,0:T(8,128)(2,1)}, bf16[42,128,128]{2,1,0:T(8,128)(2,1)S(1)}, u32[]{:S(2)}, u32[]{:S(2)}) collective-permute-start(bf16[42,128,128]{2,1,0:T(8,128)(2,1)} %copy-done.7), channel_id=1, source_target_pairs={{0,8},{8,0},{16,24},{24,16},{1,9},{9,1},{17,25},{25,17},{2,10},{10... | collective-permute-start | bytes 4128776 | tf_op jit(solution)/shard_map/cond/branch_1_fun/ppermute | solution.py:553
  120.5 1.1 copy-start.31
  120.7 1.4 copy-start.32
  133.2 124.7 %all-gather.26.cloned.1.call-start = ((), (), s32[]{:S(2)}) async-start(), calls=%async_computation.7 | async-start | bytes 4128768 | tf_op jit(solution)/shard_map/cond/branch_1_fun/all_gather | solution.py:556
  143.1 36.6 %collective-permute-start.28 = (bf16[1024,512]{1,0:T(8,128)(2,1)}, bf16[1024,512]{1,0:T(8,128)(2,1)S(1)}, u32[]{:S(2)}, u32[]{:S(2)}) collective-permute-start(bf16[1024,512]{1,0:T(8,128)(2,1)} %get-tuple-element.90.refs_0_), channel_id=1, source_target_pairs={{0,16},{8,24},{16,0},{24,8},{1,17},{9,25},{17,1},{25,9},{2,18},{10... | collective-permute-start | bytes 3145736 | tf_op jit(solution)/shard_map/cond/branch_1_fun/ppermute | solution.py:553
  144.3 35.5 %collective-permute-start.27 = (bf16[1024,512]{1,0:T(8,128)(2,1)}, bf16[1024,512]{1,0:T(8,128)(2,1)S(1)}, u32[]{:S(2)}, u32[]{:S(2)}) collective-permute-start(bf16[1024,512]{1,0:T(8,128)(2,1)} %get-tuple-element.90.refs_0_), channel_id=1, source_target_pairs={{0,8},{8,0},{16,24},{24,16},{1,9},{9,1},{17,25},{25,17},{2,10},{10... | collective-permute-start | bytes 3145736 | tf_op jit(solution)/shard_map/cond/branch_1_fun/ppermute | solution.py:553
  176.8 26.3 %collective-permute-start.32 = (bf16[1024,512]{1,0:T(8,128)(2,1)}, bf16[1024,512]{1,0:T(8,128)(2,1)S(1)}, u32[]{:S(2)}, u32[]{:S(2)}) collective-permute-start(bf16[1024,512]{1,0:T(8,128)(2,1)} %get-tuple-element.93.refs_5_), channel_id=1, source_target_pairs={{0,16},{8,24},{16,0},{24,8},{1,17},{9,25},{17,1},{25,9},{2,18},{10... | collective-permute-start | bytes 3145736 | tf_op jit(solution)/shard_map/cond/branch_1_fun/ppermute | solution.py:553
  178.3 26.3 %collective-permute-start.31 = (bf16[1024,512]{1,0:T(8,128)(2,1)}, bf16[1024,512]{1,0:T(8,128)(2,1)}, u32[]{:S(2)}, u32[]{:S(2)}) collective-permute-start(bf16[1024,512]{1,0:T(8,128)(2,1)} %get-tuple-element.93.refs_5_), channel_id=1, source_target_pairs={{0,8},{8,0},{16,24},{24,16},{1,9},{9,1},{17,25},{25,17},{2,10},{10... | collective-permute-start | bytes 3145736 | tf_op jit(solution)/shard_map/cond/branch_1_fun/ppermute | solution.py:553
  179.7 1.0 copy-start.1
  180.7 1.0 copy-start.3
  183.9 51.7 %collective-permute-start.29 = (bf16[512,512]{1,0:T(8,128)(2,1)}, bf16[512,512]{1,0:T(8,128)(2,1)S(1)}, u32[]{:S(2)}, u32[]{:S(2)}) collective-permute-start(bf16[512,512]{1,0:T(8,128)(2,1)} %get-tuple-element.91), channel_id=1, source_target_pairs={{0,16},{8,24},{16,0},{24,8},{1,17},{9,25},{17,1},{25,9},{2,18},{10... | collective-permute-start | bytes 1572872 | tf_op jit(solution)/shard_map/cond/branch_1_fun/ppermute | solution.py:553
  184.5 51.7 %collective-permute-start.30 = (bf16[512,512]{1,0:T(8,128)(2,1)}, bf16[512,512]{1,0:T(8,128)(2,1)S(1)}, u32[]{:S(2)}, u32[]{:S(2)}) collective-permute-start(bf16[512,512]{1,0:T(8,128)(2,1)} %get-tuple-element.92), channel_id=1, source_target_pairs={{0,8},{8,0},{16,24},{24,16},{1,9},{9,1},{17,25},{25,17},{2,10},{10... | collective-permute-start | bytes 1572872 | tf_op jit(solution)/shard_map/cond/branch_1_fun/ppermute | solution.py:553
  203.1 1.5 copy-start.5
  206.8 29.9 %collective-permute-start.34 = (bf16[512,512]{1,0:T(8,128)(2,1)}, bf16[512,512]{1,0:T(8,128)(2,1)S(1)}, u32[]{:S(2)}, u32[]{:S(2)}) collective-permute-start(bf16[512,512]{1,0:T(8,128)(2,1)} %get-tuple-element.95), channel_id=1, source_target_pairs={{0,8},{8,0},{16,24},{24,16},{1,9},{9,1},{17,25},{25,17},{2,10},{10... | collective-permute-start | bytes 1572872 | tf_op jit(solution)/shard_map/cond/branch_1_fun/ppermute | solution.py:553
  208.3 29.4 %copy-start.17 = (s32[64,64]{1,0:T(8,128)S(1)}, s32[64,64]{1,0:T(8,128)}, u32[]{:S(2)}) copy-start(s32[64,64]{1,0:T(8,128)} %get-tuple-element.99.refs_19_.refs_21_.refs_20_) | copy-start | bytes 49156 | tf_op jit(solution)/shard_map/cond
  208.3 29.4 %copy-start.20 = (s32[64,64]{1,0:T(8,128)S(1)}, s32[64,64]{1,0:T(8,128)}, u32[]{:S(2)}) copy-start(s32[64,64]{1,0:T(8,128)} %get-tuple-element.100.refs_20_.refs_22_.refs_21_) | copy-start | bytes 49156 | tf_op jit(solution)/shard_map/cond
  208.3 28.4 %collective-permute-start.33 = (bf16[512,512]{1,0:T(8,128)(2,1)}, bf16[512,512]{1,0:T(8,128)(2,1)S(1)}, u32[]{:S(2)}, u32[]{:S(2)}) collective-permute-start(bf16[512,512]{1,0:T(8,128)(2,1)} %get-tuple-element.94.refs_5_), channel_id=1, source_target_pairs={{0,16},{8,24},{16,0},{24,8},{1,17},{9,25},{17,1},{25,9},{2,18},{10... | collective-permute-start | bytes 1572872 | tf_op jit(solution)/shard_map/cond/branch_1_fun/ppermute | solution.py:553
  233.1 62.2 %collective-permute-start.39 = (bf16[1024,512]{1,0:T(8,128)(2,1)}, bf16[1024,512]{1,0:T(8,128)(2,1)}, u32[]{:S(2)}, u32[]{:S(2)}) collective-permute-start(bf16[1024,512]{1,0:T(8,128)(2,1)} %get-tuple-element.106.refs_0_), channel_id=1, source_target_pairs={{0,24},{8,16},{16,8},{24,0},{1,25},{9,17},{17,9},{25,1},{2,26},{10... | collective-permute-start | bytes 3145736 | tf_op jit(solution)/shard_map/cond/branch_1_fun/ppermute | solution.py:553
  235.6 1.1 copy-start.24
  235.6 59.8 %collective-permute-start.38 = (bf16[1024,512]{1,0:T(8,128)(2,1)}, bf16[1024,512]{1,0:T(8,128)(2,1)}, u32[]{:S(2)}, u32[]{:S(2)}) collective-permute-start(bf16[1024,512]{1,0:T(8,128)(2,1)} %get-tuple-element.106.refs_0_), channel_id=1, source_target_pairs={{0,16},{8,24},{16,0},{24,8},{1,17},{9,25},{17,1},{25,9},{2,18},{10... | collective-permute-start | bytes 3145736 | tf_op jit(solution)/shard_map/cond/branch_1_fun/ppermute | solution.py:553
  236.2 0.8 copy-start.26
  236.2 59.2 %collective-permute-start.37 = (bf16[1024,512]{1,0:T(8,128)(2,1)}, bf16[1024,512]{1,0:T(8,128)(2,1)}, u32[]{:S(2)}, u32[]{:S(2)}) collective-permute-start(bf16[1024,512]{1,0:T(8,128)(2,1)} %get-tuple-element.106.refs_0_), channel_id=1, source_target_pairs={{0,8},{8,0},{16,24},{24,16},{1,9},{9,1},{17,25},{25,17},{2,10},{10... | collective-permute-start | bytes 3145736 | tf_op jit(solution)/shard_map/cond/branch_1_fun/ppermute | solution.py:553
  236.7 0.8 copy-start.28
  236.7 1.0 copy-start.30
  276.3 36.2 %collective-permute-start.36 = (bf16[1024,512]{1,0:T(8,128)(2,1)}, bf16[1024,512]{1,0:T(8,128)(2,1)S(1)}, u32[]{:S(2)}, u32[]{:S(2)}) collective-permute-start(bf16[1024,512]{1,0:T(8,128)(2,1)} %get-tuple-element.105.refs_0_), channel_id=1, source_target_pairs={{0,16},{8,24},{16,0},{24,8},{1,17},{9,25},{17,1},{25,9},{2,18},{10... | collective-permute-start | bytes 3145736 | tf_op jit(solution)/shard_map/cond/branch_1_fun/ppermute | solution.py:553
  277.8 34.7 %collective-permute-start.35 = (bf16[1024,512]{1,0:T(8,128)(2,1)}, bf16[1024,512]{1,0:T(8,128)(2,1)S(1)}, u32[]{:S(2)}, u32[]{:S(2)}) collective-permute-start(bf16[1024,512]{1,0:T(8,128)(2,1)} %get-tuple-element.105.refs_0_), channel_id=1, source_target_pairs={{0,8},{8,0},{16,24},{24,16},{1,9},{9,1},{17,25},{25,17},{2,10},{10... | collective-permute-start | bytes 3145736 | tf_op jit(solution)/shard_map/cond/branch_1_fun/ppermute | solution.py:553
  312.5 1.0 copy-start.13
  312.5 1.3 copy-start.15
  316.0 16.4 %collective-permute-start.40 = (bf16[512,512]{1,0:T(8,128)(2,1)}, bf16[512,512]{1,0:T(8,128)(2,1)S(1)}, u32[]{:S(2)}, u32[]{:S(2)}) collective-permute-start(bf16[512,512]{1,0:T(8,128)(2,1)} %get-tuple-element.114), channel_id=1, source_target_pairs={{0,16},{8,24},{16,0},{24,8},{1,17},{9,25},{17,1},{25,9},{2,18},{10... | collective-permute-start | bytes 1572872 | tf_op jit(solution)/shard_map/cond/branch_1_fun/ppermute | solution.py:553
  316.5 15.9 %collective-permute-start.41 = (bf16[512,512]{1,0:T(8,128)(2,1)}, bf16[512,512]{1,0:T(8,128)(2,1)S(1)}, u32[]{:S(2)}, u32[]{:S(2)}) collective-permute-start(bf16[512,512]{1,0:T(8,128)(2,1)} %get-tuple-element.115), channel_id=1, source_target_pairs={{0,8},{8,0},{16,24},{24,16},{1,9},{9,1},{17,25},{25,17},{2,10},{10... | collective-permute-start | bytes 1572872 | tf_op jit(solution)/shard_map/cond/branch_1_fun/ppermute | solution.py:553
  332.4 0.8 copy-start.36
  332.4 1.0 copy-start.38
Sparse Core Ops, SparseCore 0:
  21.8 76.0 all-gather.19
  99.5 59.0 all-gather.21
  160.2 54.7 all-gather.23
  216.5 41.3 all-gather.25

commit v4 on v3

--- a/solution.py
+++ b/solution.py
@@ -121,20 +121,20 @@
         pltpu.make_async_copy(out, out, sems.at[q]).wait()
 
 
-def pack(table, place, density, spans):
+def pack(table, place, density, spans, after=()):
     shape = density.shape[0] // TILE, density.shape[1] // TILE
 
     def kernel(table_ref, place_ref, x_ref, *refs):
-        send_kept(table_ref, place_ref, x_ref, refs[:-1], refs[-1], spans, shape)
+        send_kept(table_ref, place_ref, x_ref, refs[len(after) : -1], refs[-1], spans, shape)
 
     return pl.pallas_call(
         kernel,
         out_shape=[jax.ShapeDtypeStruct((hi - lo, TILE, TILE), density.dtype) for lo, hi in spans],
-        in_specs=[SMEM, SMEM, VMEM],
+        in_specs=[SMEM, SMEM, VMEM] + [ANY] * len(after),
         out_specs=[ANY] * len(spans),
         scratch_shapes=[pltpu.SemaphoreType.DMA((len(spans),))],
         name="pack",
-    )(table, place, density)
+    )(table, place, density, *after)
 
 
 def stage(halves, lo, hi, after):
@@ -357,7 +357,7 @@
 
 
 def cube_part(strips, panels, jobs, widths, before, keep=None, squares=None, base=None, joined=False, after=()):
-    groups = sorted({g for job in jobs.values() for g in job})
+    groups = sorted({g for job in jobs.values() for g, _ in job})
     firsts = [sum(widths[:h]) for h in range(len(widths))]
     tile_cols = sum(widths)
     span = tile_cols * TILE
@@ -365,11 +365,10 @@
     tile_rows = nrows // TILE
     lefts, start = [], {}
     at = 0
-    for group in groups:
-        g, ks = group
-        start[group] = at
-        for k in ks:
-            lefts += [(x, row, at, group) for x, row in strips[g][k]]
+    for g in groups:
+        for k in range(ROW_GROUP):
+            start[g, k] = at
+            lefts += [(x, row, at, (g, k)) for x, row in strips[g][k]]
             at += widths[g] * TILE
     total = at
     hs = list(jobs)
@@ -407,13 +406,12 @@
         outs = take(len(out_shape))
         left, right, acc, held, left_sems, right_sems, acc_sems, held_sems, out_sems = refs
 
-        def left_copies(g):
+        def left_copies(g, k):
+            sem = left_sems.at[groups.index(g) * ROW_GROUP + k]
             return [
-                pltpu.make_async_copy(
-                    ref, left.at[pl.ds(row, x.shape[0]), pl.ds(at, x.shape[1])], left_sems.at[groups.index(g)]
-                )
-                for ref, (x, row, at, group) in zip(left_refs, lefts)
-                if group == g
+                pltpu.make_async_copy(ref, left.at[pl.ds(row, x.shape[0]), pl.ds(at, x.shape[1])], sem)
+                for ref, (x, row, at, spot) in zip(left_refs, lefts)
+                if spot == (g, k)
             ]
 
         def right_copies(n, at, group):
@@ -453,16 +451,19 @@
             return found
 
         def loads(n):
-            copies = []
-            for m, (at, g) in enumerate(steps(hs[n])):
+            copies, begun = [], set()
+            for m, (at, group) in enumerate(steps(hs[n])):
                 if n == 0:
-                    copies += left_copies(g)
-                copies += right_copies(n, at, g)
+                    g, ks = group
+                    copies += [copy for k in ks for copy in left_copies(g, k)]
+                    begun |= {(g, k) for k in ks}
+                copies += right_copies(n, at, group)
                 if m == 0:
                     copies += acc_copies(n)
+            copies += held_copies(n)
             if n == 0:
-                copies += [copy for g in groups if g not in jobs[hs[0]] for copy in left_copies(g)]
-            return copies + held_copies(n)
+                copies += [copy for spot in start if spot not in begun for copy in left_copies(*spot)]
+            return copies
 
         def store(n):
             h, t = hs[n], n % 3
@@ -486,9 +487,9 @@
                 copy.wait()
             found = steps(h)
             for m, (at, g) in enumerate(found):
-                if g not in arrived:
-                    arrived.add(g)
-                    for copy in left_copies(g):
+                for spot in [(g[0], k) for k in g[1] if (g[0], k) not in arrived]:
+                    arrived.add(spot)
+                    for copy in left_copies(*spot):
                         copy.wait()
                 for copy in right_copies(n, at, g):
                     copy.wait()
@@ -500,7 +501,7 @@
                 other = jnp.concatenate(
                     [right[s, j, at : at + depth].reshape(depth * TILE, TILE) for j in range(widths[h])], 1
                 )
-                lanes = slice(start[g], start[g] + depth * TILE)
+                lanes = slice(start[g[0], g[1][0]], start[g[0], g[1][0]] + depth * TILE)
                 part = jnp.dot(left[:, lanes], other, preferred_element_type=jnp.float32)
                 if m > 0 or h in before_refs:
                     part += acc[t, :, :wide]
@@ -530,7 +531,7 @@
             pltpu.VMEM((2, widest, deepest, TILE, TILE), jnp.bfloat16),
             pltpu.VMEM((3, nrows, widest * TILE), jnp.float32),
             pltpu.VMEM((3, nrows, widest * TILE) if keep is not None else (3, 8, TILE), jnp.float32),
-            pltpu.SemaphoreType.DMA((len(groups),)),
+            pltpu.SemaphoreType.DMA((ROW_GROUP * len(groups),)),
             pltpu.SemaphoreType.DMA((2, max(len(job) for job in jobs.values()))),
             pltpu.SemaphoreType.DMA((3,)),
             pltpu.SemaphoreType.DMA((3,)),
@@ -547,7 +548,8 @@
     shape = nrows // TILE, ncols // TILE
     widths = WIDTHS
     cap = spans[-1][1]
-    *halves, first_chunk = pack(table, place, density, [(0, cap // 2), (cap // 2, cap), spans[0]])
+    first_chunk, = pack(table, place, density, [spans[0]])
+    halves = pack(table, place, density, [(0, cap // 2), (cap // 2, cap)], [first_chunk])
 
     def swap(x, k):
         return lax.ppermute(x, "row", [(i, i ^ k) for i in range(ROW_GROUP)])
@@ -600,6 +602,9 @@
     keep = place, pattern_square, pattern_cube
 
     def add(jobs, base=None, joined=False, after=()):
+        h = next(iter(jobs))
+        (g, ks), *more = jobs[h]
+        jobs = {**jobs, h: [(g, ks[:2]), (g, ks[2:]), *more]}
         return dict(zip(jobs, cube_part(
             strips, panels, jobs, widths, {}, keep, squares if base is None else None, base, joined, after
         )))
@@ -607,10 +612,10 @@
     parts = add({0: [first, second], 1: [first, second]}, after=[squares[2]])
     next_group(3, False, [parts[0]])
     parts.update(add({2: [first, second], 3: [first, second]}))
-    parts = add({h: [third] for h in range(4)}, parts)
-    forward(3, [parts[0]])
-    parts = add({h: [(3, every[:3])] for h in range(4)}, parts)
-    return add({h: [(3, every[3:])] for h in range(4)}, parts, True)[0]
+    parts.update(add({0: [third], 1: [third]}, parts, after=[parts[2]]))
+    sent = forward(3, [parts[0]])
+    parts.update(add({2: [third], 3: [third]}, parts, after=[sent]))
+    return add({h: [(3, every)] for h in range(4)}, parts, True)[0]
 
 
 def local(density, pattern_p, pattern_square, pattern_cube):

time: 354 us -> 342 us (0.966); the launches traced: 357 us -> 336 us
  waiting for transfers between devices: 101 us -> 83.1 us
    all_gather x4, waiting for transfers between devices: 22.2 us -> 7.78 us  [gather(): return lax.all_gather(x, 'col', axis=0, tiled=True)]
    pallas_call x1 -> x2, Pallas kernels: 5.83 us -> 9.83 us  [pack(): pl.pallas_call(kernel, out_shape=[jax.ShapeDtypeStruct((hi - lo, TILE, TI...]
    pallas_call x5, Pallas kernels: 75.9 us -> 72 us  [cube_part(): pl.pallas_call(kernel, out_shape=out_shape, in_specs=specs, out_specs=[AN...]
    ppermute x21, waiting for transfers between devices: 79 us -> 75.3 us  [swap(): return lax.ppermute(x, 'row', [(i, i ^ k) for i in range(ROW_GROUP)])]
  transfers between devices with their start and end apart: 25 -> 25, of which waited for: 10 -> 12; matrix products, arithmetic and copies ran while one was open for 1% -> 1% of each run, Pallas kernels for 49% -> 51%
where the time goes in v4:
time: 342 us; the launch traced here: 336 us
  Pallas kernels  193 us (56%)
  waiting for transfers between devices  83.1 us (24%)
  starting transfers between devices  24.4 us (7%)
  between operations  14.9 us (4%)
  loops' own time  10.3 us (3%)
  local copies, waits for them, and re-layouts  6.81 us (2%)
    pallas_call x5, Pallas kernels, square_group(): pl.pallas_call(kernel, out_shape=[jax.ShapeDtypeStruct((width, count * ti...  77.5 us
    ppermute x21, waiting for transfers between devices, swap(): return lax.ppermute(x, 'row', [(i, i ^ k) for i in range(ROW_GROUP)])  75.3 us
    pallas_call x5, Pallas kernels, cube_part(): pl.pallas_call(kernel, out_shape=out_shape, in_specs=specs, out_specs=[AN...  72 us
    ppermute x21, starting transfers between devices, swap(): return lax.ppermute(x, 'row', [(i, i ^ k) for i in range(ROW_GROUP)])  24.2 us
    pallas_call x2, Pallas kernels, row_unpack(): pl.pallas_call(kernel, grid=(tile_rows,), out_shape=jax.ShapeDtypeStruct(...  21.2 us
    another operation x1, loops' own time, local(): return lax.switch(level, ways)  10.3 us
    pallas_call x2, Pallas kernels, pack(): pl.pallas_call(kernel, out_shape=[jax.ShapeDtypeStruct((hi - lo, TILE, TI...  9.83 us
    all_gather x4, waiting for transfers between devices, gather(): return lax.all_gather(x, 'col', axis=0, tiled=True)  7.78 us
  transfers between devices with their start and end apart: 25, of which 12 were waited for; matrix products, arithmetic and copies ran while one was open for 1% of the time, Pallas kernels for 51%

profile of v4, /device:TPU:0, one launch (start us, length us, event | category | flops | bytes accessed | tf_op | source)
XLA Modules:
  0.0 336.4 jit_solution(13799042616865144553)
XLA Ops:
  6.6 0.9 fusion.7
  7.5 1.8 compare_reduce_fusion
  10.5 318.7 %conditional.1 = (f32[1024,2048]{1,0:T(8,128)}) conditional(s32[]{:T(128)} %clamp.3, (s32[]{:T(128)}, s32[64,64]{1,0:T(8,128)S(1)}, s32[2]{0:T(128)S(1)}, bf16[1024,2048]{1,0:T(8,128)(2,1)}, s32[64,64]{1,0:T(8,128)}, /*index=5*/s32[64,64]{1,0:T(8,128)}) %tuple.14, (s32[]{:T(128)}, s32[64,64]{1,0:T(8,128)S(1)}, s32[2]{0:T(128)S(1)}, ...), branch_computations={%region_2.5_spmd, %region_5.8_spmd, %region_8.9_spmd} | conditional | flops 68740448256 | bytes 515693568 | solution.py:639
  10.6 4.3 %pack.4.refs_0_ = bf16[26,128,128]{2,1,0:T(8,128)(2,1)} custom-call(s32[64,64]{1,0:T(8,128)S(1)} %get-tuple-element.40.table_ref, s32[2]{0:T(128)S(1)} %get-tuple-element.43.place_ref.refs_18_.refs_12_.refs_21_, bf16[1024,2048]{1,0:T(8,128)(2,1)} %get-tuple-element.44.x_ref), custom_call_target="tpu_custom_call" | custom-call | tf_op jit(solution)/shard_map/cond/branch_0_fun/pack/pallas_call | solution.py:130
  15.0 5.5 %pack.5 = (bf16[38,128,128]{2,1,0:T(8,128)(2,1)}, bf16[38,128,128]{2,1,0:T(8,128)(2,1)}) custom-call(s32[64,64]{1,0:T(8,128)S(1)} %get-tuple-element.40.table_ref, s32[2]{0:T(128)S(1)} %get-tuple-element.43.place_ref.refs_18_.refs_12_.refs_21_, bf16[1024,2048]{1,0:T(8,128)(2,1)} %get-tuple-element.44.x_ref, bf16[26,128,128]{2,1,0:T(8,128)(2,1)} %pack.4.refs_0_), custom_call_target="tpu_custom_call" | custom-call | tf_op jit(solution)/shard_map/cond/branch_0_fun/pack/pallas_call | solution.py:130
  20.5 3.0 collective-permute-start.2
  23.5 1.6 collective-permute-start
  25.1 0.5 collective-permute-start.3
  25.6 26.3 %collective-permute-done.2.refs_2_ = bf16[38,128,128]{2,1,0:T(8,128)(2,1)S(1)} collective-permute-done((bf16[38,128,128]{2,1,0:T(8,128)(2,1)}, bf16[38,128,128]{2,1,0:T(8,128)(2,1)S(1)}, u32[]{:S(2)}, u32[]{:S(2)}) %collective-permute-start.2) | collective-permute-done | bytes 1245216 | tf_op jit(solution)/shard_map/cond/branch_0_fun/ppermute | solution.py:555
  51.9 2.1 collective-permute-done.refs_0_
  54.0 23.8 %collective-permute-done.3.refs_3_ = bf16[38,128,128]{2,1,0:T(8,128)(2,1)S(1)} collective-permute-done((bf16[38,128,128]{2,1,0:T(8,128)(2,1)}, bf16[38,128,128]{2,1,0:T(8,128)(2,1)S(1)}, u32[]{:S(2)}, u32[]{:S(2)}) %collective-permute-start.3) | collective-permute-done | bytes 1245216 | tf_op jit(solution)/shard_map/cond/branch_0_fun/ppermute | solution.py:555
  77.8 1.6 collective-permute-done.1.refs_1_
  79.4 2.0 stage.6
  81.4 1.3 collective-permute-start.4
  82.7 1.6 collective-permute-start.5
  84.6 0.4 select_reduce_fusion.1
  85.0 0.7 copy.40.counts_ref
  85.6 0.9 select_reduce_fusion.lists_ref
  86.5 12.3 %row_unpack.4.refs_0_ = bf16[1024,6144]{1,0:T(8,128)(2,1)} custom-call(s32[64,64]{1,0:T(8,128)S(1)} %get-tuple-element.40.table_ref, s32[2]{0:T(128)S(1)} %get-tuple-element.43.place_ref.refs_18_.refs_12_.refs_21_, bf16[1024,2048]{1,0:T(8,128)(2,1)} %get-tuple-element.44.x_ref, bf16[38,128,128]{2,1,0:T(8,128)(2,1)} %copy-done.9, ...), custom_call_target="tpu_custom_call" | custom-call | flops 1 | bytes 1 | tf_op jit(solution)/shard_map/cond/branch_0_fun/row_unpack/pallas_call | solution.py:230
  98.9 14.6 %square_group.10 = (bf16[4,48,128,128]{3,2,1,0:T(8,128)(2,1)}, f32[1024,512]{1,0:T(8,128)}, bf16[1024,512]{1,0:T(8,128)(2,1)}) custom-call(s32[8,128]{1,0:T(8,128)} %select_reduce_fusion.lists_ref, s32[8,17]{1,0:T(8,128)} %copy.40.counts_ref, s32[2]{0:T(128)S(1)} %get-tuple-element.43.place_ref.refs_18_.refs_12_.refs_21_, ...), custom_call_target="tpu_custom_call" | custom-call | flops 1 | bytes 1 | tf_op jit(solution)/shard_map/cond/branch_0_fun/square_group/pallas_call | solution.py:335
  113.6 1.0 copy-done.27
  114.6 0.4 copy-done.28
  115.0 8.9 %row_unpack.5.refs_0_.refs_1_ = bf16[1024,2048]{1,0:T(8,128)(2,1)} custom-call(s32[64,64]{1,0:T(8,128)S(1)} %get-tuple-element.40.table_ref, s32[2]{0:T(128)S(1)} %get-tuple-element.43.place_ref.refs_18_.refs_12_.refs_21_, bf16[1024,2048]{1,0:T(8,128)(2,1)} %get-tuple-element.44.x_ref, bf16[38,128,128]{2,1,0:T(8,128)(2,1)} %copy-done.27, ...), custom_call_target="tpu_custom_call" | custom-call | flops 1 | bytes 1 | tf_op jit(solution)/shard_map/cond/branch_0_fun/row_unpack/pallas_call | solution.py:230
  123.9 1.9 stage.7
  125.9 8.0 %square_group.11 = (bf16[4,16,128,128]{3,2,1,0:T(8,128)(2,1)}, f32[1024,512]{1,0:T(8,128)}, bf16[1024,512]{1,0:T(8,128)(2,1)}) custom-call(s32[8,128]{1,0:T(8,128)} %select_reduce_fusion.lists_ref, s32[8,17]{1,0:T(8,128)} %copy.40.counts_ref, s32[2]{0:T(128)S(1)} %get-tuple-element.43.place_ref.refs_18_.refs_12_.refs_21_, ...), custom_call_target="tpu_custom_call" | custom-call | flops 1 | bytes 1 | tf_op jit(solution)/shard_map/cond/branch_0_fun/square_group/pallas_call | solution.py:335
  133.9 1.8 stage.8
  135.7 0.6 collective-permute-start.7
  136.4 0.5 collective-permute-start.6
  136.9 6.4 %all-gather.14.cloned.1.call-done.refs_3_ = bf16[160,128,128]{2,1,0:T(8,128)(2,1)} async-done(((bf16[20,128,128]{2,1,0:T(8,128)(2,1)}), bf16[160,128,128]{2,1,0:T(8,128)(2,1)}) %all-gather.14.cloned.1.call-update) | async-done | bytes 5242896 | tf_op jit(solution)/shard_map/cond/branch_0_fun/all_gather | solution.py:558
  143.2 18.4 %square_group.12 = (bf16[4,64,128,128]{3,2,1,0:T(8,128)(2,1)}, f32[1024,512]{1,0:T(8,128)}, bf16[1024,512]{1,0:T(8,128)(2,1)}) custom-call(s32[8,128]{1,0:T(8,128)} %select_reduce_fusion.lists_ref, s32[8,17]{1,0:T(8,128)} %copy.40.counts_ref, s32[2]{0:T(128)S(1)} %get-tuple-element.43.place_ref.refs_18_.refs_12_.refs_21_, ...), custom_call_target="tpu_custom_call" | custom-call | flops 1 | bytes 1 | tf_op jit(solution)/shard_map/cond/branch_0_fun/square_group/pallas_call | solution.py:335
  161.6 1.4 collective-permute-start.11
  163.1 1.4 collective-permute-start.10
  164.5 1.0 copy-done
  165.5 1.0 copy-done.2
  166.5 2.2 split.6
  168.7 0.6 collective-permute-start.8
  169.4 0.6 collective-permute-start.9
  170.0 17.9 %collective-permute-done.11.y_ref.refs_7_ = bf16[1024,512]{1,0:T(8,128)(2,1)S(1)} collective-permute-done((bf16[1024,512]{1,0:T(8,128)(2,1)}, bf16[1024,512]{1,0:T(8,128)(2,1)S(1)}, u32[]{:S(2)}, u32[]{:S(2)}) %collective-permute-start.11) | collective-permute-done | bytes 1048608 | tf_op jit(solution)/shard_map/cond/branch_0_fun/ppermute | solution.py:555
  187.9 1.5 collective-permute-done.10.x_ref.refs_6_
  189.4 2.2 split.7
  191.7 1.5 collective-permute-start.13
  193.2 0.8 collective-permute-start.12
  194.0 1.4 all-gather.16.cloned.1.call-done.refs_4_
  195.4 18.1 %square_group.13 = (bf16[4,64,128,128]{3,2,1,0:T(8,128)(2,1)}, f32[1024,512]{1,0:T(8,128)}, bf16[1024,512]{1,0:T(8,128)(2,1)}) custom-call(s32[8,128]{1,0:T(8,128)} %select_reduce_fusion.lists_ref, s32[8,17]{1,0:T(8,128)} %copy.40.counts_ref, s32[2]{0:T(128)S(1)} %get-tuple-element.43.place_ref.refs_18_.refs_12_.refs_21_, ...), custom_call_target="tpu_custom_call" | custom-call | flops 1 | bytes 1 | tf_op jit(solution)/shard_map/cond/branch_0_fun/square_group/pallas_call | solution.py:335
  213.5 2.4 collective-permute-start.18
  215.9 0.6 collective-permute-start.17
  216.5 0.6 collective-permute-start.16
  217.1 17.2 %cube_part.10 = (f32[1024,512]{1,0:T(8,128)}, f32[1024,512]{1,0:T(8,128)}) custom-call(bf16[1024,512]{1,0:T(8,128)(2,1)} %get-tuple-element.48.refs_0_, bf16[1024,512]{1,0:T(8,128)(2,1)} %copy-done.2, bf16[1024,512]{1,0:T(8,128)(2,1)} %copy-done, bf16[512,512]{1,0:T(8,128)(2,1)} %collective-permute-done.8.refs_3_, ...), custom_call_target="tpu_custom_call" | custom-call | flops 1 | bytes 1 | tf_op jit(solution)/shard_map/cond/branch_0_fun/cube_part/pallas_call | solution.py:524
  234.3 18.3 %square_group.14 = (bf16[4,64,128,128]{3,2,1,0:T(8,128)(2,1)}, f32[1024,512]{1,0:T(8,128)}, bf16[1024,512]{1,0:T(8,128)(2,1)}) custom-call(s32[8,128]{1,0:T(8,128)} %select_reduce_fusion.lists_ref, s32[8,17]{1,0:T(8,128)} %copy.40.counts_ref, s32[2]{0:T(128)S(1)} %get-tuple-element.43.place_ref.refs_18_.refs_12_.refs_21_, ...), custom_call_target="tpu_custom_call" | custom-call | flops 1 | bytes 1 | tf_op jit(solution)/shard_map/cond/branch_0_fun/square_group/pallas_call | solution.py:335
  252.6 1.6 collective-permute-start.15
  254.2 1.3 collective-permute-start.14
  255.5 16.2 %cube_part.11 = (f32[1024,512]{1,0:T(8,128)}, f32[1024,512]{1,0:T(8,128)}) custom-call(bf16[1024,512]{1,0:T(8,128)(2,1)} %get-tuple-element.48.refs_0_, bf16[1024,512]{1,0:T(8,128)(2,1)} %copy-done.2, bf16[1024,512]{1,0:T(8,128)(2,1)} %copy-done, bf16[512,512]{1,0:T(8,128)(2,1)} %collective-permute-done.8.refs_3_, ...), custom_call_target="tpu_custom_call" | custom-call | flops 1 | bytes 1 | tf_op jit(solution)/shard_map/cond/branch_0_fun/cube_part/pallas_call | solution.py:524
  271.8 0.9 copy-done.12
  272.7 0.4 copy-done.14
  273.1 0.3 copy-done.16
  273.4 11.3 %cube_part.12 = (f32[1024,512]{1,0:T(8,128)}, f32[1024,512]{1,0:T(8,128)}) custom-call(bf16[1024,512]{1,0:T(8,128)(2,1)} %get-tuple-element.64.refs_0_, bf16[1024,512]{1,0:T(8,128)(2,1)} %copy-done.16, bf16[1024,512]{1,0:T(8,128)(2,1)} %copy-done.14, bf16[1024,512]{1,0:T(8,128)(2,1)} %copy-done.12, ...), custom_call_target="tpu_custom_call" | custom-call | flops 1 | bytes 1 | tf_op jit(solution)/shard_map/cond/branch_0_fun/cube_part/pallas_call | solution.py:524
  285.1 2.2 split.8
  287.3 1.4 collective-permute-start.20
  288.7 0.8 collective-permute-start.19
  289.6 11.3 %cube_part.13 = (f32[1024,512]{1,0:T(8,128)}, f32[1024,512]{1,0:T(8,128)}) custom-call(bf16[1024,512]{1,0:T(8,128)(2,1)} %get-tuple-element.64.refs_0_, bf16[1024,512]{1,0:T(8,128)(2,1)} %copy-done.16, bf16[1024,512]{1,0:T(8,128)(2,1)} %copy-done.14, bf16[1024,512]{1,0:T(8,128)(2,1)} %copy-done.12, ...), custom_call_target="tpu_custom_call" | custom-call | flops 1 | bytes 1 | tf_op jit(solution)/shard_map/cond/branch_0_fun/cube_part/pallas_call | solution.py:524
  300.8 0.5 collective-permute-done.20.refs_4_
  301.3 1.2 collective-permute-done.19.refs_3_
  302.5 0.8 copy-done.31
  303.3 16.1 %cube_part.14 = f32[1024,2048]{1,0:T(8,128)} custom-call(bf16[1024,512]{1,0:T(8,128)(2,1)} %get-tuple-element.63.refs_0_, bf16[1024,512]{1,0:T(8,128)(2,1)} %collective-permute-done.14.x_ref.refs_1_, bf16[1024,512]{1,0:T(8,128)(2,1)} %collective-permute-done.15.y_ref.refs_2_, bf16[512,512]{1,0:T(8,128)(2,1)} %copy-done.31, bf16[512,512]{1,0:T(8,128)(2,1)} %copy-done.29, ...), custom_call_target="tpu_custom_call" | custom-call | flops 1 | bytes 1 | tf_op jit(solution)/shard_map/cond/branch_0_fun/cube_part/pallas_call | solution.py:524
  (54 shorter events, 1.1 us)
Async XLA Ops:
  10.6 88.3 %all-gather.12.cloned.1.call-start = ((), (), s32[]{:S(2)}) async-start(), calls=%async_computation | async-start | bytes 7667712 | tf_op jit(solution)/shard_map/cond/branch_0_fun/all_gather | solution.py:558
  14.9 128.3 %all-gather.14.cloned.1.call-start = ((), (), s32[]{:S(2)}) async-start(), calls=%async_computation.1 | async-start | bytes 5898240 | tf_op jit(solution)/shard_map/cond/branch_0_fun/all_gather | solution.py:558
  20.5 31.4 %collective-permute-start.2 = (bf16[38,128,128]{2,1,0:T(8,128)(2,1)}, bf16[38,128,128]{2,1,0:T(8,128)(2,1)S(1)}, u32[]{:S(2)}, u32[]{:S(2)}) collective-permute-start(bf16[38,128,128]{2,1,0:T(8,128)(2,1)} %get-tuple-element.45.h0), channel_id=1, source_target_pairs={{0,16},{8,24},{16,0},{24,8},{1,17},{9,25},{17,1},{25,9},{2,18},{10... | collective-permute-start | bytes 3735560 | tf_op jit(solution)/shard_map/cond/branch_0_fun/ppermute | solution.py:555
  23.5 30.5 %collective-permute-start = (bf16[38,128,128]{2,1,0:T(8,128)(2,1)}, bf16[38,128,128]{2,1,0:T(8,128)(2,1)S(1)}, u32[]{:S(2)}, u32[]{:S(2)}) collective-permute-start(bf16[38,128,128]{2,1,0:T(8,128)(2,1)} %get-tuple-element.45.h0), channel_id=1, source_target_pairs={{0,8},{8,0},{16,24},{24,16},{1,9},{9,1},{17,25},{25,17},{2,10},{10... | collective-permute-start | bytes 3735560 | tf_op jit(solution)/shard_map/cond/branch_0_fun/ppermute | solution.py:555
  25.1 52.7 %collective-permute-start.3 = (bf16[38,128,128]{2,1,0:T(8,128)(2,1)}, bf16[38,128,128]{2,1,0:T(8,128)(2,1)S(1)}, u32[]{:S(2)}, u32[]{:S(2)}) collective-permute-start(bf16[38,128,128]{2,1,0:T(8,128)(2,1)} %get-tuple-element.46.h1), channel_id=1, source_target_pairs={{0,16},{8,24},{16,0},{24,8},{1,17},{9,25},{17,1},{25,9},{2,18},{10... | collective-permute-start | bytes 3735560 | tf_op jit(solution)/shard_map/cond/branch_0_fun/ppermute | solution.py:555
  25.6 53.8 %collective-permute-start.1 = (bf16[38,128,128]{2,1,0:T(8,128)(2,1)}, bf16[38,128,128]{2,1,0:T(8,128)(2,1)}, u32[]{:S(2)}, u32[]{:S(2)}) collective-permute-start(bf16[38,128,128]{2,1,0:T(8,128)(2,1)} %get-tuple-element.46.h1), channel_id=1, source_target_pairs={{0,8},{8,0},{16,24},{24,16},{1,9},{9,1},{17,25},{25,17},{2,10},{10... | collective-permute-start | bytes 3735560 | tf_op jit(solution)/shard_map/cond/branch_0_fun/ppermute | solution.py:555
  51.9 25.9 %copy-start.11 = (bf16[38,128,128]{2,1,0:T(8,128)(2,1)}, bf16[38,128,128]{2,1,0:T(8,128)(2,1)S(1)}, u32[]{:S(2)}) copy-start(bf16[38,128,128]{2,1,0:T(8,128)(2,1)S(1)} %collective-permute-done.2.refs_2_) | copy-start | bytes 3735556 | tf_op jit(solution)/shard_map/cond
  54.0 25.4 %copy-start.9 = (bf16[38,128,128]{2,1,0:T(8,128)(2,1)}, bf16[38,128,128]{2,1,0:T(8,128)(2,1)S(1)}, u32[]{:S(2)}) copy-start(bf16[38,128,128]{2,1,0:T(8,128)(2,1)S(1)} %collective-permute-done.refs_0_) | copy-start | bytes 3735556 | tf_op jit(solution)/shard_map/cond
  77.8 1.6 copy-start.10
  81.4 114.0 %all-gather.16.cloned.1.call-start = ((), (), s32[]{:S(2)}) async-start(), calls=%async_computation.2 | async-start | bytes 5308416 | tf_op jit(solution)/shard_map/cond/branch_0_fun/all_gather | solution.py:558
  81.4 32.1 %collective-permute-start.4 = (bf16[38,128,128]{2,1,0:T(8,128)(2,1)}, bf16[38,128,128]{2,1,0:T(8,128)(2,1)S(1)}, u32[]{:S(2)}, u32[]{:S(2)}) collective-permute-start(bf16[38,128,128]{2,1,0:T(8,128)(2,1)} %copy-done.9), channel_id=1, source_target_pairs={{0,16},{8,24},{16,0},{24,8},{1,17},{9,25},{17,1},{25,9},{2,18},{10... | collective-permute-start | bytes 3735560 | tf_op jit(solution)/shard_map/cond/branch_0_fun/ppermute | solution.py:555
  82.7 30.8 %collective-permute-start.5 = (bf16[38,128,128]{2,1,0:T(8,128)(2,1)}, bf16[38,128,128]{2,1,0:T(8,128)(2,1)S(1)}, u32[]{:S(2)}, u32[]{:S(2)}) collective-permute-start(bf16[38,128,128]{2,1,0:T(8,128)(2,1)} %copy-done.10), channel_id=1, source_target_pairs={{0,8},{8,0},{16,24},{24,16},{1,9},{9,1},{17,25},{25,17},{2,10},{10... | collective-permute-start | bytes 3735560 | tf_op jit(solution)/shard_map/cond/branch_0_fun/ppermute | solution.py:555
  113.5 1.0 copy-start.27
  113.5 1.5 copy-start.28
  125.9 108.4 %all-gather.18.cloned.1.call-start = ((), (), s32[]{:S(2)}) async-start(), calls=%async_computation.3 | async-start | bytes 3538944 | tf_op jit(solution)/shard_map/cond/branch_0_fun/all_gather | solution.py:558
  135.7 28.8 %collective-permute-start.7 = (bf16[1024,512]{1,0:T(8,128)(2,1)}, bf16[1024,512]{1,0:T(8,128)(2,1)S(1)}, u32[]{:S(2)}, u32[]{:S(2)}) collective-permute-start(bf16[1024,512]{1,0:T(8,128)(2,1)} %get-tuple-element.48.refs_0_), channel_id=1, source_target_pairs={{0,16},{8,24},{16,0},{24,8},{1,17},{9,25},{17,1},{25,9},{2,18},{10... | collective-permute-start | bytes 3145736 | tf_op jit(solution)/shard_map/cond/branch_0_fun/ppermute | solution.py:555
  136.4 28.1 %collective-permute-start.6 = (bf16[1024,512]{1,0:T(8,128)(2,1)}, bf16[1024,512]{1,0:T(8,128)(2,1)S(1)}, u32[]{:S(2)}, u32[]{:S(2)}) collective-permute-start(bf16[1024,512]{1,0:T(8,128)(2,1)} %get-tuple-element.48.refs_0_), channel_id=1, source_target_pairs={{0,8},{8,0},{16,24},{24,16},{1,9},{9,1},{17,25},{25,17},{2,10},{10... | collective-permute-start | bytes 3145736 | tf_op jit(solution)/shard_map/cond/branch_0_fun/ppermute | solution.py:555
  161.6 26.3 %collective-permute-start.11 = (bf16[1024,512]{1,0:T(8,128)(2,1)}, bf16[1024,512]{1,0:T(8,128)(2,1)S(1)}, u32[]{:S(2)}, u32[]{:S(2)}) collective-permute-start(bf16[1024,512]{1,0:T(8,128)(2,1)} %get-tuple-element.51.refs_5_), channel_id=1, source_target_pairs={{0,16},{8,24},{16,0},{24,8},{1,17},{9,25},{17,1},{25,9},{2,18},{10... | collective-permute-start | bytes 3145736 | tf_op jit(solution)/shard_map/cond/branch_0_fun/ppermute | solution.py:555
  163.1 26.3 %collective-permute-start.10 = (bf16[1024,512]{1,0:T(8,128)(2,1)}, bf16[1024,512]{1,0:T(8,128)(2,1)}, u32[]{:S(2)}, u32[]{:S(2)}) collective-permute-start(bf16[1024,512]{1,0:T(8,128)(2,1)} %get-tuple-element.51.refs_5_), channel_id=1, source_target_pairs={{0,8},{8,0},{16,24},{24,16},{1,9},{9,1},{17,25},{25,17},{2,10},{10... | collective-permute-start | bytes 3145736 | tf_op jit(solution)/shard_map/cond/branch_0_fun/ppermute | solution.py:555
  164.5 1.0 copy-start
  165.5 1.0 copy-start.2
  168.7 47.2 %collective-permute-start.8 = (bf16[512,512]{1,0:T(8,128)(2,1)}, bf16[512,512]{1,0:T(8,128)(2,1)}, u32[]{:S(2)}, u32[]{:S(2)}) collective-permute-start(bf16[512,512]{1,0:T(8,128)(2,1)} %get-tuple-element.49), channel_id=1, source_target_pairs={{0,16},{8,24},{16,0},{24,8},{1,17},{9,25},{17,1},{25,9},{2,18},{10... | collective-permute-start | bytes 1572872 | tf_op jit(solution)/shard_map/cond/branch_0_fun/ppermute | solution.py:555
  169.4 47.1 %collective-permute-start.9 = (bf16[512,512]{1,0:T(8,128)(2,1)}, bf16[512,512]{1,0:T(8,128)(2,1)}, u32[]{:S(2)}, u32[]{:S(2)}) collective-permute-start(bf16[512,512]{1,0:T(8,128)(2,1)} %get-tuple-element.50), channel_id=1, source_target_pairs={{0,8},{8,0},{16,24},{24,16},{1,9},{9,1},{17,25},{25,17},{2,10},{10... | collective-permute-start | bytes 1572872 | tf_op jit(solution)/shard_map/cond/branch_0_fun/ppermute | solution.py:555
  187.9 1.5 copy-start.4
  191.7 25.4 %collective-permute-start.13 = (bf16[512,512]{1,0:T(8,128)(2,1)}, bf16[512,512]{1,0:T(8,128)(2,1)}, u32[]{:S(2)}, u32[]{:S(2)}) collective-permute-start(bf16[512,512]{1,0:T(8,128)(2,1)} %get-tuple-element.53), channel_id=1, source_target_pairs={{0,8},{8,0},{16,24},{24,16},{1,9},{9,1},{17,25},{25,17},{2,10},{10... | collective-permute-start | bytes 1572872 | tf_op jit(solution)/shard_map/cond/branch_0_fun/ppermute | solution.py:555
  193.2 23.9 %copy-start.18 = (s32[64,64]{1,0:T(8,128)S(1)}, s32[64,64]{1,0:T(8,128)}, u32[]{:S(2)}) copy-start(s32[64,64]{1,0:T(8,128)} %get-tuple-element.57.refs_19_.refs_13_.refs_22_) | copy-start | bytes 49156 | tf_op jit(solution)/shard_map/cond
  193.2 23.9 %copy-start.21 = (s32[64,64]{1,0:T(8,128)S(1)}, s32[64,64]{1,0:T(8,128)}, u32[]{:S(2)}) copy-start(s32[64,64]{1,0:T(8,128)} %get-tuple-element.58.refs_20_.refs_14_.refs_23_) | copy-start | bytes 49156 | tf_op jit(solution)/shard_map/cond
  193.2 23.9 %collective-permute-start.12 = (bf16[512,512]{1,0:T(8,128)(2,1)}, bf16[512,512]{1,0:T(8,128)(2,1)}, u32[]{:S(2)}, u32[]{:S(2)}) collective-permute-start(bf16[512,512]{1,0:T(8,128)(2,1)} %get-tuple-element.52.refs_5_), channel_id=1, source_target_pairs={{0,16},{8,24},{16,0},{24,8},{1,17},{9,25},{17,1},{25,9},{2,18},{10... | collective-permute-start | bytes 1572872 | tf_op jit(solution)/shard_map/cond/branch_0_fun/ppermute | solution.py:555
  213.5 58.3 %collective-permute-start.18 = (bf16[1024,512]{1,0:T(8,128)(2,1)}, bf16[1024,512]{1,0:T(8,128)(2,1)S(1)}, u32[]{:S(2)}, u32[]{:S(2)}) collective-permute-start(bf16[1024,512]{1,0:T(8,128)(2,1)} %get-tuple-element.64.refs_0_), channel_id=1, source_target_pairs={{0,24},{8,16},{16,8},{24,0},{1,25},{9,17},{17,9},{25,1},{2,26},{10... | collective-permute-start | bytes 3145736 | tf_op jit(solution)/shard_map/cond/branch_0_fun/ppermute | solution.py:555
  215.9 55.9 %collective-permute-start.17 = (bf16[1024,512]{1,0:T(8,128)(2,1)}, bf16[1024,512]{1,0:T(8,128)(2,1)S(1)}, u32[]{:S(2)}, u32[]{:S(2)}) collective-permute-start(bf16[1024,512]{1,0:T(8,128)(2,1)} %get-tuple-element.64.refs_0_), channel_id=1, source_target_pairs={{0,16},{8,24},{16,0},{24,8},{1,17},{9,25},{17,1},{25,9},{2,18},{10... | collective-permute-start | bytes 3145736 | tf_op jit(solution)/shard_map/cond/branch_0_fun/ppermute | solution.py:555
  216.5 55.3 %collective-permute-start.16 = (bf16[1024,512]{1,0:T(8,128)(2,1)}, bf16[1024,512]{1,0:T(8,128)(2,1)S(1)}, u32[]{:S(2)}, u32[]{:S(2)}) collective-permute-start(bf16[1024,512]{1,0:T(8,128)(2,1)} %get-tuple-element.64.refs_0_), channel_id=1, source_target_pairs={{0,8},{8,0},{16,24},{24,16},{1,9},{9,1},{17,25},{25,17},{2,10},{10... | collective-permute-start | bytes 3145736 | tf_op jit(solution)/shard_map/cond/branch_0_fun/ppermute | solution.py:555
  252.6 32.4 %collective-permute-start.15 = (bf16[1024,512]{1,0:T(8,128)(2,1)}, bf16[1024,512]{1,0:T(8,128)(2,1)}, u32[]{:S(2)}, u32[]{:S(2)}) collective-permute-start(bf16[1024,512]{1,0:T(8,128)(2,1)} %get-tuple-element.63.refs_0_), channel_id=1, source_target_pairs={{0,16},{8,24},{16,0},{24,8},{1,17},{9,25},{17,1},{25,9},{2,18},{10... | collective-permute-start | bytes 3145736 | tf_op jit(solution)/shard_map/cond/branch_0_fun/ppermute | solution.py:555
  254.2 30.9 %collective-permute-start.14 = (bf16[1024,512]{1,0:T(8,128)(2,1)}, bf16[1024,512]{1,0:T(8,128)(2,1)}, u32[]{:S(2)}, u32[]{:S(2)}) collective-permute-start(bf16[1024,512]{1,0:T(8,128)(2,1)} %get-tuple-element.63.refs_0_), channel_id=1, source_target_pairs={{0,8},{8,0},{16,24},{24,16},{1,9},{9,1},{17,25},{25,17},{2,10},{10... | collective-permute-start | bytes 3145736 | tf_op jit(solution)/shard_map/cond/branch_0_fun/ppermute | solution.py:555
  271.7 1.0 copy-start.12
  271.8 1.4 copy-start.14
  271.8 1.6 copy-start.16
  287.3 14.0 %collective-permute-start.20 = (bf16[512,512]{1,0:T(8,128)(2,1)}, bf16[512,512]{1,0:T(8,128)(2,1)S(1)}, u32[]{:S(2)}, u32[]{:S(2)}) collective-permute-start(bf16[512,512]{1,0:T(8,128)(2,1)} %get-tuple-element.72), channel_id=1, source_target_pairs={{0,8},{8,0},{16,24},{24,16},{1,9},{9,1},{17,25},{25,17},{2,10},{10... | collective-permute-start | bytes 1572872 | tf_op jit(solution)/shard_map/cond/branch_0_fun/ppermute | solution.py:555
  288.7 13.8 %collective-permute-start.19 = (bf16[512,512]{1,0:T(8,128)(2,1)}, bf16[512,512]{1,0:T(8,128)(2,1)S(1)}, u32[]{:S(2)}, u32[]{:S(2)}) collective-permute-start(bf16[512,512]{1,0:T(8,128)(2,1)} %get-tuple-element.71.refs_17_), channel_id=1, source_target_pairs={{0,16},{8,24},{16,0},{24,8},{1,17},{9,25},{17,1},{25,9},{2,18},{10... | collective-permute-start | bytes 1572872 | tf_op jit(solution)/shard_map/cond/branch_0_fun/ppermute | solution.py:555
  301.3 1.2 copy-start.29
  302.5 0.8 copy-start.31
Sparse Core Ops, SparseCore 0:
  15.1 71.7 all-gather.11
  88.5 54.6 all-gather.13
  144.9 50.4 all-gather.15
  196.9 37.0 all-gather.17
